TPU v7x, 32 devices: a whole 2x2x4 slice. The times are simulated.
32 devices in a mesh: dp: 8 (over z, y), tensor: 4 (over x, core).
Axes of the slice: x: 2, y: 2, z: 4, core: 2. Of those that a mesh axis runs over, the one named last changes fastest.
Arguments:
- tokens: bfloat16 [5120, 2048], P('dp'), may hold values from -6 to 6
- cotangent: bfloat16 [5120, 2048], P('dp'), may hold values from -6 to 6
- lengths: int32 [8], P('dp'), may hold values from 213 to 640, as said below
- w_query: float32 [2048, 2048], P('dp', 'tensor'), may hold values from -0.125 to 0.125
- w_keyval: float32 [2048, 512], P('dp'), may hold values from -0.125 to 0.125
- w_output: float32 [2048, 2048], P('tensor', 'dp'), may hold values from -2.5 to 2.5
- w_gateup: float32 [2, 2048, 16384], P(None, 'dp', 'tensor'), may hold values from -0.125 to 0.125
- w_down: float32 [16384, 2048], P('tensor', 'dp'), may hold values from -0.046875 to 0.046875
- norm_gains: float32 [2, 2048], P(None, 'dp'), may hold values from 0.5 to 1.5
- first_query: float32 [2048, 2048], P('dp', 'tensor'), may hold values from -28 to 28
- first_keyval: float32 [2048, 512], P('dp'), may hold values from -80 to 80
- first_output: float32 [2048, 2048], P('tensor', 'dp'), may hold values from -3.5 to 3.5
- first_gateup: float32 [2, 2048, 16384], P(None, 'dp', 'tensor'), may hold values from -8 to 8
- first_down: float32 [16384, 2048], P('tensor', 'dp'), may hold values from -24 to 24
- first_gains: float32 [2, 2048], P(None, 'dp'), may hold values from -40 to 40
- second_query: float32 [2048, 2048], P('dp', 'tensor'), may hold values from 87.04 to 343.04
- second_keyval: float32 [2048, 512], P('dp'), may hold values from 819.2 to 81920
- second_output: float32 [2048, 2048], P('tensor', 'dp'), may hold values from 1.52 to 6
- second_gateup: float32 [2, 2048, 16384], P(None, 'dp', 'tensor'), may hold values from 9.28 to 37.12
- second_down: float32 [16384, 2048], P('tensor', 'dp'), may hold values from 74.24 to 296.96
- second_gains: float32 [2, 2048], P(None, 'dp'), may hold values from 204.8 to 20480
Outputs:
- block_output: float32 [5120, 2048], P('dp')
- input_grad: float32 [5120, 2048], P('dp')
- query_grad: float32 [2048, 2048], P('dp', 'tensor')
- query_first: float32 [2048, 2048], P('dp', 'tensor')
- query_second: float32 [2048, 2048], P('dp', 'tensor')
- query_update: float32 [2048, 2048], P('dp', 'tensor')
- keyval_grad: float32 [2048, 512], P('dp')
- keyval_first: float32 [2048, 512], P('dp')
- keyval_second: float32 [2048, 512], P('dp')
- keyval_update: float32 [2048, 512], P('dp')
- output_grad: float32 [2048, 2048], P('tensor', 'dp')
- output_first: float32 [2048, 2048], P('tensor', 'dp')
- output_second: float32 [2048, 2048], P('tensor', 'dp')
- output_update: float32 [2048, 2048], P('tensor', 'dp')
- gateup_grad: float32 [2, 2048, 16384], P(None, 'dp', 'tensor')
- gateup_first: float32 [2, 2048, 16384], P(None, 'dp', 'tensor')
- gateup_second: float32 [2, 2048, 16384], P(None, 'dp', 'tensor')
- gateup_update: float32 [2, 2048, 16384], P(None, 'dp', 'tensor')
- down_grad: float32 [16384, 2048], P('tensor', 'dp')
- down_first: float32 [16384, 2048], P('tensor', 'dp')
- down_second: float32 [16384, 2048], P('tensor', 'dp')
- down_update: float32 [16384, 2048], P('tensor', 'dp')
- gains_grad: float32 [2, 2048], P(None, 'dp')
- gains_first: float32 [2, 2048], P(None, 'dp')
- gains_second: float32 [2, 2048], P(None, 'dp')
- gains_update: float32 [2, 2048], P(None, 'dp')
Inputs may be any that keep to these rules, and one draw needn't show every extreme that they name: Slot s holds a sequence in its first lengths[s] positions, the rest is padding; in every draw some slot is full (640 tokens) and some holds 213 tokens.
All inputs are finite; a program needn't handle non-finite values.
Results may differ from a plain program's by a relative error of at most 0.024.
Values may be sent and summed in bfloat16 or wider, within the bound.
A program may use at most 384 MiB of HBM per device.

v0:
```python
import jax
import jax.numpy as jnp
from jax import lax
from jax.sharding import PartitionSpec as P

HD = 256


norm_eps = 1e-06
beta_first = 0.9
beta_second = 0.95
learn_rate = 0.01
decay_rate = 0.1
adam_eps = 1e-08
masked_score = -1e30


def rms_scale(values, gain):
    inverse = lax.rsqrt(jnp.mean(values * values, axis=-1, keepdims=True) + norm_eps)
    return values * inverse * gain


def inner_rows(left, right):
    return lax.dot_general(
        left, right, (((0,), (0,)), ((), ())), preferred_element_type=jnp.float32
    )


def times_trans(left, right):
    return lax.dot_general(
        left, right, (((1,), (1,)), ((), ())), preferred_element_type=jnp.float32
    )


def slot_scores(query, keyval, length):
    slot = query.shape[0]
    heads = query.shape[1] // HD
    places = jnp.arange(slot)
    allowed = (places[None, :] <= places[:, None]) & (places[None, :] < length)
    raw = jnp.einsum(
        "qhd,kd->hqk",
        query.reshape(slot, heads, HD),
        keyval[:, :HD],
        preferred_element_type=jnp.float32,
    )
    return jnp.where(allowed[None], raw * HD ** (-0.5), masked_score)


def slot_forward(items):
    query, keyval, length = items
    scores = slot_scores(query, keyval, length)
    top = jnp.max(scores, axis=-1, keepdims=True)
    expo = jnp.exp(scores - top)
    total = jnp.sum(expo, axis=-1, keepdims=True)
    probs = expo / total
    mixed = jnp.einsum(
        "hqk,kd->qhd",
        probs.astype(jnp.bfloat16),
        keyval[:, HD:],
        preferred_element_type=jnp.float32,
    )
    return (mixed.reshape(query.shape), (top + jnp.log(total))[..., 0])


def slot_backward(items):
    query, keyval, length, logsum, grad_mixed = items
    slot, width = query.shape
    heads = width // HD
    probs = jnp.exp(slot_scores(query, keyval, length) - logsum[..., None])
    grad_three = grad_mixed.reshape(slot, heads, HD)
    grad_value = jnp.einsum(
        "hqk,qhd->kd", probs.astype(jnp.bfloat16), grad_three, preferred_element_type=jnp.float32
    )
    grad_probs = jnp.einsum(
        "qhd,kd->hqk", grad_three, keyval[:, HD:], preferred_element_type=jnp.float32
    )
    grad_scores = probs * (grad_probs - jnp.sum(grad_probs * probs, axis=-1, keepdims=True))
    grad_raw = (grad_scores * HD ** (-0.5)).astype(jnp.bfloat16)
    grad_query = jnp.einsum(
        "hqk,kd->qhd", grad_raw, keyval[:, :HD], preferred_element_type=jnp.float32
    )
    grad_key = jnp.einsum(
        "hqk,qhd->kd", grad_raw, query.reshape(slot, heads, HD), preferred_element_type=jnp.float32
    )
    return (grad_query.reshape(slot, width), jnp.concatenate([grad_key, grad_value], axis=1))


def adamw(weight, grad, first, second, decay):
    first_new = beta_first * first + (1.0 - beta_first) * grad
    second_new = beta_second * second + (1.0 - beta_second) * grad * grad
    update = -learn_rate * (first_new / (jnp.sqrt(second_new) + adam_eps) + decay * weight)
    return (grad, first_new, second_new, update)


def shards(
    tokens,
    cotangent,
    lengths,
    w_query,
    w_keyval,
    w_output,
    w_gateup,
    w_down,
    norm_gains,
    first_query,
    first_keyval,
    first_output,
    first_gateup,
    first_down,
    first_gains,
    second_query,
    second_keyval,
    second_output,
    second_gateup,
    second_down,
    second_gains,
):
    bf = jnp.bfloat16
    fl = jnp.float32
    query_w, keyval_w, output_w, gateup_w, down_w, gain_w = (
        lax.all_gather(w_query.astype(bf), "dp", axis=0, tiled=True),
        lax.all_gather(w_keyval.astype(bf), "dp", axis=0, tiled=True),
        lax.all_gather(w_output.astype(bf), "dp", axis=1, tiled=True),
        lax.all_gather(w_gateup.astype(bf), "dp", axis=1, tiled=True),
        lax.all_gather(w_down.astype(bf), "dp", axis=1, tiled=True),
        lax.all_gather(norm_gains.astype(bf), "dp", axis=1, tiled=True),
    )
    gain_full = gain_w.astype(fl)
    x = tokens.astype(fl)
    count = lengths.shape[0]
    slot = x.shape[0] // count
    valid = (jnp.arange(slot)[None, :] < lengths[:, None]).reshape(-1, 1)
    normed_one = rms_scale(x, gain_full[0]).astype(bf)
    query = jnp.dot(normed_one, query_w, preferred_element_type=fl).astype(bf)
    keyval = jnp.dot(normed_one, keyval_w, preferred_element_type=fl).astype(bf)
    width = query.shape[1]
    query_slots = query.reshape(count, slot, width)
    keyval_slots = keyval.reshape(count, slot, 2 * HD)
    mixed, logsum = lax.map(slot_forward, (query_slots, keyval_slots, lengths))
    mixed = mixed.reshape(-1, width).astype(bf)
    attn = lax.psum(
        jnp.dot(mixed, output_w, preferred_element_type=fl).astype(jnp.bfloat16), "tensor"
    ).astype(jnp.float32)
    resid = x + attn
    normed_two = rms_scale(resid, gain_full[1]).astype(bf)
    gate = jnp.dot(normed_two, gateup_w[0], preferred_element_type=fl)
    upper = jnp.dot(normed_two, gateup_w[1], preferred_element_type=fl)
    hidden = (jax.nn.gelu(gate, approximate=True) * upper).astype(bf)
    block_output = resid + lax.psum(
        jnp.dot(hidden, down_w, preferred_element_type=fl).astype(jnp.bfloat16), "tensor"
    ).astype(jnp.float32)
    query_w, keyval_w, output_w, gateup_w, down_w, gain_w = (
        lax.all_gather(w_query.astype(bf), "dp", axis=0, tiled=True),
        lax.all_gather(w_keyval.astype(bf), "dp", axis=0, tiled=True),
        lax.all_gather(w_output.astype(bf), "dp", axis=1, tiled=True),
        lax.all_gather(w_gateup.astype(bf), "dp", axis=1, tiled=True),
        lax.all_gather(w_down.astype(bf), "dp", axis=1, tiled=True),
        lax.all_gather(norm_gains.astype(bf), "dp", axis=1, tiled=True),
    )
    grad_out = jnp.where(valid, cotangent.astype(fl), 0.0)
    grad_low = grad_out.astype(bf)
    down_grad = inner_rows(hidden, grad_low)
    grad_hidden = times_trans(grad_low, down_w)
    _, pull_gelu = jax.vjp(
        lambda left, right: jax.nn.gelu(left, approximate=True) * right, gate, upper
    )
    grad_gate, grad_up = pull_gelu(grad_hidden)
    grad_gate = grad_gate.astype(bf)
    grad_up = grad_up.astype(bf)
    gateup_grad = jnp.stack([inner_rows(normed_two, grad_gate), inner_rows(normed_two, grad_up)])
    grad_normed_two = lax.psum(
        (times_trans(grad_gate, gateup_w[0]) + times_trans(grad_up, gateup_w[1])).astype(
            jnp.bfloat16
        ),
        "tensor",
    ).astype(jnp.float32)
    _, pull_second = jax.vjp(rms_scale, resid, gain_full[1])
    grad_resid_norm, grad_gain_two = pull_second(grad_normed_two)
    grad_resid = grad_out + grad_resid_norm
    grad_attn = grad_resid.astype(bf)
    output_grad = inner_rows(mixed, grad_attn)
    grad_mixed = times_trans(grad_attn, output_w).astype(bf)
    grad_query, grad_keyval = lax.map(
        slot_backward,
        (query_slots, keyval_slots, lengths, logsum, grad_mixed.reshape(count, slot, width)),
    )
    grad_query = grad_query.reshape(-1, width).astype(bf)
    grad_keyval = grad_keyval.reshape(-1, 2 * HD)
    from_query, keyval_total = (
        lax.psum(times_trans(grad_query, query_w).astype(jnp.bfloat16), "tensor").astype(
            jnp.float32
        ),
        lax.psum(grad_keyval.astype(jnp.bfloat16), "tensor").astype(jnp.float32),
    )
    keyval_low = keyval_total.astype(bf)
    grad_normed_one = from_query + times_trans(keyval_low, keyval_w)
    query_grad = inner_rows(normed_one, grad_query)
    keyval_grad = inner_rows(normed_one, keyval_low)
    _, pull_first = jax.vjp(rms_scale, x, gain_full[0])
    grad_x_norm, grad_gain_one = pull_first(grad_normed_one)
    input_grad = grad_resid + grad_x_norm
    gains_grad = jnp.stack([grad_gain_one, grad_gain_two])
    query_shard, keyval_shard, output_shard, gateup_shard, down_shard, gains_shard = (
        lax.psum_scatter(
            query_grad.astype(jnp.bfloat16), "dp", scatter_dimension=0, tiled=True
        ).astype(jnp.float32),
        lax.psum_scatter(
            keyval_grad.astype(jnp.bfloat16), "dp", scatter_dimension=0, tiled=True
        ).astype(jnp.float32),
        lax.psum_scatter(
            output_grad.astype(jnp.bfloat16), "dp", scatter_dimension=1, tiled=True
        ).astype(jnp.float32),
        lax.psum_scatter(
            gateup_grad.astype(jnp.bfloat16), "dp", scatter_dimension=1, tiled=True
        ).astype(jnp.float32),
        lax.psum_scatter(
            down_grad.astype(jnp.bfloat16), "dp", scatter_dimension=1, tiled=True
        ).astype(jnp.float32),
        lax.psum_scatter(
            gains_grad.astype(jnp.bfloat16), "dp", scatter_dimension=1, tiled=True
        ).astype(jnp.float32),
    )
    qa = adamw(w_query, query_shard, first_query, second_query, decay_rate)
    ka = adamw(w_keyval, keyval_shard, first_keyval, second_keyval, decay_rate)
    oa = adamw(w_output, output_shard, first_output, second_output, decay_rate)
    ga = adamw(w_gateup, gateup_shard, first_gateup, second_gateup, decay_rate)
    da = adamw(w_down, down_shard, first_down, second_down, decay_rate)
    na = adamw(norm_gains, gains_shard, first_gains, second_gains, 0.0)
    return (
        block_output,
        input_grad,
        qa[0],
        qa[1],
        qa[2],
        qa[3],
        ka[0],
        ka[1],
        ka[2],
        ka[3],
        oa[0],
        oa[1],
        oa[2],
        oa[3],
        ga[0],
        ga[1],
        ga[2],
        ga[3],
        da[0],
        da[1],
        da[2],
        da[3],
        na[0],
        na[1],
        na[2],
        na[3],
    )


def solution(mesh):
    return jax.shard_map(
        shards,
        mesh=mesh,
        in_specs=(
            P("dp", None),
            P("dp", None),
            P("dp"),
            P("dp", "tensor"),
            P("dp", None),
            P("tensor", "dp"),
            P(None, "dp", "tensor"),
            P("tensor", "dp"),
            P(None, "dp"),
            P("dp", "tensor"),
            P("dp", None),
            P("tensor", "dp"),
            P(None, "dp", "tensor"),
            P("tensor", "dp"),
            P(None, "dp"),
            P("dp", "tensor"),
            P("dp", None),
            P("tensor", "dp"),
            P(None, "dp", "tensor"),
            P("tensor", "dp"),
            P(None, "dp"),
        ),
        out_specs=(
            P("dp", None),
            P("dp", None),
            P("dp", "tensor"),
            P("dp", "tensor"),
            P("dp", "tensor"),
            P("dp", "tensor"),
            P("dp", None),
            P("dp", None),
            P("dp", None),
            P("dp", None),
            P("tensor", "dp"),
            P("tensor", "dp"),
            P("tensor", "dp"),
            P("tensor", "dp"),
            P(None, "dp", "tensor"),
            P(None, "dp", "tensor"),
            P(None, "dp", "tensor"),
            P(None, "dp", "tensor"),
            P("tensor", "dp"),
            P("tensor", "dp"),
            P("tensor", "dp"),
            P("tensor", "dp"),
            P(None, "dp"),
            P(None, "dp"),
            P(None, "dp"),
            P(None, "dp"),
        ),
        check_vma=False,
    )
```

profile of v0, /device:TPU:0, one launch (start us, length us, event | category | flops | bytes accessed | tf_op | source)
XLA Modules:
  0.0 2524.9 jit_solution(11860935050053479509)
XLA Ops:
  14.3 22.3 all_gather.23
  39.7 23.0 all-gather.8.cloned.1.call-done
  67.2 46.1 %all-gather.6.cloned.1.call-done = bf16[2048,512]{1,0:T(8,128)(2,1)} async-done(((bf16[256,512]{1,0:T(8,128)(2,1)}), bf16[2048,512]{1,0:T(8,128)(2,1)}) %all-gather.6.cloned.1.call-update) | async-done | bytes 2097168 | tf_op jit(solution)/shard_map/all_gather | solution.py:122
  120.6 44.9 %all-gather.10.cloned.1.call-done = bf16[512,2048]{1,0:T(8,128)(2,1)} async-done(((bf16[512,256]{1,0:T(8,128)(2,1)}), bf16[512,2048]{1,0:T(8,128)(2,1)}) %all-gather.10.cloned.1.call-update) | async-done | bytes 2097168 | tf_op jit(solution)/shard_map/all_gather | solution.py:123
  180.9 47.7 %all-reduce.5.cloned.1.call-done = bf16[640,2048]{1,0:T(8,128)(2,1)} async-done(((bf16[640,2048]{1,0:T(8,128)(2,1)}), bf16[640,2048]{1,0:T(8,128)(2,1)}) %all-reduce.5.cloned.1.call-update) | async-done | bytes 2621456 | tf_op jit(solution)/shard_map/psum | solution.py:141
  234.4 634.0 %all-gather.12.cloned.1.call-done = bf16[2,2048,4096]{2,1,0:T(8,128)(2,1)} async-done(((bf16[2,256,4096]{2,1,0:T(8,128)(2,1)}), bf16[2,2048,4096]{2,1,0:T(8,128)(2,1)}) %all-gather.12.cloned.1.call-update) | async-done | bytes 33554448 | tf_op jit(solution)/shard_map/all_gather | solution.py:124
  868.5 20.1 fusion.4
  888.6 17.1 fusion.2
  905.7 193.0 %all-gather.14.cloned.1.call-done = bf16[4096,2048]{1,0:T(8,128)(2,1)} async-done(((bf16[4096,256]{1,0:T(8,128)(2,1)}), bf16[4096,2048]{1,0:T(8,128)(2,1)}) %all-gather.14.cloned.1.call-update) | async-done | bytes 16777232 | tf_op jit(solution)/shard_map/all_gather | solution.py:125
  1098.7 28.8 %multiply_convert_fusion = (bf16[640,4096]{1,0:T(8,128)(2,1)}, bf16[640,4096]{1,0:T(8,128)(2,1)}, bf16[640,4096]{1,0:T(8,128)(2,1)}) fusion(f32[640,4096]{1,0:T(8,128)} %fusion.2, f32[640,4096]{1,0:T(8,128)} %fusion.4, bf16[4096,2048]{1,0:T(8,128)(2,1)} %all-gather.14.cloned.1.call-done, bf16[640,2048]{1,0:T(8,128)(2,1)S(1)} %copy-done.8, ...), kind=kOutput, calls=%fused_computation.21 | convolution fusion | flops 10809507840 | bytes 56099456 | tf_op jit(solution)/shard_map/dot_general | solution.py:30
  1127.5 29.2 %fusion.1 = f32[640,2048]{1,0:T(8,128)} fusion(bf16[640,4096]{1,0:T(8,128)(2,1)} %get-tuple-element.100, bf16[2,2048,4096]{2,1,0:T(8,128)(2,1)} %all-gather.12.cloned.1.call-done), kind=kOutput, calls=%fused_computation.9 | convolution fusion | flops 10737418240 | bytes 27262976 | tf_op jit(solution)/shard_map/dot_general | solution.py:30
  1173.2 17.7 convolution_convert_fusion.3
  1191.0 40.5 %all-reduce.7.cloned.1.call-done = bf16[640,2048]{1,0:T(8,128)(2,1)} async-done(((bf16[640,2048]{1,0:T(8,128)(2,1)}), bf16[640,2048]{1,0:T(8,128)(2,1)}) %all-reduce.7.cloned.1.call-update) | async-done | bytes 2621456 | tf_op jit(solution)/shard_map/psum | solution.py:171
  1264.6 113.8 %all-reduce.9.cloned.1.call-done = (bf16[640,2048]{1,0:T(8,128)(2,1)}, bf16[640,2048]{1,0:T(8,128)(2,1)}, bf16[640,512]{0,1:T(8,128)(2,1)}) async-done(((bf16[640,2048]{1,0:T(8,128)(2,1)}, bf16[640,2048]{1,0:T(8,128)(2,1)}, bf16[640,512]{0,1:T(8,128)(2,1)}), (bf16[640,2048]{1,0:T(8,128)(2,1)}, bf16[640,2048]{1,0:T(8,128)(2,1)}, bf16[640,512]{0,1:T(8,128)(2,1)})) %all-reduce.9.cloned.1.call-update) | async-done | bytes 5898256 | tf_op jit(solution)/shard_map/psum | solution.py:149
  1402.2 19.9 convolution_convert_fusion
  1422.3 19.8 convert_bitcast_fusion
  1442.1 18.4 convert_bitcast_fusion.1
  1460.6 23.4 pad_maximum_fusion
  1496.1 24.5 reduce-scatter.13.cloned.1.call-done
  1523.4 68.7 %reduce-scatter.9.cloned.1.call-done = bf16[256,512]{1,0:T(8,128)(2,1)} async-done(((bf16[2048,512]{1,0:T(8,128)(2,1)}), bf16[256,512]{1,0:T(8,128)(2,1)}) %reduce-scatter.9.cloned.1.call-update) | async-done | bytes 262160 | tf_op jit(solution)/shard_map/reduce_scatter | solution.py:204
  1595.0 68.5 %reduce-scatter.11.cloned.1.call-done = bf16[256,512]{1,0:T(8,128)(2,1)} async-done(((bf16[2048,512]{1,0:T(8,128)(2,1)}), bf16[256,512]{1,0:T(8,128)(2,1)}) %reduce-scatter.11.cloned.1.call-update) | async-done | bytes 262160 | tf_op jit(solution)/shard_map/reduce_scatter | solution.py:207
  1665.9 283.5 %reduce-scatter.17.cloned.1.call-done = bf16[4096,256]{1,0:T(8,128)(2,1)} async-done(((bf16[4096,2048]{1,0:T(8,128)(2,1)}), bf16[4096,256]{1,0:T(8,128)(2,1)}) %reduce-scatter.17.cloned.1.call-update) | async-done | bytes 2097168 | tf_op jit(solution)/shard_map/reduce_scatter | solution.py:216
  1959.9 535.4 %reduce-scatter.15.cloned.1.call-done = bf16[2,256,4096]{2,1,0:T(8,128)(2,1)} async-done(((bf16[2,2048,4096]{2,1,0:T(8,128)(2,1)}), bf16[2,256,4096]{2,1,0:T(8,128)(2,1)}) %reduce-scatter.15.cloned.1.call-update) | async-done | bytes 4194320 | tf_op jit(solution)/shard_map/reduce_scatter | solution.py:213
  2495.4 22.6 add_multiply_fusion
  (151 shorter events, 146.4 us)
Async XLA Ops:
  7.2 55.6 %all-gather.8.cloned.1.call-start = ((), (), s32[]{:S(2)}) async-start(), calls=%async_computation.7 | async-start | bytes 2359296 | tf_op jit(solution)/shard_map/all_gather | solution.py:121
  9.2 104.1 %all-gather.6.cloned.1.call-start = ((), (), s32[]{:S(2)}) async-start(), calls=%async_computation.6 | async-start | bytes 2359296 | tf_op jit(solution)/shard_map/all_gather | solution.py:122
  11.1 154.4 %all-gather.10.cloned.1.call-start = ((), (), s32[]{:S(2)}) async-start(), calls=%async_computation.8 | async-start | bytes 2359296 | tf_op jit(solution)/shard_map/all_gather | solution.py:123
  12.9 215.7 %all-reduce.5.cloned.1.call-start = ((), (), s32[]{:S(2)}) async-start(), calls=%async_computation.9 | async-start | bytes 5242880 | tf_op jit(solution)/shard_map/psum | solution.py:141
  39.5 73.8 %copy-start.28 = (f32[640]{0:T(1024)}, f32[640]{0:T(1024)S(1)}, u32[]{:S(2)}) copy-start(f32[640]{0:T(1024)S(1)} %fusion.59) | copy-start | bytes 7684
  39.7 191.8 %copy-start.18 = (f32[1,2048]{1,0:T(1,128)}, f32[1,2048]{1,0:T(1,128)S(1)}, u32[]{:S(2)}) copy-start(f32[1,2048]{1,0:T(1,128)S(1)} %get-tuple-element.104) | copy-start | bytes 24580
  170.4 698.1 %all-gather.12.cloned.1.call-start = ((), (), s32[]{:S(2)}) async-start(), calls=%async_computation.10 | async-start | bytes 37748736 | tf_op jit(solution)/shard_map/all_gather | solution.py:124
  176.5 922.2 %all-gather.14.cloned.1.call-start = ((), (), s32[]{:S(2)}) async-start(), calls=%async_computation.11 | async-start | bytes 18874368 | tf_op jit(solution)/shard_map/all_gather | solution.py:125
  180.3 1051.2 %all-reduce.7.cloned.1.call-start = ((), (), s32[]{:S(2)}) async-start(), calls=%async_computation.12 | async-start | bytes 5242880 | tf_op jit(solution)/shard_map/psum | solution.py:171
  231.4 657.1 %copy-start.24 = (f32[640]{0:T(1024)}, f32[640]{0:T(1024)S(1)}, u32[]{:S(2)}) copy-start(f32[640]{0:T(1024)S(1)} %multiply_reduce_fusion) | copy-start | bytes 7684
  231.5 657.1 %copy-start.20 = (f32[640]{0:T(1024)}, f32[640]{0:T(1024)S(1)}, u32[]{:S(2)}) copy-start(f32[640]{0:T(1024)S(1)} %fusion.60) | copy-start | bytes 7684
  888.6 210.1 %copy-start.8 = (bf16[640,2048]{1,0:T(8,128)(2,1)S(1)}, bf16[640,2048]{1,0:T(8,128)(2,1)}, u32[]{:S(2)}) copy-start(bf16[640,2048]{1,0:T(8,128)(2,1)} %param.22) | copy-start | bytes 7864324
  1173.2 205.3 %all-reduce.9.cloned.1.call-start = ((), (), s32[]{:S(2)}) async-start(), calls=%async_computation.19 | async-start | bytes 11796480 | tf_op jit(solution)/shard_map/psum | solution.py:149
  1264.6 113.9 %copy-start.27 = (f32[1,2048]{1,0:T(1,128)S(1)}, f32[1,2048]{1,0:T(1,128)}, u32[]{:S(2)}) copy-start(f32[1,2048]{1,0:T(1,128)} %copy-done.26) | copy-start | bytes 24580
  1264.6 113.9 %copy-start.29 = (f32[640]{0:T(1024)S(1)}, f32[640]{0:T(1024)}, u32[]{:S(2)}) copy-start(f32[640]{0:T(1024)} %copy-done.28) | copy-start | bytes 7684
  1264.6 229.9 %reduce-scatter.19.cloned.1.call-start = ((), (), s32[]{:S(2)}) async-start(), calls=%async_computation.18 | async-start | bytes 589824
  1387.0 133.7 %reduce-scatter.13.cloned.1.call-start = ((), (), s32[]{:S(2)}) async-start(), calls=%async_computation.15 | async-start | bytes 2359296 | tf_op jit(solution)/shard_map/reduce_scatter | solution.py:210
  1392.9 199.2 %reduce-scatter.9.cloned.1.call-start = ((), (), s32[]{:S(2)}) async-start(), calls=%async_computation.13 | async-start | bytes 2359296 | tf_op jit(solution)/shard_map/reduce_scatter | solution.py:204
  1397.6 265.9 %reduce-scatter.11.cloned.1.call-start = ((), (), s32[]{:S(2)}) async-start(), calls=%async_computation.14 | async-start | bytes 2359296 | tf_op jit(solution)/shard_map/reduce_scatter | solution.py:207
  1402.1 547.4 %reduce-scatter.17.cloned.1.call-start = ((), (), s32[]{:S(2)}) async-start(), calls=%async_computation.17 | async-start | bytes 18874368 | tf_op jit(solution)/shard_map/reduce_scatter | solution.py:216
  1422.0 1073.3 %reduce-scatter.15.cloned.1.call-start = ((), (), s32[]{:S(2)}) async-start(), calls=%async_computation.16 | async-start | bytes 37748736 | tf_op jit(solution)/shard_map/reduce_scatter | solution.py:213
  1494.4 169.1 %copy-start.13 = (f32[256,512]{1,0:T(8,128)S(1)}, f32[256,512]{1,0:T(8,128)}, u32[]{:S(2)}) copy-start(f32[256,512]{1,0:T(8,128)} %param.25) | copy-start | bytes 1572868
  1494.4 169.1 %copy-start.14 = (f32[256,512]{1,0:T(8,128)S(1)}, f32[256,512]{1,0:T(8,128)}, u32[]{:S(2)}) copy-start(f32[256,512]{1,0:T(8,128)} %param.37) | copy-start | bytes 1572868
  1494.4 169.1 %copy-start.15 = (f32[256,512]{1,0:T(8,128)S(1)}, f32[256,512]{1,0:T(8,128)}, u32[]{:S(2)}) copy-start(f32[256,512]{1,0:T(8,128)} %param.31) | copy-start | bytes 1572868
  (27 other events, 529.9 us)
Sparse Core Ops, SparseCore 0:
  10.7 51.9 all-gather.7
  65.5 47.7 all-gather.5
  115.9 49.5 all-gather.9
  170.5 58.0 all-reduce.4
  230.6 637.8 all-gather.11
  870.9 227.7 all-gather.13
  1173.3 58.1 all-reduce.6
  1264.7 113.6 all-reduce.8
  1387.1 62.0 reduce-scatter.18
  1453.6 67.0 reduce-scatter.12
  1525.2 66.8 reduce-scatter.8
  1596.5 66.9 reduce-scatter.10
  1667.7 281.6 reduce-scatter.16
  1953.1 542.2 reduce-scatter.14
where the time goes:
time: 2530 us; the launch traced here: 2520 us
  waiting for transfers between devices  2120 us (84%)
  matrix products  248 us (10%)
  other arithmetic  109 us (4%)
    all_gather x1, waiting for transfers between devices, shards(): lax.all_gather(w_gateup.astype(bf), 'dp', axis=1, tiled=True)  634 us
    reduce_scatter x1, waiting for transfers between devices, shards(): lax.psum_scatter(gateup_grad.astype(jnp.bfloat16), 'dp', scatter_dimensio...  535 us
    reduce_scatter x1, waiting for transfers between devices, shards(): lax.psum_scatter(down_grad.astype(jnp.bfloat16), 'dp', scatter_dimension=...  284 us
    all_gather x1, waiting for transfers between devices, shards(): lax.all_gather(w_down.astype(bf), 'dp', axis=1, tiled=True)  193 us
    psum x1, waiting for transfers between devices, shards(): lax.psum(jnp.dot(hidden, down_w, preferred_element_type=fl).astype(jnp.bf...  114 us
    dot_general x6, matrix products, times_trans(): lax.dot_general(left, right, (((1,), (1,)), ((), ())), preferred_element_...  88.6 us
    dot_general x6, matrix products, inner_rows(): lax.dot_general(left, right, (((0,), (0,)), ((), ())), preferred_element_...  72.8 us
    reduce_scatter x1, waiting for transfers between devices, shards(): lax.psum_scatter(query_grad.astype(jnp.bfloat16), 'dp', scatter_dimension...  68.7 us
  transfers between devices with their start and end apart: 14, of which 13 were waited for; matrix products, arithmetic and copies ran while one was open for 8% of the time, Pallas kernels for 0%

commit v1 on v0

v1 whole, which is shorter than its diff:
```python
import jax
import jax.numpy as jnp
from jax import lax
from jax.sharding import PartitionSpec as P

HD = 256
ZN = 4

norm_eps = 1e-06
beta_first = 0.9
beta_second = 0.95
learn_rate = 0.01
decay_rate = 0.1
adam_eps = 1e-08
masked_score = -1e30

bf = jnp.bfloat16
fl = jnp.float32


def rms_scale(values, gain):
    inverse = lax.rsqrt(jnp.mean(values * values, axis=-1, keepdims=True) + norm_eps)
    return values * inverse * gain


def dot(left, right):
    return jnp.dot(left, right, preferred_element_type=fl)


def inner_rows(left, right):
    return lax.dot_general(left, right, (((0,), (0,)), ((), ())), preferred_element_type=fl)


def times_trans(left, right):
    return lax.dot_general(left, right, (((1,), (1,)), ((), ())), preferred_element_type=fl)


def slot_scores(query, keyval, length):
    slot = query.shape[0]
    heads = query.shape[1] // HD
    places = jnp.arange(slot)
    allowed = (places[None, :] <= places[:, None]) & (places[None, :] < length)
    raw = jnp.einsum(
        "qhd,kd->hqk",
        query.reshape(slot, heads, HD),
        keyval[:, :HD],
        preferred_element_type=fl,
    )
    return jnp.where(allowed[None], raw * HD ** (-0.5), masked_score)


def slot_forward(query, keyval, length):
    scores = slot_scores(query, keyval, length)
    top = jnp.max(scores, axis=-1, keepdims=True)
    expo = jnp.exp(scores - top)
    total = jnp.sum(expo, axis=-1, keepdims=True)
    probs = expo / total
    mixed = jnp.einsum(
        "hqk,kd->qhd", probs.astype(bf), keyval[:, HD:], preferred_element_type=fl
    )
    return mixed.reshape(query.shape), (top + jnp.log(total))[..., 0]


def slot_backward(query, keyval, length, logsum, grad_mixed):
    slot, width = query.shape
    heads = width // HD
    probs = jnp.exp(slot_scores(query, keyval, length) - logsum[..., None])
    grad_three = grad_mixed.reshape(slot, heads, HD)
    grad_value = jnp.einsum("hqk,qhd->kd", probs.astype(bf), grad_three, preferred_element_type=fl)
    grad_probs = jnp.einsum("qhd,kd->hqk", grad_three, keyval[:, HD:], preferred_element_type=fl)
    grad_scores = probs * (grad_probs - jnp.sum(grad_probs * probs, axis=-1, keepdims=True))
    grad_raw = (grad_scores * HD ** (-0.5)).astype(bf)
    grad_query = jnp.einsum("hqk,kd->qhd", grad_raw, keyval[:, :HD], preferred_element_type=fl)
    grad_key = jnp.einsum(
        "hqk,qhd->kd", grad_raw, query.reshape(slot, heads, HD), preferred_element_type=fl
    )
    return grad_query.reshape(slot, width), jnp.concatenate([grad_key, grad_value], axis=1)


def adamw(weight, grad, first, second, decay):
    first_new = beta_first * first + (1.0 - beta_first) * grad
    second_new = beta_second * second + (1.0 - beta_second) * grad * grad
    update = -learn_rate * (first_new / (jnp.sqrt(second_new) + adam_eps) + decay * weight)
    return (grad, first_new, second_new, update)


def swap(value, step):
    axis, bit = step
    return lax.ppermute(value, axis, [(i, i ^ bit) for i in range(lax.axis_size(axis))])


def offset(position, steps, axis):
    total = 0
    for i, (name, bit) in enumerate(steps):
        if name == axis and position >> i & 1:
            total ^= bit
    return total


def gather(value, steps):
    parts = value[None]
    for step in steps:
        parts = jnp.concatenate([parts, swap(parts, step)], axis=0)
    return parts


def reduce(parts, steps):
    for step in reversed(steps):
        half = parts.shape[0] // 2
        got = swap(parts[half:].astype(bf), step)
        parts = parts[:half].astype(fl) + got.astype(fl)
    return parts[0]


def take(array, index, axis=0):
    return lax.dynamic_index_in_dim(array, index, axis, keepdims=False)


def pick(array, me, steps, axis_name, axis=0):
    return jnp.stack(
        [take(array, me ^ offset(p, steps, axis_name), axis) for p in range(2 ** len(steps))]
    )


def place(parts, me, steps, axis_name, axis=0):
    count = parts.shape[0]
    block = parts.shape[1:]
    shape = block[:axis] + (count,) + block[axis:]
    out = jnp.zeros(shape, parts.dtype)
    for p in range(count):
        out = lax.dynamic_update_index_in_dim(
            out, parts[p], me ^ offset(p, steps, axis_name), axis
        )
    return out


def shards(
    tokens,
    cotangent,
    lengths,
    w_query,
    w_keyval,
    w_output,
    w_gateup,
    w_down,
    norm_gains,
    first_query,
    first_keyval,
    first_output,
    first_gateup,
    first_down,
    first_gains,
    second_query,
    second_keyval,
    second_output,
    second_gateup,
    second_down,
    second_gains,
):
    dp = lax.axis_size("dp")
    tn = lax.axis_size("tensor")
    rn = dp // ZN
    me = lax.axis_index("dp")
    z, r = me // rn, me % rn
    t = lax.axis_index("tensor")
    z_steps = [("dp", 2 * rn), ("dp", rn)]
    r_steps = [("dp", 1 << i) for i in reversed(range(rn.bit_length() - 1))]
    t_steps = [("tensor", 1 << i) for i in reversed(range(tn.bit_length() - 1))]
    dp_steps = z_steps + r_steps
    group_steps = z_steps + t_steps

    model = tokens.shape[1]
    rows = model // dp
    slot = tokens.shape[0]
    quarter = slot // tn
    width = w_query.shape[1]
    kvt = w_keyval.shape[1] // tn
    ff = w_down.shape[0] // ZN

    gain_full = place(
        gather(norm_gains.astype(bf), dp_steps), me, dp_steps, "dp", axis=1
    ).reshape(2, model).astype(fl)
    own_keyval = lax.dynamic_slice_in_dim(w_keyval, t * kvt, kvt, 1)
    qkv_w = place(
        gather(jnp.concatenate([w_query, own_keyval], axis=1).astype(bf), dp_steps),
        me, dp_steps, "dp",
    ).reshape(model, width + kvt)
    output_w = place(
        gather(w_output.astype(bf), dp_steps), me, dp_steps, "dp", axis=1
    ).reshape(width, model)

    def zpos(k):
        return ("dp", k * rn)

    gateup_cols = w_gateup.astype(bf).reshape(2, rows, ZN, ff)
    down_rows = w_down.astype(bf).reshape(ZN, ff, rows)
    gateup_w = jnp.zeros((2, ZN, rn, rows, ff), bf)
    down_w = jnp.zeros((ff, ZN, rn, rows), bf)
    for k in range(ZN):
        block = take(gateup_cols, z ^ k, 2)
        if k:
            block = swap(block, zpos(k))
        block = place(gather(block, r_steps), r, r_steps, "dp", axis=1)
        gateup_w = lax.dynamic_update_index_in_dim(gateup_w, block, z ^ k, 1)
    for k in range(ZN):
        block = take(down_rows, z ^ k, 0)
        if k:
            block = swap(block, zpos(k))
        block = place(gather(block, r_steps), r, r_steps, "dp", axis=1)
        down_w = lax.dynamic_update_index_in_dim(down_w, block, z ^ k, 1)
    gateup_w = gateup_w.reshape(2, model, ff)
    down_w = down_w.reshape(ff, model)

    x = tokens.astype(fl)
    length = lengths[0]
    normed_one = rms_scale(x, gain_full[0]).astype(bf)
    projected = dot(normed_one, qkv_w).astype(bf)
    query = projected[:, :width]
    keyval = place(
        gather(projected[:, width:], t_steps), t, t_steps, "tensor", axis=1
    ).reshape(slot, tn * kvt)
    mixed, logsum = slot_forward(query, keyval, length)
    mixed = mixed.astype(bf)
    attn_part = dot(mixed, output_w).astype(bf).reshape(tn, quarter, model)
    attn = reduce(pick(attn_part, t, t_steps, "tensor"), t_steps)
    x_own = lax.dynamic_slice_in_dim(x, t * quarter, quarter, 0)
    resid = x_own + attn
    normed_two_own = rms_scale(resid, gain_full[1]).astype(bf)

    group = ZN * tn * quarter
    normed_two = gather(normed_two_own, group_steps).reshape(group, model)
    cot_own = lax.dynamic_slice_in_dim(cotangent, t * quarter, quarter, 0)
    valid = (t * quarter + jnp.arange(quarter) < length)[:, None]
    grad_own = jnp.where(valid, cot_own, jnp.zeros_like(cot_own))
    grad_low = gather(grad_own, group_steps).reshape(group, model)

    gate = dot(normed_two, gateup_w[0])
    upper = dot(normed_two, gateup_w[1])
    hidden = (jax.nn.gelu(gate, approximate=True) * upper).astype(bf)
    ff_part = dot(hidden, down_w).astype(bf).reshape(ZN * tn, quarter, model)
    out_own = resid + reduce(ff_part, group_steps)
    block_output = place(gather(out_own, t_steps), t, t_steps, "tensor").reshape(slot, model)

    grad_hidden = times_trans(grad_low, down_w)
    _, pull_gelu = jax.vjp(
        lambda left, right: jax.nn.gelu(left, approximate=True) * right, gate, upper
    )
    grad_gate, grad_up = pull_gelu(grad_hidden)
    grad_gate = grad_gate.astype(bf)
    grad_up = grad_up.astype(bf)
    grad_normed = (times_trans(grad_gate, gateup_w[0]) + times_trans(grad_up, gateup_w[1])).astype(bf)
    grad_normed_two = reduce(grad_normed.reshape(ZN * tn, quarter, model), group_steps)

    def columns(array, j):
        return take(array.reshape(group, ZN, rn, rows), r ^ j, 2).reshape(group, ZN * rows)

    def scatter_z(sums, axis):
        parts = []
        for k in range(ZN):
            block = take(sums, z ^ k, 0).astype(bf)
            parts.append(swap(block, zpos(k)) if k else block)
        shape = parts[0].shape
        out = jnp.zeros(shape[:axis] + (ZN,) + shape[axis:], bf)
        for k in range(ZN):
            out = lax.dynamic_update_index_in_dim(out, parts[k], z ^ k, axis)
        return out

    r_offsets = [offset(p, r_steps, "dp") for p in range(rn)]
    down_parts = jnp.stack(
        [
            inner_rows(hidden, columns(grad_low, j)).astype(bf).reshape(ff, ZN, rows)
            for j in r_offsets
        ]
    )
    down_sum = reduce(down_parts, r_steps)
    down_shard = scatter_z(jnp.moveaxis(down_sum, 1, 0), 0).reshape(ZN * ff, rows).astype(fl)

    shards_gu = []
    for grad in (grad_gate, grad_up):
        parts = jnp.stack(
            [
                inner_rows(columns(normed_two, j), grad).astype(bf).reshape(ZN, rows, ff)
                for j in r_offsets
            ]
        )
        sums = reduce(parts, r_steps)
        shards_gu.append(scatter_z(sums, 1).reshape(rows, ZN * ff).astype(fl))
    gateup_shard = jnp.stack(shards_gu)

    _, pull_second = jax.vjp(rms_scale, resid, gain_full[1])
    grad_resid_norm, grad_gain_two = pull_second(grad_normed_two)
    grad_resid = grad_own.astype(fl) + grad_resid_norm
    grad_attn = place(gather(grad_resid.astype(bf), t_steps), t, t_steps, "tensor").reshape(slot, model)

    output_grad = inner_rows(mixed, grad_attn).astype(bf)
    grad_mixed = times_trans(grad_attn, output_w).astype(bf)
    grad_query, grad_keyval = slot_backward(query, keyval, length, logsum, grad_mixed)
    keyval_parts = grad_keyval.astype(bf).reshape(slot, tn, kvt)
    keyval_low = reduce(pick(keyval_parts, t, t_steps, "tensor", axis=1), t_steps).astype(bf)
    grad_projected = jnp.concatenate([grad_query.astype(bf), keyval_low], axis=1)
    one_parts = times_trans(grad_projected, qkv_w).astype(bf).reshape(tn, quarter, model)
    grad_normed_one = reduce(pick(one_parts, t, t_steps, "tensor"), t_steps)
    qkv_grad = inner_rows(normed_one, grad_projected).astype(bf)
    _, pull_first = jax.vjp(rms_scale, x_own, gain_full[0])
    grad_x_norm, grad_gain_one = pull_first(grad_normed_one)
    input_own = grad_resid + grad_x_norm
    input_grad = place(gather(input_own, t_steps), t, t_steps, "tensor").reshape(slot, model)

    qkv_shard = reduce(
        pick(qkv_grad.reshape(dp, rows, width + kvt), me, dp_steps, "dp"), dp_steps
    )
    query_shard = qkv_shard[:, :width]
    keyval_shard = place(
        gather(qkv_shard[:, width:].astype(bf), t_steps), t, t_steps, "tensor", axis=1
    ).reshape(rows, tn * kvt).astype(fl)
    output_shard = reduce(
        pick(output_grad.reshape(width, dp, rows), me, dp_steps, "dp", axis=1), dp_steps
    )
    gains_grad = jnp.stack([grad_gain_one, grad_gain_two]).reshape(2, dp, rows)
    gains_parts = pick(gains_grad, me, dp_steps, "dp", axis=1)
    for step in reversed(dp_steps):
        half = gains_parts.shape[0] // 2
        gains_parts = gains_parts[:half] + swap(gains_parts[half:], step)
    gains_shard = gains_parts[0]
    for step in t_steps:
        gains_shard = gains_shard + swap(gains_shard, step)

    qa = adamw(w_query, query_shard, first_query, second_query, decay_rate)
    ka = adamw(w_keyval, keyval_shard, first_keyval, second_keyval, decay_rate)
    oa = adamw(w_output, output_shard, first_output, second_output, decay_rate)
    ga = adamw(w_gateup, gateup_shard, first_gateup, second_gateup, decay_rate)
    da = adamw(w_down, down_shard, first_down, second_down, decay_rate)
    na = adamw(norm_gains, gains_shard, first_gains, second_gains, 0.0)
    return (block_output, input_grad, *qa, *ka, *oa, *ga, *da, *na)


def solution(mesh):
    query = P("dp", "tensor")
    keyval = P("dp", None)
    output = P("tensor", "dp")
    gateup = P(None, "dp", "tensor")
    gains = P(None, "dp")
    weights = (query, keyval, output, gateup, output, gains)
    return jax.shard_map(
        shards,
        mesh=mesh,
        in_specs=(P("dp", None), P("dp", None), P("dp")) + weights * 3,
        out_specs=(P("dp", None), P("dp", None)) + tuple(w for w in weights for _ in range(4)),
        check_vma=False,
    )
```

time: 2530 us -> 1470 us (0.58)
  waiting for transfers between devices: 2120 us -> 455 us
  local copies, waits for them, and re-layouts: 5.61 us -> 552 us
  starting transfers between devices: 0.97 us -> 114 us
  matrix products: 248 us -> 210 us
    reduce_scatter x5 -> x0, waiting for transfers between devices: 981 us -> none  [the longest x1 535 us: shards(): lax.psum_scatter(gateup_grad.astype(jnp.bfloat16), 'dp', scatter_dimensio...]
    all_gather x5 -> x0, waiting for transfers between devices: 941 us -> none  [the longest x1 634 us: shards(): lax.all_gather(w_gateup.astype(bf), 'dp', axis=1, tiled=True)]
    ppermute x0 -> x78, waiting for transfers between devices: none -> 455 us  [swap(): lax.ppermute(value, axis, [(i, i ^ bit) for i in range(lax.axis_size(axis...]
    dynamic_update_slice x0 -> x76, local copies, waits for them, and re-layouts: none -> 210 us  [the longest x12 142 us: scatter_z(): out = lax.dynamic_update_index_in_dim(out, parts[k], z ^ k, axis)]
    psum x3 -> x0, waiting for transfers between devices: 202 us -> none  [the longest x1 114 us: shards(): lax.psum(jnp.dot(hidden, down_w, preferred_element_type=fl).astype(jnp.bf...]
    dynamic_slice x0 -> x14, local copies, waits for them, and re-layouts: none -> 150 us  [take(): return lax.dynamic_index_in_dim(array, index, axis, keepdims=False)]
    ppermute x0 -> x78, starting transfers between devices: none -> 114 us  [swap(): lax.ppermute(value, axis, [(i, i ^ bit) for i in range(lax.axis_size(axis...]
    broadcast_in_dim x0 -> x43, local copies, waits for them, and re-layouts: none -> 50.7 us  [the longest x12 20.7 us: shards(): down_w = lax.dynamic_update_index_in_dim(down_w, block, z ^ k, 1)]
  transfers between devices with their start and end apart: 14 -> 78, of which waited for: 13 -> 38; matrix products, arithmetic and copies ran while one was open for 8% -> 42% of each run, Pallas kernels for 0% -> 0%
where the time goes in v1:
time: 1470 us; the launch traced here: 1450 us
  local copies, waits for them, and re-layouts  552 us (38%)
  waiting for transfers between devices  455 us (31%)
  matrix products  210 us (14%)
  other arithmetic  116 us (8%)
  starting transfers between devices  114 us (8%)
    ppermute x78, waiting for transfers between devices, swap(): lax.ppermute(value, axis, [(i, i ^ bit) for i in range(lax.axis_size(axis...  455 us
    dynamic_slice x14, local copies, waits for them, and re-layouts, take(): return lax.dynamic_index_in_dim(array, index, axis, keepdims=False)  150 us
    dynamic_update_slice x12, local copies, waits for them, and re-layouts, scatter_z(): out = lax.dynamic_update_index_in_dim(out, parts[k], z ^ k, axis)  142 us
    ppermute x78, starting transfers between devices, swap(): lax.ppermute(value, axis, [(i, i ^ bit) for i in range(lax.axis_size(axis...  114 us
    dot_general x5, matrix products, times_trans(): lax.dot_general(left, right, (((1,), (1,)), ((), ())), preferred_element_...  77.8 us
    dynamic_update_slice x56, local copies, waits for them, and re-layouts, place(): lax.dynamic_update_index_in_dim(out, parts[p], me ^ offset(p, steps, axis...  57.1 us
    dot_general x8, matrix products, inner_rows(): lax.dot_general(left, right, (((0,), (0,)), ((), ())), preferred_element_...  55.6 us
    dot_general x5, matrix products, dot(): return jnp.dot(left, right, preferred_element_type=fl)  54.8 us
  transfers between devices with their start and end apart: 78, of which 38 were waited for; matrix products, arithmetic and copies ran while one was open for 42% of the time, Pallas kernels for 0%

profile of v1, /device:TPU:0, one launch (start us, length us, event | category | flops | bytes accessed | tf_op | source)
XLA Modules:
  0.0 1450.4 jit_solution(11946680034964384743)
XLA Ops:
  162.2 27.8 %collective-permute-done.37 = bf16[1,160,2048]{2,1,0:T(8,128)(2,1)S(1)} collective-permute-done((bf16[1,160,2048]{2,1,0:T(8,128)(2,1)S(1)}, bf16[1,160,2048]{2,1,0:T(8,128)(2,1)S(1)}, u32[]{:S(2)}, u32[]{:S(2)}) %collective-permute-start.37) | collective-permute-done | bytes 655392 | tf_op jit(solution)/shard_map/ppermute | solution.py:89
  204.4 27.2 %collective-permute-done.38 = bf16[2,160,2048]{2,1,0:T(8,128)(2,1)S(1)} collective-permute-done((bf16[2,160,2048]{2,1,0:T(8,128)(2,1)S(1)}, bf16[2,160,2048]{2,1,0:T(8,128)(2,1)S(1)}, u32[]{:S(2)}, u32[]{:S(2)}) %collective-permute-start.38) | collective-permute-done | bytes 1310752 | tf_op jit(solution)/shard_map/ppermute | solution.py:89
  233.9 25.7 %collective-permute-done.14 = bf16[2,160,2048]{2,1,0:T(8,128)(2,1)S(1)} collective-permute-done((bf16[2,160,2048]{2,1,0:T(8,128)(2,1)S(1)}, bf16[2,160,2048]{2,1,0:T(8,128)(2,1)S(1)}, u32[]{:S(2)}, u32[]{:S(2)}) %collective-permute-start.14) | collective-permute-done | bytes 1310752 | tf_op jit(solution)/shard_map/ppermute | solution.py:89
  385.4 43.8 %collective-permute-done.20 = bf16[2,256,1024]{2,1,0:T(8,128)(2,1)} collective-permute-done((bf16[2,256,1024]{2,1,0:T(8,128)(2,1)}, bf16[2,256,1024]{2,1,0:T(8,128)(2,1)}, u32[]{:S(2)}, u32[]{:S(2)}) %collective-permute-start.20) | collective-permute-done | bytes 1048608 | tf_op jit(solution)/shard_map/ppermute | solution.py:89
  563.5 30.0 %multiply_convert_fusion = (bf16[2560,1024]{1,0:T(8,128)(2,1)}, bf16[2560,1024]{1,0:T(8,128)(2,1)}, bf16[2560,1024]{1,0:T(8,128)(2,1)}) fusion(f32[2560,1024]{1,0:T(8,128)} %fusion.133, f32[2560,1024]{1,0:T(8,128)} %fusion.134, bf16[2560,2048]{1,0:T(8,128)(2,1)} %bitcast.19, bf16[1024,2048]{0,1:T(8,128)(2,1)} %bitcast.35), kind=kOutput, calls=%fused_computation.15 | convolution fusion | flops 10805575680 | bytes 51380224 | tf_op jit(solution)/shard_map/dot_general | solution.py:35
  612.0 47.2 %constant_dynamic-slice_fusion.16 = (bf16[2560,4,1,256]{3,2,1,0:T(2,128)(2,1)}, bf16[2560,4,1,256]{3,2,1,0:T(2,128)(2,1)}, bf16[2560,4,1,256]{3,2,1,0:T(2,128)(2,1)}, bf16[2560,4,1,256]{3,2,1,0:T(2,128)(2,1)}) fusion(bf16[2560,4,2,256]{3,2,1,0:T(2,128)(2,1)} %reshape_reshape.5, s32[]{:T(128)S(6)} %select_n.247, s32[]{:T(128)S(6)} %select_n.246, ...), kind=kLoop, calls=%fused_computation.286 | loop fusion | bytes 41943048 | tf_op jit(solution)/shard_map/jit(dynamic_index_in_dim)/dynamic_slice | solution.py:116
  659.1 21.1 %copy.198 = bf16[2560,4,1,256]{0,3,1,2:T(8,128)(2,1)} copy(bf16[2560,4,1,256]{3,2,1,0:T(2,128)(2,1)} %get-tuple-element.148) | data formatting | bytes 10485760 | tf_op jit(solution)/shard_map/jit(dynamic_index_in_dim)/dynamic_slice | solution.py:116
  697.2 20.1 %add_convert_fusion = bf16[2560,2048]{1,0:T(8,128)(2,1)} fusion(f32[2560,2048]{1,0:T(8,128)} %fusion.135, bf16[2560,1024]{1,0:T(8,128)(2,1)} %get-tuple-element.67, bf16[2048,1024]{1,0:T(8,128)(2,1)} %bitcast.477), kind=kOutput, calls=%fused_computation.1 | convolution fusion | flops 10747904000 | bytes 40894464 | tf_op jit(solution)/shard_map/dot_general | solution.py:35
  727.6 21.1 %copy.208 = bf16[2560,4,1,256]{0,3,1,2:T(8,128)(2,1)} copy(bf16[2560,4,1,256]{3,2,1,0:T(2,128)(2,1)} %get-tuple-element.70) | data formatting | bytes 10485760 | tf_op jit(solution)/shard_map/jit(dynamic_index_in_dim)/dynamic_slice | solution.py:116
  774.0 21.1 %copy.207 = bf16[2560,4,1,256]{0,3,1,2:T(8,128)(2,1)} copy(bf16[2560,4,1,256]{3,2,1,0:T(2,128)(2,1)} %get-tuple-element.71) | data formatting | bytes 10485760 | tf_op jit(solution)/shard_map/jit(dynamic_index_in_dim)/dynamic_slice | solution.py:116
  795.6 21.0 %copy.197 = bf16[2560,4,1,256]{0,3,1,2:T(8,128)(2,1)} copy(bf16[2560,4,1,256]{3,2,1,0:T(2,128)(2,1)} %get-tuple-element.147) | data formatting | bytes 10485760 | tf_op jit(solution)/shard_map/jit(dynamic_index_in_dim)/dynamic_slice | solution.py:116
  875.1 35.6 %collective-permute-done.65 = bf16[1,4,256,1024]{3,2,1,0:T(8,128)(2,1)S(1)} collective-permute-done((bf16[1,4,256,1024]{3,2,1,0:T(8,128)(2,1)}, bf16[1,4,256,1024]{3,2,1,0:T(8,128)(2,1)S(1)}, u32[]{:S(2)}, u32[]{:S(2)}) %collective-permute-start.65) | collective-permute-done | bytes 2097184 | tf_op jit(solution)/shard_map/ppermute | solution.py:89
  917.0 31.8 %collective-permute-done.63 = bf16[256,1024]{1,0:T(8,128)(2,1)} collective-permute-done((bf16[256,1024]{1,0:T(8,128)(2,1)S(1)}, bf16[256,1024]{1,0:T(8,128)(2,1)}, u32[]{:S(2)}, u32[]{:S(2)}) %collective-permute-start.63) | collective-permute-done | bytes 524320 | tf_op jit(solution)/shard_map/ppermute | solution.py:89
  956.0 18.5 %dynamic_update_slice.337 = bf16[256,4,1024]{2,1,0:T(4,128)(2,1)} dynamic-update-slice(bf16[256,4,1024]{2,1,0:T(4,128)(2,1)} %broadcast.180.clone.1, bf16[256,1,1024]{2,1,0:T(2,128)(2,1)S(1)} %copy.199, s32[]{:T(128)} %constant.463.clone.1, s32[]{:T(128)S(6)} %select_n.244, s32[]{:T(128)} %constant.463.clone.1) | dynamic-update-slice | bytes 1048580 | tf_op jit(solution)/shard_map/jit(dynamic_update_index_in_dim)/dynamic_update_slice | solution.py:265
  992.4 18.5 %dynamic_update_slice.338 = bf16[256,4,1024]{2,1,0:T(4,128)(2,1)} dynamic-update-slice(bf16[256,4,1024]{2,1,0:T(4,128)(2,1)} %dynamic_update_slice.337, bf16[256,1,1024]{2,1,0:T(2,128)(2,1)S(1)} %copy.200, s32[]{:T(128)} %constant.463.clone.1, s32[]{:T(128)S(6)} %select_n.248, s32[]{:T(128)} %constant.463.clone.1) | dynamic-update-slice | bytes 1048580 | tf_op jit(solution)/shard_map/jit(dynamic_update_index_in_dim)/dynamic_update_slice | solution.py:265
  1010.9 18.5 %dynamic_update_slice.339 = bf16[256,4,1024]{2,1,0:T(4,128)(2,1)} dynamic-update-slice(bf16[256,4,1024]{2,1,0:T(4,128)(2,1)} %dynamic_update_slice.338, bf16[256,1,1024]{2,1,0:T(2,128)(2,1)S(1)} %copy.201, s32[]{:T(128)} %constant.463.clone.1, s32[]{:T(128)S(6)} %select_n.249, s32[]{:T(128)} %constant.463.clone.1) | dynamic-update-slice | bytes 1048580 | tf_op jit(solution)/shard_map/jit(dynamic_update_index_in_dim)/dynamic_update_slice | solution.py:265
  1029.4 18.5 %dynamic_update_slice.340 = bf16[256,4,1024]{2,1,0:T(4,128)(2,1)} dynamic-update-slice(bf16[256,4,1024]{2,1,0:T(4,128)(2,1)} %dynamic_update_slice.339, bf16[256,1,1024]{2,1,0:T(2,128)(2,1)S(1)} %copy.202, s32[]{:T(128)} %constant.463.clone.1, s32[]{:T(128)S(6)} %select_n.250, s32[]{:T(128)} %constant.463.clone.1) | dynamic-update-slice | bytes 1048580 | tf_op jit(solution)/shard_map/jit(dynamic_update_index_in_dim)/dynamic_update_slice | solution.py:265
  1051.2 33.2 %collective-permute-start.71 = (bf16[1024,256]{0,1:T(8,128)(2,1)}, bf16[1024,256]{0,1:T(8,128)(2,1)}, u32[]{:S(2)}, u32[]{:S(2)}) collective-permute-start(bf16[1024,256]{0,1:T(8,128)(2,1)} %get-tuple-element.102), channel_id=1, source_target_pairs={{0,16},{4,20},{8,24},{12,28},{16,0},{20,4},{24,8},{28,12},{1,17},{... | collective-permute-start | bytes 1572872 | tf_op jit(solution)/shard_map/ppermute | solution.py:89
  1094.6 18.5 %dynamic_update_slice.342 = bf16[256,4,1024]{2,1,0:T(4,128)(2,1)} dynamic-update-slice(bf16[256,4,1024]{2,1,0:T(4,128)(2,1)} %copy-done.18, bf16[256,1,1024]{2,1,0:T(2,128)(2,1)S(1)} %copy.204, s32[]{:T(128)} %constant.463.clone.1, s32[]{:T(128)S(6)} %select_n.248, s32[]{:T(128)} %constant.463.clone.1) | dynamic-update-slice | bytes 1048580 | tf_op jit(solution)/shard_map/jit(dynamic_update_index_in_dim)/dynamic_update_slice | solution.py:265
  1113.1 18.7 %dynamic_update_slice.343 = bf16[256,4,1024]{2,1,0:T(4,128)(2,1)} dynamic-update-slice(bf16[256,4,1024]{2,1,0:T(4,128)(2,1)} %dynamic_update_slice.342, bf16[256,1,1024]{2,1,0:T(2,128)(2,1)} %copy.205, s32[]{:T(128)} %constant.463.clone.1, s32[]{:T(128)S(6)} %select_n.249, s32[]{:T(128)} %constant.463.clone.1) | dynamic-update-slice | bytes 1048580 | tf_op jit(solution)/shard_map/jit(dynamic_update_index_in_dim)/dynamic_update_slice | solution.py:265
  1131.8 18.5 %dynamic_update_slice.344 = bf16[256,4,1024]{2,1,0:T(4,128)(2,1)} dynamic-update-slice(bf16[256,4,1024]{2,1,0:T(4,128)(2,1)} %dynamic_update_slice.343, bf16[256,1,1024]{2,1,0:T(2,128)(2,1)S(1)} %copy-done.29, s32[]{:T(128)} %constant.463.clone.1, s32[]{:T(128)S(6)} %select_n.250, s32[]{:T(128)} %constant.463.clone.1) | dynamic-update-slice | bytes 1048580 | tf_op jit(solution)/shard_map/jit(dynamic_update_index_in_dim)/dynamic_update_slice | solution.py:265
  1176.5 19.6 %add_multiply_fusion = (f32[2,256,4096]{2,1,0:T(8,128)}, f32[2,256,4096]{2,1,0:T(8,128)}, f32[2,256,4096]{2,1,0:T(8,128)}, f32[2,256,4096]{2,1,0:T(8,128)}) fusion(f32[2,256,4096]{2,1,0:T(8,128)} %param.27, f32[2,256,4096]{2,1,0:T(8,128)} %param.39, f32[2,256,4096]{2,1,0:T(8,128)} %param.33, bf16[1,256,4096]{2,1,0:T(8,128)(2,1)} %convert_element_type.495, ...), kind=kLoop, calls=%fused_computation.19 | loop fusion | flops 29360128 | bytes 62914560 | tf_op jit(solution)/shard_map/mul | solution.py:83
  1247.3 19.0 %collective-permute-done.33 = bf16[2,160,2048]{2,1,0:T(8,128)(2,1)} collective-permute-done((bf16[2,160,2048]{2,1,0:T(8,128)(2,1)}, bf16[2,160,2048]{2,1,0:T(8,128)(2,1)}, u32[]{:S(2)}, u32[]{:S(2)}) %collective-permute-start.33) | collective-permute-done | bytes 1310752 | tf_op jit(solution)/shard_map/ppermute | solution.py:89
  1278.1 19.4 %collective-permute-done.34 = bf16[1,160,2048]{2,1,0:T(8,128)(2,1)S(1)} collective-permute-done((bf16[1,160,2048]{2,1,0:T(8,128)(2,1)S(1)}, bf16[1,160,2048]{2,1,0:T(8,128)(2,1)S(1)}, u32[]{:S(2)}, u32[]{:S(2)}) %collective-permute-start.34) | collective-permute-done | bytes 655392 | tf_op jit(solution)/shard_map/ppermute | solution.py:89
  (646 shorter events, 852.2 us)
Async XLA Ops:
  140.8 49.2 %collective-permute-start.37 = (bf16[1,160,2048]{2,1,0:T(8,128)(2,1)S(1)}, bf16[1,160,2048]{2,1,0:T(8,128)(2,1)S(1)}, u32[]{:S(2)}, u32[]{:S(2)}) collective-permute-start(bf16[1,160,2048]{2,1,0:T(8,128)(2,1)S(1)} %get-tuple-element.60), channel_id=1, source_target_pairs={{0,16},{4,20},{8,24},{12,28},{16,0},{20,4},{24,8},{28,12},{1,17},{... | collective-permute-start | bytes 1966088 | tf_op jit(solution)/shard_map/ppermute | solution.py:89
  203.7 55.9 %collective-permute-start.14 = (bf16[2,160,2048]{2,1,0:T(8,128)(2,1)S(1)}, bf16[2,160,2048]{2,1,0:T(8,128)(2,1)S(1)}, u32[]{:S(2)}, u32[]{:S(2)}) collective-permute-start(bf16[2,160,2048]{2,1,0:T(8,128)(2,1)S(1)} %pad_maximum_fusion.8), channel_id=1, source_target_pairs={{0,8},{4,12},{8,0},{12,4},{16,24},{20,28},{24,16},{28,20},{1,9},{5... | collective-permute-start | bytes 3932168 | tf_op jit(solution)/shard_map/ppermute | solution.py:89
  233.4 133.3 %collective-permute-start.39 = (bf16[4,160,2048]{2,1,0:T(8,128)(2,1)}, bf16[4,160,2048]{2,1,0:T(8,128)(2,1)}, u32[]{:S(2)}, u32[]{:S(2)}) collective-permute-start(bf16[4,160,2048]{2,1,0:T(8,128)(2,1)} %pad_maximum_fusion.4), channel_id=1, source_target_pairs={{0,2},{1,3},{2,0},{3,1},{4,6},{5,7},{6,4},{7,5},{8,10},{9,11},{10,... | collective-permute-start | bytes 7864328 | tf_op jit(solution)/shard_map/ppermute | solution.py:89
  261.4 111.4 %collective-permute-start.15 = (bf16[4,160,2048]{2,1,0:T(8,128)(2,1)}, bf16[4,160,2048]{2,1,0:T(8,128)(2,1)}, u32[]{:S(2)}, u32[]{:S(2)}) collective-permute-start(bf16[4,160,2048]{2,1,0:T(8,128)(2,1)} %pad_maximum_fusion.2), channel_id=1, source_target_pairs={{0,2},{1,3},{2,0},{3,1},{4,6},{5,7},{6,4},{7,5},{8,10},{9,11},{10,... | collective-permute-start | bytes 7864328 | tf_op jit(solution)/shard_map/ppermute | solution.py:89
  308.2 56.5 %collective-permute-start.17 = (bf16[1,2,256,1024]{3,2,1,0:T(8,128)(2,1)}, bf16[1,2,256,1024]{3,2,1,0:T(8,128)(2,1)}, u32[]{:S(2)}, u32[]{:S(2)}) collective-permute-start(bf16[1,2,256,1024]{3,2,1,0:T(8,128)(2,1)} %bitcast.472), channel_id=1, source_target_pairs={{0,4},{4,0},{8,12},{12,8},{16,20},{20,16},{24,28},{28,24},{1,5},{5... | collective-permute-start | bytes 3145736 | tf_op jit(solution)/shard_map/ppermute | solution.py:89
  356.9 72.3 %collective-permute-start.20 = (bf16[2,256,1024]{2,1,0:T(8,128)(2,1)}, bf16[2,256,1024]{2,1,0:T(8,128)(2,1)}, u32[]{:S(2)}, u32[]{:S(2)}) collective-permute-start(bf16[2,256,1024]{2,1,0:T(8,128)(2,1)} %bitcast.498), channel_id=1, source_target_pairs={{0,16},{4,20},{8,24},{12,28},{16,0},{20,4},{24,8},{28,12},{1,17},{... | collective-permute-start | bytes 3145736 | tf_op jit(solution)/shard_map/ppermute | solution.py:89
  364.6 66.0 %collective-permute-start.22 = (bf16[2,256,1024]{2,1,0:T(8,128)(2,1)}, bf16[2,256,1024]{2,1,0:T(8,128)(2,1)}, u32[]{:S(2)}, u32[]{:S(2)}) collective-permute-start(bf16[2,256,1024]{2,1,0:T(8,128)(2,1)} %bitcast.73), channel_id=1, source_target_pairs={{0,24},{4,28},{8,16},{12,20},{16,8},{20,12},{24,0},{28,4},{1,25},{... | collective-permute-start | bytes 3145736 | tf_op jit(solution)/shard_map/ppermute | solution.py:89
  372.8 112.0 %collective-permute-start.40 = (bf16[8,160,2048]{2,1,0:T(8,128)(2,1)}, bf16[8,160,2048]{2,1,0:T(8,128)(2,1)}, u32[]{:S(2)}, u32[]{:S(2)}) collective-permute-start(bf16[8,160,2048]{2,1,0:T(8,128)(2,1)} %pad_maximum_fusion.1), channel_id=1, source_target_pairs={{0,1},{1,0},{2,3},{3,2},{4,5},{5,4},{6,7},{7,6},{8,9},{9,8},{10,11... | collective-permute-start | bytes 15728648 | tf_op jit(solution)/shard_map/ppermute | solution.py:89
  378.6 129.5 %collective-permute-start.16 = (bf16[8,160,2048]{2,1,0:T(8,128)(2,1)}, bf16[8,160,2048]{2,1,0:T(8,128)(2,1)}, u32[]{:S(2)}, u32[]{:S(2)}) collective-permute-start(bf16[8,160,2048]{2,1,0:T(8,128)(2,1)} %pad_maximum_fusion), channel_id=1, source_target_pairs={{0,1},{1,0},{2,3},{3,2},{4,5},{5,4},{6,7},{7,6},{8,9},{9,8},{10,11... | collective-permute-start | bytes 15728648 | tf_op jit(solution)/shard_map/ppermute | solution.py:89
  383.8 61.6 %collective-permute-start.19 = (bf16[1,2,256,1024]{3,2,1,0:T(8,128)(2,1)}, bf16[1,2,256,1024]{3,2,1,0:T(8,128)(2,1)S(1)}, u32[]{:S(2)}, u32[]{:S(2)}) collective-permute-start(bf16[1,2,256,1024]{3,2,1,0:T(8,128)(2,1)} %bitcast.67), channel_id=1, source_target_pairs={{0,4},{4,0},{8,12},{12,8},{16,20},{20,16},{24,28},{28,24},{1,5},{5... | collective-permute-start | bytes 3145736 | tf_op jit(solution)/shard_map/ppermute | solution.py:89
  727.6 131.0 %collective-permute-start.41 = (bf16[8,160,2048]{2,1,0:T(8,128)(2,1)}, bf16[8,160,2048]{2,1,0:T(8,128)(2,1)}, u32[]{:S(2)}, u32[]{:S(2)}) collective-permute-start(bf16[8,160,2048]{2,1,0:T(8,128)(2,1)} %bitcast.457), channel_id=1, source_target_pairs={{0,1},{1,0},{2,3},{3,2},{4,5},{5,4},{6,7},{7,6},{8,9},{9,8},{10,11... | collective-permute-start | bytes 15728648 | tf_op jit(solution)/shard_map/ppermute | solution.py:89
  772.5 81.7 %collective-permute-start.69 = (bf16[1,1024,4,256]{1,3,2,0:T(8,128)(2,1)}, bf16[1,1024,4,256]{1,3,2,0:T(8,128)(2,1)}, u32[]{:S(2)}, u32[]{:S(2)}) collective-permute-start(bf16[1,1024,4,256]{1,3,2,0:T(8,128)(2,1)} %bitcast.153), channel_id=1, source_target_pairs={{0,4},{4,0},{8,12},{12,8},{16,20},{20,16},{24,28},{28,24},{1,5},{5... | collective-permute-start | bytes 6291464 | tf_op jit(solution)/shard_map/ppermute | solution.py:89
  795.1 73.5 %collective-permute-start.61 = (bf16[1,4,256,1024]{3,2,1,0:T(8,128)(2,1)}, bf16[1,4,256,1024]{3,2,1,0:T(8,128)(2,1)}, u32[]{:S(2)}, u32[]{:S(2)}) collective-permute-start(bf16[1,4,256,1024]{3,2,1,0:T(8,128)(2,1)} %bitcast.133), channel_id=1, source_target_pairs={{0,4},{4,0},{8,12},{12,8},{16,20},{20,16},{24,28},{28,24},{1,5},{5... | collective-permute-start | bytes 6291464 | tf_op jit(solution)/shard_map/ppermute | solution.py:89
  816.6 94.0 %collective-permute-start.65 = (bf16[1,4,256,1024]{3,2,1,0:T(8,128)(2,1)}, bf16[1,4,256,1024]{3,2,1,0:T(8,128)(2,1)S(1)}, u32[]{:S(2)}, u32[]{:S(2)}) collective-permute-start(bf16[1,4,256,1024]{3,2,1,0:T(8,128)(2,1)} %bitcast.518), channel_id=1, source_target_pairs={{0,4},{4,0},{8,12},{12,8},{16,20},{20,16},{24,28},{28,24},{1,5},{5... | collective-permute-start | bytes 6291464 | tf_op jit(solution)/shard_map/ppermute | solution.py:89
  828.6 326.2 %collective-permute-start.31 = (bf16[8,160,2048]{2,1,0:T(8,128)(2,1)}, bf16[8,160,2048]{2,1,0:T(8,128)(2,1)}, u32[]{:S(2)}, u32[]{:S(2)}) collective-permute-start(bf16[8,160,2048]{2,1,0:T(8,128)(2,1)} %bitcast.456), channel_id=1, source_target_pairs={{0,1},{1,0},{2,3},{3,2},{4,5},{5,4},{6,7},{7,6},{8,9},{9,8},{10,11... | collective-permute-start | bytes 15728648 | tf_op jit(solution)/shard_map/ppermute | solution.py:89
  857.9 55.4 %collective-permute-start.70 = (bf16[1024,256]{0,1:T(8,128)(2,1)}, bf16[1024,256]{0,1:T(8,128)(2,1)S(1)}, u32[]{:S(2)}, u32[]{:S(2)}) collective-permute-start(bf16[1024,256]{0,1:T(8,128)(2,1)} %get-tuple-element.103), channel_id=1, source_target_pairs={{0,8},{4,12},{8,0},{12,4},{16,24},{20,28},{24,16},{28,20},{1,9},{5... | collective-permute-start | bytes 1572872 | tf_op jit(solution)/shard_map/ppermute | solution.py:89
  867.1 304.2 %collective-permute-start.42 = (bf16[4,160,2048]{2,1,0:T(8,128)(2,1)}, bf16[4,160,2048]{2,1,0:T(8,128)(2,1)}, u32[]{:S(2)}, u32[]{:S(2)}) collective-permute-start(bf16[4,160,2048]{2,1,0:T(8,128)(2,1)} %slice.550), channel_id=1, source_target_pairs={{0,2},{1,3},{2,0},{3,1},{4,6},{5,7},{6,4},{7,5},{8,10},{9,11},{10,... | collective-permute-start | bytes 7864328 | tf_op jit(solution)/shard_map/ppermute | solution.py:89
  916.5 134.7 %collective-permute-start.66 = (bf16[256,1024]{1,0:T(8,128)(2,1)}, bf16[256,1024]{1,0:T(8,128)(2,1)}, u32[]{:S(2)}, u32[]{:S(2)}) collective-permute-start(bf16[256,1024]{1,0:T(8,128)(2,1)} %get-tuple-element.111), channel_id=1, source_target_pairs={{0,8},{4,12},{8,0},{12,4},{16,24},{20,28},{24,16},{28,20},{1,9},{5... | collective-permute-start | bytes 1572872 | tf_op jit(solution)/shard_map/ppermute | solution.py:89
  948.9 137.4 %collective-permute-start.67 = (bf16[256,1024]{1,0:T(8,128)(2,1)}, bf16[256,1024]{1,0:T(8,128)(2,1)}, u32[]{:S(2)}, u32[]{:S(2)}) collective-permute-start(bf16[256,1024]{1,0:T(8,128)(2,1)} %get-tuple-element.110), channel_id=1, source_target_pairs={{0,16},{4,20},{8,24},{12,28},{16,0},{20,4},{24,8},{28,12},{1,17},{... | collective-permute-start | bytes 1572872 | tf_op jit(solution)/shard_map/ppermute | solution.py:89
  948.9 142.9 %collective-permute-start.68 = (bf16[256,1024]{1,0:T(8,128)(2,1)}, bf16[256,1024]{1,0:T(8,128)(2,1)}, u32[]{:S(2)}, u32[]{:S(2)}) collective-permute-start(bf16[256,1024]{1,0:T(8,128)(2,1)} %get-tuple-element.109), channel_id=1, source_target_pairs={{0,24},{4,28},{8,16},{12,20},{16,8},{20,12},{24,0},{28,4},{1,25},{... | collective-permute-start | bytes 1572872 | tf_op jit(solution)/shard_map/ppermute | solution.py:89
  1051.2 185.4 %collective-permute-start.71 = (bf16[1024,256]{0,1:T(8,128)(2,1)}, bf16[1024,256]{0,1:T(8,128)(2,1)}, u32[]{:S(2)}, u32[]{:S(2)}) collective-permute-start(bf16[1024,256]{0,1:T(8,128)(2,1)} %get-tuple-element.102), channel_id=1, source_target_pairs={{0,16},{4,20},{8,24},{12,28},{16,0},{20,4},{24,8},{28,12},{1,17},{... | collective-permute-start | bytes 1572872 | tf_op jit(solution)/shard_map/ppermute | solution.py:89
  1086.3 151.6 %collective-permute-start.72 = (bf16[1024,256]{0,1:T(8,128)(2,1)}, bf16[1024,256]{0,1:T(8,128)(2,1)}, u32[]{:S(2)}, u32[]{:S(2)}) collective-permute-start(bf16[1024,256]{0,1:T(8,128)(2,1)} %get-tuple-element.101), channel_id=1, source_target_pairs={{0,24},{4,28},{8,16},{12,20},{16,8},{20,12},{24,0},{28,4},{1,25},{... | collective-permute-start | bytes 1572872 | tf_op jit(solution)/shard_map/ppermute | solution.py:89
  1169.8 58.2 %collective-permute-start.32 = (bf16[4,160,2048]{2,1,0:T(8,128)(2,1)}, bf16[4,160,2048]{2,1,0:T(8,128)(2,1)}, u32[]{:S(2)}, u32[]{:S(2)}) collective-permute-start(bf16[4,160,2048]{2,1,0:T(8,128)(2,1)} %slice.551), channel_id=1, source_target_pairs={{0,2},{1,3},{2,0},{3,1},{4,6},{5,7},{6,4},{7,5},{8,10},{9,11},{10,... | collective-permute-start | bytes 7864328 | tf_op jit(solution)/shard_map/ppermute | solution.py:89
  1299.6 57.8 %collective-permute-start.35 = (f32[1,160,2048]{2,1,0:T(8,128)}, f32[1,160,2048]{2,1,0:T(8,128)S(1)}, u32[]{:S(2)}, u32[]{:S(2)}) collective-permute-start(f32[1,160,2048]{2,1,0:T(8,128)} %get-tuple-element.62), channel_id=1, source_target_pairs={{0,2},{1,3},{2,0},{3,1},{4,6},{5,7},{6,4},{7,5},{8,10},{9,11},{10,... | collective-permute-start | bytes 3932168 | tf_op jit(solution)/shard_map/ppermute | solution.py:89
  (162 other events, 3086.1 us)

commit v2 on v1

--- a/solution.py
+++ b/solution.py
@@ -1,6 +1,10 @@
+import functools
+
 import jax
 import jax.numpy as jnp
 from jax import lax
+from jax.experimental import pallas as pl
+from jax.experimental.pallas import tpu as pltpu
 from jax.sharding import PartitionSpec as P
 
 HD = 256
@@ -134,7 +138,7 @@
     return out
 
 
-def shards(
+def general(
     tokens,
     cotangent,
     lengths,
@@ -334,6 +338,644 @@
     return (block_output, input_grad, *qa, *ka, *oa, *ga, *da, *na)
 
 
+MESH = pl.DeviceIdType.MESH
+ANY = pl.BlockSpec(memory_space=pl.ANY)
+VMEM = pl.BlockSpec(memory_space=pltpu.VMEM)
+LIMIT = 62 * 1024 * 1024
+
+
+def position():
+    me = lax.axis_index("dp")
+    t = lax.axis_index("tensor")
+    return me // 2, me % 2, t
+
+
+def at_z(z, r, t, k):
+    return ((z ^ k) * 2 + r, t)
+
+
+def greet(partners):
+    barrier = pltpu.get_barrier_semaphore()
+    for device in partners:
+        pl.semaphore_signal(barrier, inc=1, device_id=device, device_id_type=MESH)
+    pl.semaphore_wait(barrier, len(partners))
+
+
+class Copies:
+    def __init__(self, send, recv):
+        self.send, self.recv, self.made = send, recv, {}
+
+    def start(self, name, src, dst, device):
+        i = len(self.made)
+        copy = pltpu.make_async_remote_copy(
+            src_ref=src,
+            dst_ref=dst,
+            send_sem=self.send.at[i],
+            recv_sem=self.recv.at[i],
+            device_id=device,
+            device_id_type=MESH,
+        )
+        copy.start()
+        self.made[name] = copy
+
+    def arrived(self, name):
+        self.made[name].wait_recv()
+
+    def left(self, name):
+        self.made[name].wait_send()
+
+
+def remote_params(number, limit=LIMIT):
+    return pltpu.CompilerParams(
+        collective_id=number, has_side_effects=True, vmem_limit_bytes=limit
+    )
+
+
+def block_rows(z, t, quarter):
+    return pl.ds(pl.multiple_of((z * 4 + t) * quarter, quarter), quarter)
+
+
+class TokenGather:
+    count = 15
+
+    def __init__(self, copies, own, out, tag):
+        self.copies, self.own, self.out, self.tag = copies, own, out, tag
+        self.z, self.r, self.t = position()
+        self.quarter = own.shape[0]
+
+    def rows(self, k, j):
+        return self.out.at[block_rows(self.z ^ k, self.t ^ j, self.quarter)]
+
+    def source(self, k, j):
+        return self.own if k == 0 and j == 0 else self.rows(k, j)
+
+    def send(self, name, k, j, device):
+        self.copies.start(self.tag + name, self.source(k, j), self.rows(k, j), device)
+
+    def send_z(self):
+        self.send("z2", 0, 0, at_z(self.z, self.r, self.t, 2))
+        self.send("z1", 0, 0, at_z(self.z, self.r, self.t, 1))
+
+    def send_x(self, k):
+        me = self.z * 2 + self.r
+        self.send(f"x{k}", k, 0, (me, self.t ^ 2))
+        self.send(f"c{k}0", k, 0, (me, self.t ^ 1))
+
+    def take_z(self, k):
+        self.copies.arrived(f"{self.tag}z{k}")
+        if k == 2:
+            self.send("z3", 2, 0, at_z(self.z, self.r, self.t, 1))
+        self.send_x(k)
+
+    def take_x(self, k):
+        self.copies.arrived(f"{self.tag}x{k}")
+        self.send(f"c{k}1", k, 2, (self.z * 2 + self.r, self.t ^ 1))
+
+    def finish(self):
+        for k in range(4):
+            for j in range(2):
+                self.copies.arrived(f"{self.tag}c{k}{j}")
+        for name, copy in self.copies.made.items():
+            if name.startswith(self.tag):
+                copy.wait_send()
+
+
+def partners_of(z, r, t, zs=(1, 2, 3), y=True, tensor=True):
+    out = [at_z(z, r, t, k) for k in zs]
+    if y:
+        out.append((z * 2 + (r ^ 1), t))
+    if tensor:
+        out += [(z * 2 + r, t ^ 2), (z * 2 + r, t ^ 1)]
+    return out
+
+
+def gather_kernel(own, out, send, recv, local):
+    z, r, t = position()
+    keep = pltpu.make_async_copy(own, out.at[block_rows(z, t, own.shape[0])], local)
+    keep.start()
+    greet(partners_of(z, r, t, zs=(1, 2), y=False))
+    g = TokenGather(Copies(send, recv), own, out, "n")
+    g.send_z()
+    g.send_x(0)
+    g.take_z(1)
+    g.take_z(2)
+    g.take_x(0)
+    g.take_z(3)
+    for k in (1, 2, 3):
+        g.take_x(k)
+    g.finish()
+    keep.wait()
+
+
+def gather_tokens(own):
+    quarter, model = own.shape
+    n = TokenGather.count
+    return pl.pallas_call(
+        gather_kernel,
+        out_shape=jax.ShapeDtypeStruct((16 * quarter, model), own.dtype),
+        in_specs=[ANY],
+        out_specs=ANY,
+        scratch_shapes=[
+            pltpu.SemaphoreType.DMA((n,)),
+            pltpu.SemaphoreType.DMA((n,)),
+            pltpu.SemaphoreType.DMA,
+        ],
+        compiler_params=remote_params(1),
+        name="gather_tokens",
+    )(own)
+
+
+def weights_kernel(pack, three, dy, pack_out, three_out, dy_out, send, recv, local):
+    z, r, t = position()
+    rows = pack.shape[0]
+    ff = three_out.shape[2]
+    quarter = dy.shape[0]
+    me = z * 2 + r
+    other = (z * 2 + (r ^ 1), t)
+
+    def rows_of(k):
+        return pl.ds(pl.multiple_of(((z ^ k) * 2 + r) * rows, rows), rows)
+
+    def cols_of(k):
+        return pl.ds(pl.multiple_of((z ^ k) * ff, ff), ff)
+
+    keeps = [
+        pltpu.make_async_copy(pack, pack_out.at[rows_of(0)], local.at[0]),
+        pltpu.make_async_copy(dy, dy_out.at[block_rows(z, t, quarter)], local.at[1]),
+        pltpu.make_async_copy(three.at[:, :, cols_of(0)], three_out.at[:, rows_of(0)], local.at[2]),
+    ]
+    for keep in keeps:
+        keep.start()
+    greet(partners_of(z, r, t))
+    copies = Copies(send, recv)
+    g = TokenGather(copies, dy, dy_out, "d")
+
+    def pack_send(name, k, device):
+        src = pack if k == 0 else pack_out.at[rows_of(k)]
+        copies.start(name, src, pack_out.at[rows_of(k)], device)
+
+    pack_send("pz2", 0, at_z(z, r, t, 2))
+    pack_send("pz1", 0, at_z(z, r, t, 1))
+    pack_send("py0", 0, other)
+    copies.arrived("pz1")
+    pack_send("py1", 1, other)
+    copies.arrived("pz2")
+    pack_send("pz3", 2, at_z(z, r, t, 1))
+    pack_send("py2", 2, other)
+    g.send_x(0)
+    copies.arrived("pz3")
+    pack_send("py3", 3, other)
+
+    for k in (2, 3, 1):
+        for m in range(3):
+            copies.start(
+                f"wz{k}{m}",
+                three.at[m, :, cols_of(k)],
+                three_out.at[m, rows_of(0)],
+                at_z(z, r, t, k),
+            )
+    g.send_z()
+
+    def forward(k, m):
+        src = three.at[m, :, cols_of(0)] if k == 0 else three_out.at[m, rows_of(k)]
+        copies.start(f"wy{k}{m}", src, three_out.at[m, rows_of(k)], other)
+
+    for m in range(3):
+        forward(0, m)
+    for m in range(3):
+        copies.arrived(f"wz1{m}")
+        forward(1, m)
+    g.take_z(1)
+    g.take_x(0)
+    for m in range(3):
+        copies.arrived(f"wz2{m}")
+        forward(2, m)
+    g.take_z(2)
+    g.take_x(1)
+    g.take_z(3)
+    for m in range(3):
+        copies.arrived(f"wz3{m}")
+        forward(3, m)
+    g.take_x(2)
+    g.take_x(3)
+    g.finish()
+    for k in range(4):
+        copies.arrived(f"py{k}")
+        for m in range(3):
+            copies.arrived(f"wy{k}{m}")
+    for name, copy in copies.made.items():
+        if not name.startswith("d"):
+            copy.wait_send()
+    for keep in keeps:
+        keep.wait()
+
+
+def gather_weights(pack, three, dy):
+    rows, width = pack.shape
+    n = 7 + 21 + TokenGather.count
+    return pl.pallas_call(
+        weights_kernel,
+        out_shape=(
+            jax.ShapeDtypeStruct((8 * rows, width), bf),
+            jax.ShapeDtypeStruct((3, 8 * rows, three.shape[2] // ZN), bf),
+            jax.ShapeDtypeStruct((16 * dy.shape[0], dy.shape[1]), bf),
+        ),
+        in_specs=[ANY] * 3,
+        out_specs=(ANY,) * 3,
+        scratch_shapes=[
+            pltpu.SemaphoreType.DMA((n,)),
+            pltpu.SemaphoreType.DMA((n,)),
+            pltpu.SemaphoreType.DMA((3,)),
+        ],
+        compiler_params=remote_params(2),
+        name="gather_weights",
+    )(pack, three, dy)
+
+
+ROOT = 0.7978845608028654
+CUBE = 0.044715
+
+
+def ff_kernel(
+    nt_hbm, dy_hbm, w_hbm, hgu_hbm, sums,
+    w, xin, hgu, sendc, recvc, sendx, kept, recvx, recvz,
+    send, recv, load, wload, store,
+):
+    z, r, t = position()
+    x, c = t // 2, t % 2
+    me = z * 2 + r
+    quarter = sums.shape[1]
+    model, ff = w.shape[1], w.shape[2]
+    tile = 256
+
+    loads = [pltpu.make_async_copy(w_hbm.at[m], w.at[m], wload.at[m]) for m in range(3)]
+    for copy in loads:
+        copy.start()
+
+    order = (1, 3, 2, 0)
+
+    def rows(i, b):
+        cc = c if i % 2 else c ^ 1
+        xx = x if b else x ^ 1
+        return block_rows(z ^ order[i // 2], xx * 2 + cc, quarter)
+
+    def fetch(i):
+        out = []
+        for a, src in enumerate((nt_hbm, dy_hbm)):
+            for b in range(2):
+                copy = pltpu.make_async_copy(
+                    src.at[rows(i, b)],
+                    xin.at[i % 2, a, pl.ds(b * quarter, quarter)],
+                    load.at[i % 2, a, b],
+                )
+                copy.start()
+                out.append(copy)
+        return out
+
+    pending = fetch(0)
+    greet(partners_of(z, r, t, zs=(1, 2), y=False))
+    copies = Copies(send, recv)
+    for copy in loads:
+        copy.wait()
+
+    def take_x(s):
+        copies.arrived(f"x{s}")
+        if s == 2:
+            copies.arrived("z1")
+        if s == 3:
+            copies.arrived("z0")
+            copies.arrived("z2")
+
+        @pl.loop(0, model // tile)
+        def _(n):
+            cols = pl.ds(pl.multiple_of(n * tile, tile), tile)
+            for a in range(2):
+                total = kept[s, a, :, cols].astype(fl) + recvx[s, a, :, cols].astype(fl)
+                if s == 2:
+                    total += recvz[1, a, :, cols].astype(fl)
+                if s == 3:
+                    total += recvz[0, a, :, cols].astype(fl) + recvz[2, a, :, cols].astype(fl)
+                    sums[a, :, cols] = total
+                else:
+                    recvx[s, a, :, cols] = total.astype(bf)
+
+        if s < 3:
+            copies.start(f"z{s}", recvx.at[s], recvz.at[s], at_z(z, r, t, 2 if s == 2 else 1))
+
+    stores = {}
+    for i in range(8):
+        s, own = i // 2, i % 2
+        for copy in pending:
+            copy.wait()
+        if i < 7:
+            pending = fetch(i + 1)
+        if i >= 2:
+            for copy in stores[i - 2]:
+                copy.wait()
+
+        @pl.loop(0, ff // tile)
+        def _(n):
+            cols = pl.ds(pl.multiple_of(n * tile, tile), tile)
+            gate = jnp.dot(xin[i % 2, 0], w[0, :, cols], preferred_element_type=fl)
+            upper = jnp.dot(xin[i % 2, 0], w[1, :, cols], preferred_element_type=fl)
+            dh = jnp.dot(xin[i % 2, 1], w[2, :, cols], preferred_element_type=fl)
+            square = gate * gate
+            bend = jnp.tanh(ROOT * gate * (1.0 + CUBE * square))
+            half = 0.5 * (1.0 + bend)
+            gelu = gate * half
+            slope = half + 0.5 * gate * (1.0 - bend * bend) * (ROOT * (1.0 + 3.0 * CUBE * square))
+            hgu[i % 2, 0, :, cols] = (gelu * upper).astype(bf)
+            hgu[i % 2, 1, :, cols] = (dh * upper * slope).astype(bf)
+            hgu[i % 2, 2, :, cols] = (dh * gelu).astype(bf)
+
+        stores[i] = []
+        for m in range(3):
+            for b in range(2):
+                copy = pltpu.make_async_copy(
+                    hgu.at[i % 2, m, pl.ds(b * quarter, quarter)],
+                    hgu_hbm.at[m, rows(i, b)],
+                    store.at[i % 2, m, b],
+                )
+                copy.start()
+                stores[i].append(copy)
+
+        if own:
+            copies.arrived(f"c{s}")
+            if s >= 2:
+                copies.left(f"x{s - 2}")
+        elif s >= 1:
+            copies.left(f"c{s - 1}")
+
+        @pl.loop(0, model // tile)
+        def _(n):
+            cols = pl.ds(pl.multiple_of(n * tile, tile), tile)
+            out = times_trans(hgu[i % 2, 0], w[2, cols])
+            back = times_trans(hgu[i % 2, 1], w[0, cols]) + times_trans(hgu[i % 2, 2], w[1, cols])
+            for a, part in enumerate((out, back)):
+                if own:
+                    total = part + recvc[s % 2, a, :, cols].astype(fl)
+                    sendx[s % 2, a, :, cols] = total[:quarter].astype(bf)
+                    kept[s, a, :, cols] = total[quarter:].astype(bf)
+                else:
+                    sendc[a, :, cols] = part.astype(bf)
+
+        if own:
+            copies.start(f"x{s}", sendx.at[s % 2], recvx.at[s], (me, t ^ 2))
+            if s >= 2:
+                take_x(s - 2)
+        else:
+            copies.start(f"c{s}", sendc, recvc.at[s % 2], (me, t ^ 1))
+
+    take_x(2)
+    take_x(3)
+    for i in (6, 7):
+        for copy in stores[i]:
+            copy.wait()
+    for name in ("c3", "x2", "x3", "z0", "z1", "z2"):
+        copies.left(name)
+
+
+def feed_forward(nt, dy, w):
+    group, model = nt.shape
+    ff = w.shape[2]
+    quarter = group // 16
+    return pl.pallas_call(
+        ff_kernel,
+        out_shape=(
+            jax.ShapeDtypeStruct((3, group, ff), bf),
+            jax.ShapeDtypeStruct((2, quarter, model), fl),
+        ),
+        in_specs=[ANY] * 3,
+        out_specs=(ANY, VMEM),
+        scratch_shapes=[
+            pltpu.VMEM((3, model, ff), bf),
+            pltpu.VMEM((2, 2, 2 * quarter, model), bf),
+            pltpu.VMEM((2, 3, 2 * quarter, ff), bf),
+            pltpu.VMEM((2, 2 * quarter, model), bf),
+            pltpu.VMEM((2, 2, 2 * quarter, model), bf),
+            pltpu.VMEM((2, 2, quarter, model), bf),
+            pltpu.VMEM((4, 2, quarter, model), bf),
+            pltpu.VMEM((4, 2, quarter, model), bf),
+            pltpu.VMEM((3, 2, quarter, model), bf),
+            pltpu.SemaphoreType.DMA((11,)),
+            pltpu.SemaphoreType.DMA((11,)),
+            pltpu.SemaphoreType.DMA((2, 2, 2)),
+            pltpu.SemaphoreType.DMA((3,)),
+            pltpu.SemaphoreType.DMA((2, 3, 2)),
+        ],
+        compiler_params=remote_params(3),
+        name="feed_forward",
+    )(nt, dy, w)
+
+
+def grads_kernel(
+    nt_hbm, dy_hbm, hgu_hbm, out,
+    hgu, lhs, sendy, recvy, sendz,
+    send, recv, load, hload, local,
+):
+    z, r, t = position()
+    rows = lhs.shape[3]
+    ff = hgu.shape[2]
+    other = (z * 2 + (r ^ 1), t)
+
+    loads = [pltpu.make_async_copy(hgu_hbm.at[m], hgu.at[m], hload.at[m]) for m in range(3)]
+    zorder = (2, 3, 1, 0)
+
+    def fetch(i):
+        k, rr = zorder[i % 4], (r if i >= 4 else r ^ 1)
+        cols = pl.ds(pl.multiple_of(((z ^ k) * 2 + rr) * rows, rows), rows)
+        out = []
+        for a, src in enumerate((nt_hbm, dy_hbm)):
+            copy = pltpu.make_async_copy(src.at[:, cols], lhs.at[i % 2, a], load.at[i % 2, a])
+            copy.start()
+            out.append(copy)
+        return out
+
+    pending = fetch(0)
+    for m in (1, 2, 0):
+        loads[m].start()
+    greet(partners_of(z, r, t, tensor=False))
+    copies = Copies(send, recv)
+    for i in range(8):
+        k = zorder[i % 4]
+        for copy in pending:
+            copy.wait()
+        if i < 7:
+            pending = fetch(i + 1)
+        for m, (h, a) in enumerate(((1, 0), (2, 0), (0, 1))):
+            if i == 0:
+                loads[h].wait()
+            if i >= 4:
+                copies.arrived(f"y{k}{m}")
+
+            @pl.loop(0, ff // 512)
+            def _(n):
+                cols = pl.ds(pl.multiple_of(n * 512, 512), 512)
+                grad = inner_rows(lhs[i % 2, a], hgu[h, :, cols])
+                if i < 4:
+                    sendy[i, m, :, cols] = grad.astype(bf)
+                else:
+                    sendz[i - 4, m, :, cols] = (grad + recvy[i - 4, m, :, cols].astype(fl)).astype(bf)
+
+            if i < 4:
+                copies.start(f"y{k}{m}", sendy.at[i, m], recvy.at[i, m], other)
+            else:
+                place = out.at[m, :, pl.ds(pl.multiple_of(z * ff, ff), ff)]
+                if k:
+                    copies.start(f"z{k}{m}", sendz.at[i - 4, m], place, at_z(z, r, t, k))
+                else:
+                    pltpu.make_async_copy(sendz.at[i - 4, m], place, local.at[m]).start()
+    for m in range(3):
+        place = out.at[m, :, pl.ds(pl.multiple_of(z * ff, ff), ff)]
+        pltpu.make_async_copy(sendz.at[3, m], place, local.at[m]).wait()
+        for k in range(1, 4):
+            copies.arrived(f"z{k}{m}")
+    for copy in copies.made.values():
+        copy.wait_send()
+
+
+def weight_grads(nt, dy, hgu):
+    group, model = nt.shape
+    ff = hgu.shape[2]
+    rows = model // 8
+    return pl.pallas_call(
+        grads_kernel,
+        out_shape=jax.ShapeDtypeStruct((3, rows, ZN * ff), bf),
+        in_specs=[ANY] * 3,
+        out_specs=ANY,
+        scratch_shapes=[
+            pltpu.VMEM((3, group, ff), bf),
+            pltpu.VMEM((2, 2, group, rows), bf),
+            pltpu.VMEM((4, 3, rows, ff), bf),
+            pltpu.VMEM((4, 3, rows, ff), bf),
+            pltpu.VMEM((4, 3, rows, ff), bf),
+            pltpu.SemaphoreType.DMA((21,)),
+            pltpu.SemaphoreType.DMA((21,)),
+            pltpu.SemaphoreType.DMA((2, 2)),
+            pltpu.SemaphoreType.DMA((3,)),
+            pltpu.SemaphoreType.DMA((3,)),
+        ],
+        compiler_params=remote_params(4),
+        name="weight_grads",
+    )(nt, dy, hgu)
+
+
+def fast(
+    tokens,
+    cotangent,
+    lengths,
+    w_query,
+    w_keyval,
+    w_output,
+    w_gateup,
+    w_down,
+    norm_gains,
+    first_query,
+    first_keyval,
+    first_output,
+    first_gateup,
+    first_down,
+    first_gains,
+    second_query,
+    second_keyval,
+    second_output,
+    second_gateup,
+    second_down,
+    second_gains,
+):
+    dp = lax.axis_size("dp")
+    tn = lax.axis_size("tensor")
+    me = lax.axis_index("dp")
+    t = lax.axis_index("tensor")
+    dp_steps = [("dp", 4), ("dp", 2), ("dp", 1)]
+    t_steps = [("tensor", 2), ("tensor", 1)]
+
+    slot, model = tokens.shape
+    rows = model // dp
+    quarter = slot // tn
+    width = w_query.shape[1]
+    kvt = w_keyval.shape[1] // tn
+    length = lengths[0]
+
+    gain_full = place(
+        gather(norm_gains.astype(bf), dp_steps), me, dp_steps, "dp", axis=1
+    ).reshape(2, model).astype(fl)
+    own_keyval = lax.dynamic_slice_in_dim(w_keyval, t * kvt, kvt, 1)
+    pack = jnp.concatenate([w_query, own_keyval, w_output.T], axis=1).astype(bf)
+    three = jnp.concatenate([w_gateup.astype(bf), w_down.astype(bf).T[None]], axis=0)
+    cot_own = lax.dynamic_slice_in_dim(cotangent, t * quarter, quarter, 0)
+    valid = (t * quarter + jnp.arange(quarter) < length)[:, None]
+    grad_own = jnp.where(valid, cot_own, jnp.zeros_like(cot_own))
+    pack, three, dy = gather_weights(pack, three, grad_own)
+    qkv_w = pack[:, : width + kvt]
+    output_t = pack[:, width + kvt :]
+
+    x = tokens.astype(fl)
+    normed_one = rms_scale(x, gain_full[0]).astype(bf)
+    projected = dot(normed_one, qkv_w).astype(bf)
+    query = projected[:, :width]
+    keyval = place(
+        gather(projected[:, width:], t_steps), t, t_steps, "tensor", axis=1
+    ).reshape(slot, tn * kvt)
+    mixed, logsum = slot_forward(query, keyval, length)
+    mixed = mixed.astype(bf)
+    attn_part = times_trans(mixed, output_t).astype(bf).reshape(tn, quarter, model)
+    attn = reduce(pick(attn_part, t, t_steps, "tensor"), t_steps)
+    x_own = lax.dynamic_slice_in_dim(x, t * quarter, quarter, 0)
+    resid = x_own + attn
+    normed_two = gather_tokens(rms_scale(resid, gain_full[1]).astype(bf))
+
+    hgu, sums = feed_forward(normed_two, dy, three)
+    out_own = resid + sums[0]
+    block_output = place(gather(out_own, t_steps), t, t_steps, "tensor").reshape(slot, model)
+    ff_grads = weight_grads(normed_two, dy, hgu)
+    gateup_shard = ff_grads[:2].astype(fl)
+    down_shard = ff_grads[2].T.astype(fl)
+
+    _, pull_second = jax.vjp(rms_scale, resid, gain_full[1])
+    grad_resid_norm, grad_gain_two = pull_second(sums[1].astype(bf).astype(fl))
+    grad_resid = grad_own.astype(fl) + grad_resid_norm
+    grad_attn = place(gather(grad_resid.astype(bf), t_steps), t, t_steps, "tensor").reshape(slot, model)
+
+    grad_mixed = dot(grad_attn, output_t).astype(bf)
+    grad_query, grad_keyval = slot_backward(query, keyval, length, logsum, grad_mixed)
+    keyval_parts = grad_keyval.astype(bf).reshape(slot, tn, kvt)
+    keyval_low = reduce(pick(keyval_parts, t, t_steps, "tensor", axis=1), t_steps).astype(bf)
+    grad_projected = jnp.concatenate([grad_query.astype(bf), keyval_low], axis=1)
+    one_parts = times_trans(grad_projected, qkv_w).astype(bf).reshape(tn, quarter, model)
+    grad_normed_one = reduce(pick(one_parts, t, t_steps, "tensor"), t_steps)
+    pack_grad = jnp.concatenate(
+        [inner_rows(normed_one, grad_projected).astype(bf), inner_rows(grad_attn, mixed).astype(bf)], axis=1
+    )
+    _, pull_first = jax.vjp(rms_scale, x_own, gain_full[0])
+    grad_x_norm, grad_gain_one = pull_first(grad_normed_one)
+    input_own = grad_resid + grad_x_norm
+    input_grad = place(gather(input_own, t_steps), t, t_steps, "tensor").reshape(slot, model)
+
+    pack_shard = reduce(pick(pack_grad.reshape(dp, rows, -1), me, dp_steps, "dp"), dp_steps)
+    query_shard = pack_shard[:, :width]
+    keyval_shard = place(
+        gather(pack_shard[:, width : width + kvt].astype(bf), t_steps), t, t_steps, "tensor", axis=1
+    ).reshape(rows, tn * kvt).astype(fl)
+    output_shard = pack_shard[:, width + kvt :].T
+    gains_grad = jnp.stack([grad_gain_one, grad_gain_two]).reshape(2, dp, rows)
+    gains_parts = pick(gains_grad, me, dp_steps, "dp", axis=1)
+    for step in reversed(dp_steps):
+        half = gains_parts.shape[0] // 2
+        gains_parts = gains_parts[:half] + swap(gains_parts[half:], step)
+    gains_shard = gains_parts[0]
+    for step in t_steps:
+        gains_shard = gains_shard + swap(gains_shard, step)
+
+    qa = adamw(w_query, query_shard, first_query, second_query, decay_rate)
+    ka = adamw(w_keyval, keyval_shard, first_keyval, second_keyval, decay_rate)
+    oa = adamw(w_output, output_shard, first_output, second_output, decay_rate)
+    ga = adamw(w_gateup, gateup_shard, first_gateup, second_gateup, decay_rate)
+    da = adamw(w_down, down_shard, first_down, second_down, decay_rate)
+    na = adamw(norm_gains, gains_shard, first_gains, second_gains, 0.0)
+    return (block_output, input_grad, *qa, *ka, *oa, *ga, *da, *na)
+
+
 def solution(mesh):
     query = P("dp", "tensor")
     keyval = P("dp", None)
@@ -342,7 +984,7 @@
     gains = P(None, "dp")
     weights = (query, keyval, output, gateup, output, gains)
     return jax.shard_map(
-        shards,
+        fast if mesh.shape["dp"] == 2 * ZN and mesh.shape["tensor"] == 4 else general,
         mesh=mesh,
         in_specs=(P("dp", None), P("dp", None), P("dp")) + weights * 3,
         out_specs=(P("dp", None), P("dp", None)) + tuple(w for w in weights for _ in range(4)),

time: 1470 us -> 1060 us (0.72)
  Pallas kernels: 0 us -> 676 us
  local copies, waits for them, and re-layouts: 552 us -> 122 us
  waiting for transfers between devices: 455 us -> 78.8 us
  matrix products: 210 us -> 42.9 us
  starting transfers between devices: 114 us -> 39 us
  other arithmetic: 116 us -> 91.9 us
    pallas_call x0 -> x4, Pallas kernels: none -> 676 us  [the longest x1 245 us: gather_weights(): pl.pallas_call(weights_kernel, out_shape=(jax.ShapeDtypeStruct((8 * rows,...]
    ppermute x78 -> x27, waiting for transfers between devices: 455 us -> 78.8 us  [swap(): lax.ppermute(value, axis, [(i, i ^ bit) for i in range(lax.axis_size(axis...]
    dynamic_update_slice x20 -> x0, local copies, waits for them, and re-layouts: 153 us -> none  [the longest x12 142 us: scatter_z(): out = lax.dynamic_update_index_in_dim(out, parts[k], z ^ k, axis)]
    dynamic_slice x14 -> x3, local copies, waits for them, and re-layouts: 150 us -> 11.4 us  [take(): return lax.dynamic_index_in_dim(array, index, axis, keepdims=False)]
    ppermute x78 -> x27, starting transfers between devices: 114 us -> 39 us  [swap(): lax.ppermute(value, axis, [(i, i ^ bit) for i in range(lax.axis_size(axis...]
    dot_general x5 -> x2, matrix products: 77.8 us -> 7.73 us  [times_trans(): lax.dot_general(left, right, (((1,), (1,)), ((), ())), preferred_element_...]
    dot_general x8 -> x2, matrix products: 55.6 us -> 7.64 us  [inner_rows(): lax.dot_general(left, right, (((0,), (0,)), ((), ())), preferred_element_...]
    broadcast_in_dim x28 -> x0, local copies, waits for them, and re-layouts: 45.4 us -> none  [the longest x12 20.7 us: shards(): down_w = lax.dynamic_update_index_in_dim(down_w, block, z ^ k, 1)]
  transfers between devices with their start and end apart: 78 -> 27, of which waited for: 38 -> 10; matrix products, arithmetic and copies ran while one was open for 42% -> 21% of each run, Pallas kernels for 0% -> 39%
where the time goes in v2:
time: 1060 us; the launch traced here: 1050 us
  Pallas kernels  676 us (64%)
  local copies, waits for them, and re-layouts  122 us (12%)
  other arithmetic  91.9 us (9%)
  waiting for transfers between devices  78.8 us (7%)
  matrix products  42.9 us (4%)
  starting transfers between devices  39 us (4%)
    pallas_call x1, Pallas kernels, gather_weights(): pl.pallas_call(weights_kernel, out_shape=(jax.ShapeDtypeStruct((8 * rows,...  245 us
    pallas_call x1, Pallas kernels, feed_forward(): pl.pallas_call(ff_kernel, out_shape=(jax.ShapeDtypeStruct((3, group, ff),...  199 us
    pallas_call x1, Pallas kernels, weight_grads(): pl.pallas_call(grads_kernel, out_shape=jax.ShapeDtypeStruct((3, rows, ZN...  165 us
    ppermute x27, waiting for transfers between devices, swap(): lax.ppermute(value, axis, [(i, i ^ bit) for i in range(lax.axis_size(axis...  78.8 us
    unnamed x116, local copies, waits for them, and re-layouts  74.8 us
    pallas_call x1, Pallas kernels, gather_tokens(): pl.pallas_call(gather_kernel, out_shape=jax.ShapeDtypeStruct((16 * quarte...  66.8 us
    mul x6, other arithmetic, adamw(): -learn_rate  39.2 us
    ppermute x27, starting transfers between devices, swap(): lax.ppermute(value, axis, [(i, i ^ bit) for i in range(lax.axis_size(axis...  39 us
  transfers between devices with their start and end apart: 27, of which 10 were waited for; matrix products, arithmetic and copies ran while one was open for 21% of the time, Pallas kernels for 39%

profile of v2, /device:TPU:0, one launch (start us, length us, event | category | flops | bytes accessed | tf_op | source)
XLA Modules:
  0.0 1053.9 jit_solution(908430294495163755)
XLA Ops:
  7.7 5.6 copy.93
  17.0 6.2 convert_element_type.159
  25.4 6.1 pad_maximum_fusion.three
  34.5 245.2 %gather_weights.1 = (bf16[2048,1152]{1,0:T(8,128)(2,1)}, bf16[3,2048,1024]{2,1,0:T(8,128)(2,1)}, bf16[2560,2048]{1,0:T(8,128)(2,1)}) custom-call(bf16[256,1152]{1,0:T(8,128)(2,1)} %pad_maximum_fusion.9.pack, bf16[3,256,4096]{2,1,0:T(8,128)(2,1)} %pad_maximum_fusion.three, bf16[160,2048]{1,0:T(8,128)(2,1)} %dynamic-slice_select_fusion.dy), custom_call_target="tpu_custom_call" | custom-call | tf_op jit(solution)/shard_map/gather_weights/pallas_call | solution.py:576
  279.7 16.8 %collective-permute-start.1 = (bf16[2,2,256]{2,1,0:T(2,128)(2,1)S(1)}, bf16[2,2,256]{2,1,0:T(2,128)(2,1)S(1)}, u32[]{:S(2)}, u32[]{:S(2)}) collective-permute-start(bf16[2,2,256]{2,1,0:T(2,128)(2,1)S(1)} %pad_maximum_fusion.17), channel_id=1, source_target_pairs={{0,8},{4,12},{8,0},{12,4},{16,24},{20,28},{24,16},{28,20},{1,9},{5... | collective-permute-start | bytes 6152 | tf_op jit(solution)/shard_map/ppermute | solution.py:93
  315.0 7.4 dynamic_update_slice.100
  344.2 5.6 copy.126
  349.8 5.6 copy.125
  358.5 66.8 %gather_tokens.1.nt_hbm = bf16[2560,2048]{1,0:T(8,128)(2,1)} custom-call(bf16[160,2048]{1,0:T(8,128)(2,1)} %multiply_convert_fusion.1.own), custom_call_target="tpu_custom_call" | custom-call | tf_op jit(solution)/shard_map/gather_tokens/pallas_call | solution.py:473
  425.4 199.0 %feed_forward.1 = (bf16[3,2560,1024]{2,1,0:T(8,128)(2,1)}, f32[2,160,2048]{2,1,0:T(8,128)}) custom-call(bf16[2560,2048]{1,0:T(8,128)(2,1)} %gather_tokens.1.nt_hbm, bf16[2560,2048]{1,0:T(8,128)(2,1)} %get-tuple-element.32.dy_hbm, bf16[3,2048,1024]{2,1,0:T(8,128)(2,1)} %get-tuple-element.33.w_hbm), custom_call_target="tpu_custom_call" | custom-call | tf_op jit(solution)/shard_map/feed_forward/pallas_call | solution.py:742
  636.0 165.4 %weight_grads.1 = bf16[3,256,4096]{2,1,0:T(8,128)(2,1)} custom-call(bf16[2560,2048]{1,0:T(8,128)(2,1)} %gather_tokens.1.nt_hbm, bf16[2560,2048]{1,0:T(8,128)(2,1)} %get-tuple-element.32.dy_hbm, bf16[3,2560,1024]{2,1,0:T(8,128)(2,1)} %get-tuple-element.35.hgu_hbm), custom_call_target="tpu_custom_call" | custom-call | tf_op jit(solution)/shard_map/weight_grads/pallas_call | solution.py:841
  801.5 22.6 %add_multiply_fusion = (f32[2,256,4096]{2,1,0:T(8,128)}, f32[2,256,4096]{2,1,0:T(8,128)}, f32[2,256,4096]{2,1,0:T(8,128)}, f32[2,256,4096]{2,1,0:T(8,128)}) fusion(f32[2,256,4096]{2,1,0:T(8,128)} %param.27, f32[2,256,4096]{2,1,0:T(8,128)} %param.39, f32[2,256,4096]{2,1,0:T(8,128)} %param.33, bf16[3,256,4096]{2,1,0:T(8,128)(2,1)} %weight_grads.1), kind=kLoop, calls=%fused_computation.3 | loop fusion | flops 27262976 | bytes 62914560 | tf_op jit(solution)/shard_map/mul | solution.py:87
  825.4 10.6 %add_multiply_fusion.1 = (f32[4096,256]{0,1:T(8,128)}, f32[4096,256]{0,1:T(8,128)}, f32[4096,256]{0,1:T(8,128)}) fusion(f32[4096,256]{0,1:T(8,128)} %copy.93, bf16[3,256,4096]{2,1,0:T(8,128)(2,1)} %weight_grads.1, f32[4096,256]{0,1:T(8,128)} %copy.126, f32[4096,256]{0,1:T(8,128)} %copy.125), kind=kLoop, calls=%fused_computation.13 | loop fusion | flops 13631488 | bytes 27262976 | tf_op jit(solution)/shard_map/mul | solution.py:87
  848.5 6.4 fusion.49
  855.3 5.1 convolution_convert_fusion.3
  861.6 7.2 fusion.30
  880.5 10.9 %constant_dynamic-slice_fusion.7 = (bf16[1,256,1152]{1,0,2:T(2,128)(2,1)}, bf16[1,256,1152]{1,0,2:T(2,128)(2,1)S(1)}, bf16[1,256,1152]{1,0,2:T(2,128)(2,1)S(1)},...) fusion(bf16[8,256,1152]{1,0,2:T(8,128)(2,1)S(1)} %bitcast.285, ...), kind=kLoop, calls=%fused_computation.186 | loop fusion | bytes 9437216 | tf_op jit(solution)/shard_map/jit(dynamic_index_in_dim)/dynamic_slice | solution.py:120
  902.3 5.6 copy.135
  907.9 5.6 copy.136
  913.5 5.6 copy.137
  919.1 5.9 copy.138
  935.8 11.6 %collective-permute-done.22 = f32[4,2,256]{2,1,0:T(2,128)S(1)} collective-permute-done((f32[4,2,256]{2,1,0:T(2,128)S(1)}, f32[4,2,256]{2,1,0:T(2,128)S(1)}, u32[]{:S(2)}, u32[]{:S(2)}) %collective-permute-start.22) | collective-permute-done | bytes 8224 | tf_op jit(solution)/shard_map/ppermute | solution.py:93
  963.0 24.0 %collective-permute-done.25 = f32[2,256]{1,0:T(2,128)S(1)} collective-permute-done((f32[2,256]{1,0:T(2,128)S(1)}, f32[2,256]{1,0:T(2,128)S(1)}, u32[]{:S(2)}, u32[]{:S(2)}) %collective-permute-start.25) | collective-permute-done | bytes 2080 | tf_op jit(solution)/shard_map/ppermute | solution.py:93
  990.3 26.5 %collective-permute-done.19 = bf16[1,256,1152]{1,2,0:T(8,128)(2,1)S(1)} collective-permute-done((bf16[1,256,1152]{1,2,0:T(8,128)(2,1)S(1)}, bf16[1,256,1152]{1,2,0:T(8,128)(2,1)S(1)}, u32[]{:S(2)}, u32[]{:S(2)}) %collective-permute-start.19) | collective-permute-done | bytes 589856 | tf_op jit(solution)/shard_map/ppermute | solution.py:93
  (276 shorter events, 173.9 us)
Async XLA Ops:
  1.4 278.3 %collective-permute-start = (bf16[1,2,256]{2,1,0:T(2,128)(2,1)S(1)}, bf16[1,2,256]{2,1,0:T(2,128)(2,1)S(1)}, u32[]{:S(2)}, u32[]{:S(2)}) collective-permute-start(bf16[1,2,256]{2,1,0:T(2,128)(2,1)S(1)} %convert_bitcast_fusion.4), channel_id=1, source_target_pairs={{0,16},{4,20},{8,24},{12,28},{16,0},{20,4},{24,8},{28,12},{1,17},{... | collective-permute-start | bytes 3080 | tf_op jit(solution)/shard_map/ppermute | solution.py:93
  279.7 18.3 %collective-permute-start.1 = (bf16[2,2,256]{2,1,0:T(2,128)(2,1)S(1)}, bf16[2,2,256]{2,1,0:T(2,128)(2,1)S(1)}, u32[]{:S(2)}, u32[]{:S(2)}) collective-permute-start(bf16[2,2,256]{2,1,0:T(2,128)(2,1)S(1)} %pad_maximum_fusion.17), channel_id=1, source_target_pairs={{0,8},{4,12},{8,0},{12,4},{16,24},{20,28},{24,16},{28,20},{1,9},{5... | collective-permute-start | bytes 6152 | tf_op jit(solution)/shard_map/ppermute | solution.py:93
  298.1 3.7 collective-permute-start.2
  306.7 5.4 collective-permute-start.3
  328.8 3.1 collective-permute-start.5
  334.0 21.4 %collective-permute-start.6 = (bf16[1,160,2048]{2,1,0:T(8,128)(2,1)S(1)}, bf16[1,160,2048]{2,1,0:T(8,128)(2,1)S(1)}, u32[]{:S(2)}, u32[]{:S(2)}) collective-permute-start(bf16[1,160,2048]{2,1,0:T(8,128)(2,1)S(1)} %slice.366), channel_id=1, source_target_pairs={{0,2},{1,3},{2,0},{3,1},{4,6},{5,7},{6,4},{7,5},{8,10},{9,11},{10,... | collective-permute-start | bytes 1966088 | tf_op jit(solution)/shard_map/ppermute | solution.py:93
  629.2 206.9 %collective-permute-start.7 = (f32[1,160,2048]{2,1,0:T(8,128)}, f32[1,160,2048]{2,1,0:T(8,128)}, u32[]{:S(2)}, u32[]{:S(2)}) collective-permute-start(f32[1,160,2048]{2,1,0:T(8,128)} %get-tuple-element.118), channel_id=1, source_target_pairs={{0,2},{1,3},{2,0},{3,1},{4,6},{5,7},{6,4},{7,5},{8,10},{9,11},{10,... | collective-permute-start | bytes 3932168 | tf_op jit(solution)/shard_map/ppermute | solution.py:93
  634.9 189.1 %collective-permute-start.9 = (bf16[1,160,2048]{2,1,0:T(8,128)(2,1)}, bf16[1,160,2048]{2,1,0:T(8,128)(2,1)S(1)}, u32[]{:S(2)}, u32[]{:S(2)}) collective-permute-start(bf16[1,160,2048]{2,1,0:T(8,128)(2,1)} %get-tuple-element.116), channel_id=1, source_target_pairs={{0,2},{1,3},{2,0},{3,1},{4,6},{5,7},{6,4},{7,5},{8,10},{9,11},{10,... | collective-permute-start | bytes 1966088 | tf_op jit(solution)/shard_map/ppermute | solution.py:93
  825.3 14.9 %collective-permute-start.10 = (bf16[2,160,2048]{2,1,0:T(8,128)(2,1)S(1)}, bf16[2,160,2048]{2,1,0:T(8,128)(2,1)S(1)}, u32[]{:S(2)}, u32[]{:S(2)}) collective-permute-start(bf16[2,160,2048]{2,1,0:T(8,128)(2,1)S(1)} %pad_maximum_fusion.6), channel_id=1, source_target_pairs={{0,1},{1,0},{2,3},{3,2},{4,5},{5,4},{6,7},{7,6},{8,9},{9,8},{10,11... | collective-permute-start | bytes 3932168 | tf_op jit(solution)/shard_map/ppermute | solution.py:93
  839.7 93.6 %collective-permute-start.8 = (f32[2,160,2048]{2,1,0:T(8,128)}, f32[2,160,2048]{2,1,0:T(8,128)}, u32[]{:S(2)}, u32[]{:S(2)}) collective-permute-start(f32[2,160,2048]{2,1,0:T(8,128)} %pad_maximum_fusion.2), channel_id=1, source_target_pairs={{0,1},{1,0},{2,3},{3,2},{4,5},{5,4},{6,7},{7,6},{8,9},{9,8},{10,11... | collective-permute-start | bytes 7864328 | tf_op jit(solution)/shard_map/ppermute | solution.py:93
  855.2 5.2 collective-permute-start.11
  860.5 8.3 collective-permute-start.12
  876.3 18.1 %collective-permute-start.13 = (bf16[2,160,2048]{2,1,0:T(8,128)(2,1)S(1)}, bf16[2,160,2048]{2,1,0:T(8,128)(2,1)S(1)}, u32[]{:S(2)}, u32[]{:S(2)}) collective-permute-start(bf16[2,160,2048]{2,1,0:T(8,128)(2,1)S(1)} %pad_maximum_fusion.7), channel_id=1, source_target_pairs={{0,1},{1,0},{2,3},{3,2},{4,5},{5,4},{6,7},{7,6},{8,9},{9,8},{10,11... | collective-permute-start | bytes 3932168 | tf_op jit(solution)/shard_map/ppermute | solution.py:93
  893.6 58.0 %collective-permute-start.17 = (bf16[4,256,1152]{1,2,0:T(8,128)(2,1)}, bf16[4,256,1152]{1,2,0:T(8,128)(2,1)}, u32[]{:S(2)}, u32[]{:S(2)}) collective-permute-start(bf16[4,256,1152]{1,2,0:T(8,128)(2,1)} %pad_maximum_fusion.4), channel_id=1, source_target_pairs={{0,4},{4,0},{8,12},{12,8},{16,20},{20,16},{24,28},{28,24},{1,5},{5... | collective-permute-start | bytes 7077896 | tf_op jit(solution)/shard_map/ppermute | solution.py:93
  897.4 33.5 %collective-permute-start.14 = (bf16[1,160,2048]{2,1,0:T(8,128)(2,1)}, bf16[1,160,2048]{2,1,0:T(8,128)(2,1)S(1)}, u32[]{:S(2)}, u32[]{:S(2)}) collective-permute-start(bf16[1,160,2048]{2,1,0:T(8,128)(2,1)} %slice.365), channel_id=1, source_target_pairs={{0,2},{1,3},{2,0},{3,1},{4,6},{5,7},{6,4},{7,5},{8,10},{9,11},{10,... | collective-permute-start | bytes 1966088 | tf_op jit(solution)/shard_map/ppermute | solution.py:93
  931.8 15.6 %collective-permute-start.22 = (f32[4,2,256]{2,1,0:T(2,128)S(1)}, f32[4,2,256]{2,1,0:T(2,128)S(1)}, u32[]{:S(2)}, u32[]{:S(2)}) collective-permute-start(f32[4,2,256]{2,1,0:T(2,128)S(1)} %pad_maximum_fusion.15), channel_id=1, source_target_pairs={{0,4},{4,0},{8,12},{12,8},{16,20},{20,16},{24,28},{28,24},{1,5},{5... | collective-permute-start | bytes 24584 | tf_op jit(solution)/shard_map/ppermute | solution.py:93
  947.4 3.7 collective-permute-start.23
  951.1 8.4 collective-permute-start.24
  954.0 33.1 %collective-permute-start.18 = (bf16[2,256,1152]{1,2,0:T(8,128)(2,1)S(1)}, bf16[2,256,1152]{1,2,0:T(8,128)(2,1)S(1)}, u32[]{:S(2)}, u32[]{:S(2)}) collective-permute-start(bf16[2,256,1152]{1,2,0:T(8,128)(2,1)S(1)} %slice.364), channel_id=1, source_target_pairs={{0,8},{4,12},{8,0},{12,4},{16,24},{20,28},{24,16},{28,20},{1,9},{5... | collective-permute-start | bytes 3538952 | tf_op jit(solution)/shard_map/ppermute | solution.py:93
  958.4 31.2 %collective-permute-start.15 = (f32[1,160,2048]{2,1,0:T(8,128)S(1)}, f32[1,160,2048]{2,1,0:T(8,128)S(1)}, u32[]{:S(2)}, u32[]{:S(2)}) collective-permute-start(f32[1,160,2048]{2,1,0:T(8,128)S(1)} %get-tuple-element.114), channel_id=1, source_target_pairs={{0,2},{1,3},{2,0},{3,1},{4,6},{5,7},{6,4},{7,5},{8,10},{9,11},{10,... | collective-permute-start | bytes 3932168 | tf_op jit(solution)/shard_map/ppermute | solution.py:93
  959.4 27.6 %collective-permute-start.25 = (f32[2,256]{1,0:T(2,128)S(1)}, f32[2,256]{1,0:T(2,128)S(1)}, u32[]{:S(2)}, u32[]{:S(2)}) collective-permute-start(f32[2,256]{1,0:T(2,128)S(1)} %fusion.83), channel_id=1, source_target_pairs={{0,2},{1,3},{2,0},{3,1},{4,6},{5,7},{6,4},{7,5},{8,10},{9,11},{10,... | collective-permute-start | bytes 6152 | tf_op jit(solution)/shard_map/ppermute | solution.py:93
  987.4 29.3 %collective-permute-start.19 = (bf16[1,256,1152]{1,2,0:T(8,128)(2,1)S(1)}, bf16[1,256,1152]{1,2,0:T(8,128)(2,1)S(1)}, u32[]{:S(2)}, u32[]{:S(2)}) collective-permute-start(bf16[1,256,1152]{1,2,0:T(8,128)(2,1)S(1)} %slice.367), channel_id=1, source_target_pairs={{0,16},{4,20},{8,24},{12,28},{16,0},{20,4},{24,8},{28,12},{1,17},{... | collective-permute-start | bytes 1769480 | tf_op jit(solution)/shard_map/ppermute | solution.py:93
  989.8 58.6 %collective-permute-start.16 = (f32[2,160,2048]{2,1,0:T(8,128)S(1)}, f32[2,160,2048]{2,1,0:T(8,128)}, u32[]{:S(2)}, u32[]{:S(2)}) collective-permute-start(f32[2,160,2048]{2,1,0:T(8,128)S(1)} %pad_maximum_fusion.3), channel_id=1, source_target_pairs={{0,1},{1,0},{2,3},{3,2},{4,5},{5,4},{6,7},{7,6},{8,9},{9,8},{10,11... | collective-permute-start | bytes 7864328 | tf_op jit(solution)/shard_map/ppermute | solution.py:93
  1016.9 12.2 %collective-permute-start.20 = (bf16[1,256,128]{1,2,0:T(8,128)(2,1)S(1)}, bf16[1,256,128]{1,2,0:T(8,128)(2,1)S(1)}, u32[]{:S(2)}, u32[]{:S(2)}) collective-permute-start(bf16[1,256,128]{1,2,0:T(8,128)(2,1)S(1)} %fusion.73), channel_id=1, source_target_pairs={{0,2},{1,3},{2,0},{3,1},{4,6},{5,7},{6,4},{7,5},{8,10},{9,11},{10,... | collective-permute-start | bytes 196616 | tf_op jit(solution)/shard_map/ppermute | solution.py:93
  (45 other events, 279.4 us)

commit v3 on v1

--- a/solution.py
+++ b/solution.py
@@ -1,6 +1,10 @@
+import functools
+
 import jax
 import jax.numpy as jnp
 from jax import lax
+from jax.experimental import pallas as pl
+from jax.experimental.pallas import tpu as pltpu
 from jax.sharding import PartitionSpec as P
 
 HD = 256
@@ -134,7 +138,7 @@
     return out
 
 
-def shards(
+def general(
     tokens,
     cotangent,
     lengths,
@@ -334,6 +338,1080 @@
     return (block_output, input_grad, *qa, *ka, *oa, *ga, *da, *na)
 
 
+MESH = pl.DeviceIdType.MESH
+ANY = pl.BlockSpec(memory_space=pl.ANY)
+VMEM = pl.BlockSpec(memory_space=pltpu.VMEM)
+LIMIT = 62 * 1024 * 1024
+WINDOW = 4
+
+
+def position():
+    me = lax.axis_index("dp")
+    t = lax.axis_index("tensor")
+    return me // 2, me % 2, t
+
+
+def at_z(z, r, t, k):
+    return ((z ^ k) * 2 + r, t)
+
+
+def greet(partners):
+    barrier = pltpu.get_barrier_semaphore()
+    for device in partners:
+        pl.semaphore_signal(barrier, inc=1, device_id=device, device_id_type=MESH)
+    pl.semaphore_wait(barrier, len(partners))
+
+
+class Copies:
+    def __init__(self, send, recv):
+        self.send, self.recv, self.made, self.gone = send, recv, {}, set()
+
+    def start(self, name, src, dst, device):
+        i = len(self.made)
+        self.made[name] = lambda: pltpu.make_async_remote_copy(
+            src_ref=src() if callable(src) else src,
+            dst_ref=dst() if callable(dst) else dst,
+            send_sem=self.send.at[i],
+            recv_sem=self.recv.at[i],
+            device_id=device,
+            device_id_type=MESH,
+        )
+        self.made[name]().start()
+
+    def arrived(self, name):
+        self.made[name]().wait_recv()
+
+    def left(self, name):
+        if name not in self.gone:
+            self.gone.add(name)
+            self.made[name]().wait_send()
+
+    def all_left(self, keep=lambda name: True):
+        for name in self.made:
+            if keep(name):
+                self.left(name)
+
+
+def remote_params(number, limit=LIMIT):
+    return pltpu.CompilerParams(
+        collective_id=number, has_side_effects=True, vmem_limit_bytes=limit
+    )
+
+
+def block_rows(z, t, quarter):
+    return pl.ds(pl.multiple_of((z * 4 + t) * quarter, quarter), quarter)
+
+
+class TokenGather:
+    count = 15
+
+    def __init__(self, copies, own, out, tag):
+        self.copies, self.own, self.out, self.tag = copies, own, out, tag
+        self.z, self.r, self.t = position()
+        self.quarter = own.shape[0]
+
+    def rows(self, k, j):
+        return self.out.at[block_rows(self.z ^ k, self.t ^ j, self.quarter)]
+
+    def source(self, k, j):
+        return self.own if k == 0 and j == 0 else self.rows(k, j)
+
+    def send(self, name, k, j, device):
+        self.copies.start(self.tag + name, self.source(k, j), self.rows(k, j), device)
+
+    def send_z(self):
+        self.send("z2", 0, 0, at_z(self.z, self.r, self.t, 2))
+        self.send("z1", 0, 0, at_z(self.z, self.r, self.t, 1))
+
+    def send_x(self, k):
+        me = self.z * 2 + self.r
+        self.send(f"x{k}", k, 0, (me, self.t ^ 2))
+        self.send(f"c{k}0", k, 0, (me, self.t ^ 1))
+
+    def take_z(self, k):
+        self.copies.arrived(f"{self.tag}z{k}")
+        if k == 2:
+            self.send("z3", 2, 0, at_z(self.z, self.r, self.t, 1))
+        self.send_x(k)
+
+    def take_x(self, k):
+        self.copies.arrived(f"{self.tag}x{k}")
+        self.send(f"c{k}1", k, 2, (self.z * 2 + self.r, self.t ^ 1))
+
+    def finish(self):
+        for k in range(4):
+            for j in range(2):
+                self.copies.arrived(f"{self.tag}c{k}{j}")
+        self.copies.all_left(lambda name: name.startswith(self.tag))
+
+
+def partners_of(z, r, t, zs=(1, 2, 3), y=True, tensor=True):
+    out = [at_z(z, r, t, k) for k in zs]
+    if y:
+        out.append((z * 2 + (r ^ 1), t))
+    if tensor:
+        out += [(z * 2 + r, t ^ 2), (z * 2 + r, t ^ 1)]
+    return out
+
+
+def rms_into(src, gain, dst, slab=16):
+    @pl.loop(0, dst.shape[0] // slab)
+    def _(i):
+        rows = pl.ds(pl.multiple_of(i * slab, slab), slab)
+        v = src[rows].astype(fl)
+        inverse = lax.rsqrt(jnp.mean(v * v, axis=-1, keepdims=True) + norm_eps)
+        dst[rows] = (v * inverse * gain).astype(bf)
+
+
+def cast_into(src, dst, slab=16):
+    @pl.loop(0, src.shape[0] // slab)
+    def _(i):
+        rows = pl.ds(pl.multiple_of(i * slab, slab), slab)
+        dst[rows] = src[rows].astype(bf)
+
+
+def probabilities(q, key, length, first):
+    scores = times_trans(q, key) * HD ** (-0.5)
+    row = first + lax.broadcasted_iota(jnp.int32, scores.shape, 0)
+    col = lax.broadcasted_iota(jnp.int32, scores.shape, 1)
+    scores = jnp.where((col <= row) & (col < length), scores, masked_score)
+    expo = jnp.exp(scores - jnp.max(scores, axis=-1, keepdims=True))
+    return expo / jnp.sum(expo, axis=-1, keepdims=True)
+
+
+def forward_kernel(
+    lengths, wq, wkv, wo, wgu, wd, gains, tokens, dy,
+    gu_out, d_out, dy_out, nt_out, resid_out, one_out, q_out, kv_out, mixed_out, qkv_out, o_out, gain_out,
+    wq_f, wkv_f, wo_f, gu_f, d_f, gu_b, d_b, x, qkv, o, gain, one, q, kv, mixed,
+    part, recvc, sendx, recvx, resid, nt_own,
+    send, recv, load, store,
+):
+    z, r, t = position()
+    me = z * 2 + r
+    rows = wq.shape[0]
+    slot, model = tokens.shape
+    quarter = dy.shape[0]
+    width = wq.shape[1]
+    kvt = qkv.shape[1] - width
+    ff = d_out.shape[0]
+    other = (z * 2 + (r ^ 1), t)
+    x_peer, core_peer, far_peer = (me, t ^ 2), (me, t ^ 1), (me, t ^ 3)
+
+    def d_block(k):
+        return pl.ds(pl.multiple_of(((z ^ k) * 2 + r) * rows, rows), rows)
+
+    def f_block(k):
+        return pl.ds(pl.multiple_of((z ^ k) * ff, ff), ff)
+
+    kv_cols = pl.ds(pl.multiple_of(t * kvt, kvt), kvt)
+    loads = [
+        pltpu.make_async_copy(wq, wq_f, load.at[0]),
+        pltpu.make_async_copy(wkv.at[:, kv_cols], wkv_f, load.at[1]),
+        pltpu.make_async_copy(wo, wo_f, load.at[2]),
+        pltpu.make_async_copy(gains, gain.at[:, d_block(0)], load.at[3]),
+        pltpu.make_async_copy(tokens, x, load.at[4]),
+        pltpu.make_async_copy(wgu, gu_f, load.at[5]),
+        pltpu.make_async_copy(wd, d_f, load.at[6]),
+    ]
+    for copy in loads:
+        copy.start()
+    stores = []
+
+    def keep(src, dst):
+        copy = pltpu.make_async_copy(src, dst, store.at[len(stores)])
+        copy.start()
+        stores.append(copy)
+
+    keep(dy, dy_out.at[block_rows(z, t, quarter)])
+    for copy in loads[:4]:
+        copy.wait()
+
+    @pl.loop(0, rows // 16)
+    def _(i):
+        own = pl.ds(pl.multiple_of(me * rows + i * 16, 16), 16)
+        at = pl.ds(pl.multiple_of(i * 16, 16), 16)
+        qkv[own, pl.ds(0, width)] = wq_f[at].astype(bf)
+        qkv[own, pl.ds(width, kvt)] = wkv_f[at].astype(bf)
+
+    @pl.loop(0, width // 16)
+    def _(i):
+        at = pl.ds(pl.multiple_of(i * 16, 16), 16)
+        o[at, d_block(0)] = wo_f[at].astype(bf)
+
+    greet(partners_of(z, r, t, zs=(1, 2, 3)) + [far_peer] + [((z ^ k) * 2 + (r ^ 1), t) for k in (1, 2, 3)])
+    copies = Copies(send, recv)
+    d = TokenGather(copies, dy, dy_out, "d")
+
+    for k in range(4):
+        for j in range(2):
+            if k or j:
+                copies.start(
+                    f"g{k}{j}", gain.at[:, d_block(0)], gain.at[:, d_block(0)], ((z ^ k) * 2 + (r ^ j), t)
+                )
+
+    def pack_send(name, k, device):
+        copies.start("q" + name, qkv.at[d_block(k)], qkv.at[d_block(k)], device)
+        copies.start("o" + name, o.at[:, d_block(k)], o.at[:, d_block(k)], device)
+
+    def pack_arrived(name):
+        copies.arrived("q" + name)
+        copies.arrived("o" + name)
+
+    pack_send("z2", 0, at_z(z, r, t, 2))
+    pack_send("z1", 0, at_z(z, r, t, 1))
+    pack_send("y0", 0, other)
+    d.send_z()
+    d.send_x(0)
+
+    for copy in loads[4:]:
+        copy.wait()
+    for m in range(2):
+        cast_into(gu_f.at[m], gu_b.at[m])
+    cast_into(d_f, d_b, 64)
+
+    pieces = 2
+
+    def owned(m, k, p):
+        if m == 2:
+            n = ff // pieces
+            return d_b.at[pl.ds(pl.multiple_of((z ^ k) * ff + p * n, n), n)]
+        n = rows // pieces
+        return gu_b.at[m, p * n : (p + 1) * n, f_block(k)]
+
+    def landed(m, k, p):
+        if m == 2:
+            n = ff // pieces
+            return d_out.at[p * n : (p + 1) * n, d_block(k)]
+        n = rows // pieces
+        return gu_out.at[m, pl.ds(pl.multiple_of(((z ^ k) * 2 + r) * rows + p * n, n), n)]
+
+    flows = [(m, k, p) for m in range(3) for k in (1, 3, 2) for p in range(pieces)]
+    counts = [0, 0]
+
+    def issue():
+        if counts[0] < len(flows):
+            m, k, p = flows[counts[0]]
+            copies.start(f"wz{k}{m}{p}", owned(m, k, p), landed(m, 0, p), at_z(z, r, t, k))
+            counts[0] += 1
+
+    def forward(m, k, p):
+        copies.start(f"wy{k}{m}{p}", owned(m, 0, p) if k == 0 else landed(m, k, p), landed(m, k, p), other)
+
+    def pump(n, more=True):
+        for _ in range(n):
+            if counts[1] < counts[0]:
+                m, k, p = flows[counts[1]]
+                copies.arrived(f"wz{k}{m}{p}")
+                forward(m, k, p)
+                counts[1] += 1
+            if more:
+                issue()
+
+    for _ in range(WINDOW):
+        issue()
+    for m in range(3):
+        for p in range(pieces):
+            keep(owned(m, 0, p), landed(m, 0, p))
+
+    for k in range(4):
+        for j in range(2):
+            if k or j:
+                copies.arrived(f"g{k}{j}")
+    keep(gain, gain_out)
+    rms_into(x, gain[0:1, :], one)
+    keep(one, one_out)
+
+    pack_arrived("z1")
+    pack_send("y1", 1, other)
+    pack_arrived("z2")
+    pack_send("z3", 2, at_z(z, r, t, 1))
+    pack_send("y2", 2, other)
+    d.take_z(1)
+    d.take_z(2)
+    pack_arrived("z3")
+    pack_send("y3", 3, other)
+    pump(2)
+    for k in range(4):
+        pack_arrived(f"y{k}")
+    for m in range(3):
+        for p in range(pieces):
+            forward(m, 0, p)
+    keep(qkv, qkv_out)
+    keep(o, o_out)
+
+    kv[:, kv_cols] = dot(one[...], qkv[:, width:]).astype(bf)
+    for name, peer in (("k1", core_peer), ("k2", x_peer), ("k3", far_peer)):
+        copies.start(name, kv.at[:, kv_cols], kv.at[:, kv_cols], peer)
+    q[...] = dot(one[...], qkv[:, :width]).astype(bf)
+    keep(q, q_out)
+    pump(1)
+    for name in ("k1", "k2", "k3"):
+        copies.arrived(name)
+    keep(kv, kv_out)
+    length = lengths[0]
+    step = 128
+    for h in range(width // HD):
+        for i in range(slot // step):
+            at, upto = pl.ds(i * step, step), pl.ds(0, (i + 1) * step)
+            probs = probabilities(q[at, h * HD : (h + 1) * HD], kv[upto, :HD], length, i * step)
+            mixed[at, h * HD : (h + 1) * HD] = dot(probs.astype(bf), kv[upto, HD:]).astype(bf)
+        pump(1)
+    keep(mixed, mixed_out)
+
+    def part_of(j, store_part):
+        at = pl.ds(pl.multiple_of((t ^ j) * quarter, quarter), quarter)
+        for n in range(0, model, 512):
+            store_part(dot(mixed[at], o[:, n : n + 512]), slice(n, n + 512))
+
+    def into_part(i):
+        def put(value, cols):
+            part[i, :, cols] = value.astype(bf)
+
+        return put
+
+    part_of(3, into_part(0))
+    part_of(1, into_part(1))
+    copies.start("a1", part, recvc, core_peer)
+    d.take_x(0)
+    d.take_z(3)
+    copies.arrived("a1")
+
+    def into_x(value, cols):
+        sendx[:, cols] = (value + recvc[0, :, cols].astype(fl)).astype(bf)
+
+    part_of(2, into_x)
+    copies.start("a2", sendx, recvx, x_peer)
+
+    def into_resid(value, cols):
+        resid[:, cols] = value + recvc[1, :, cols].astype(fl)
+
+    part_of(0, into_resid)
+    copies.arrived("a2")
+    first_row = t * quarter
+
+    @pl.loop(0, quarter // 16)
+    def _(i):
+        at = pl.ds(pl.multiple_of(i * 16, 16), 16)
+        mine = pl.ds(pl.multiple_of(first_row + i * 16, 16), 16)
+        v = x[mine].astype(fl) + (resid[at] + recvx[at].astype(fl))
+        resid[at] = v
+        inverse = lax.rsqrt(jnp.mean(v * v, axis=-1, keepdims=True) + norm_eps)
+        nt_own[at] = (v * inverse * gain[1:2, :]).astype(bf)
+
+    keep(resid, resid_out)
+    keep(nt_own, nt_out.at[block_rows(z, t, quarter)])
+    n = TokenGather(copies, nt_own, nt_out, "n")
+    n.send_z()
+    n.send_x(0)
+    d.take_x(1)
+    pump(WINDOW, more=False)
+    n.take_z(1)
+    n.take_z(2)
+    for _ in range(WINDOW):
+        issue()
+    d.take_x(2)
+    d.take_x(3)
+    n.take_x(0)
+    pump(2)
+    n.take_z(3)
+    n.take_x(1)
+    pump(2)
+    n.take_x(2)
+    pump(2)
+    n.take_x(3)
+    pump(len(flows))
+    n.finish()
+    d.finish()
+    for k in range(4):
+        for m in range(3):
+            for p in range(pieces):
+                copies.arrived(f"wy{k}{m}{p}")
+    copies.all_left(lambda name: name[0] not in "nd")
+    for copy in stores:
+        copy.wait()
+
+
+def forward_part(lengths, wq, wkv, wo, wgu, wd, gains, tokens, dy):
+    rows, width = wq.shape
+    slot, model = tokens.shape
+    quarter = dy.shape[0]
+    kvt = wkv.shape[1] // 4
+    ff = wd.shape[0] // ZN
+    n = 7 + 14 + 42 + 3 + 2 + 2 * TokenGather.count
+    shape = jax.ShapeDtypeStruct
+    return pl.pallas_call(
+        forward_kernel,
+        out_shape=(
+            shape((2, model, ff), bf),
+            shape((ff, model), bf),
+            shape((16 * quarter, model), bf),
+            shape((16 * quarter, model), bf),
+            shape((quarter, model), fl),
+            shape((slot, model), bf),
+            shape((slot, width), bf),
+            shape((slot, 4 * kvt), bf),
+            shape((slot, width), bf),
+            shape((model, width + kvt), bf),
+            shape((width, model), bf),
+            shape((8, model), fl),
+        ),
+        in_specs=[pl.BlockSpec(memory_space=pltpu.SMEM)] + [ANY] * 8,
+        out_specs=(ANY,) * 12,
+        scratch_shapes=[
+            pltpu.VMEM((rows, width), fl),
+            pltpu.VMEM((rows, kvt), fl),
+            pltpu.VMEM((width, rows), fl),
+            pltpu.VMEM(wgu.shape, fl),
+            pltpu.VMEM(wd.shape, fl),
+            pltpu.VMEM(wgu.shape, bf),
+            pltpu.VMEM(wd.shape, bf),
+            pltpu.VMEM((slot, model), bf),
+            pltpu.VMEM((model, width + kvt), bf),
+            pltpu.VMEM((width, model), bf),
+            pltpu.VMEM((8, model), fl),
+            pltpu.VMEM((slot, model), bf),
+            pltpu.VMEM((slot, width), bf),
+            pltpu.VMEM((slot, 4 * kvt), bf),
+            pltpu.VMEM((slot, width), bf),
+            pltpu.VMEM((2, quarter, model), bf),
+            pltpu.VMEM((2, quarter, model), bf),
+            pltpu.VMEM((quarter, model), bf),
+            pltpu.VMEM((quarter, model), bf),
+            pltpu.VMEM((quarter, model), fl),
+            pltpu.VMEM((quarter, model), bf),
+            pltpu.SemaphoreType.DMA((n,)),
+            pltpu.SemaphoreType.DMA((n,)),
+            pltpu.SemaphoreType.DMA((7,)),
+            pltpu.SemaphoreType.DMA((16,)),
+        ],
+        compiler_params=remote_params(1),
+        name="forward_part",
+    )(lengths, wq, wkv, wo, wgu, wd, gains, tokens, dy)
+
+
+ROOT = 0.7978845608028654
+CUBE = 0.044715
+
+
+def ff_kernel(
+    nt_hbm, dy_hbm, gu_hbm, d_hbm, hgu_hbm, sums,
+    wgu, wd, dots, xin, hgu, sendc, recvc, sendx, kept, recvx, recvz,
+    send, recv, load, wload, store,
+):
+    z, r, t = position()
+    x, c = t // 2, t % 2
+    me = z * 2 + r
+    quarter = sums.shape[1]
+    ff, model = wd.shape
+    tile = 256
+    wide = 1024
+
+    loads = [pltpu.make_async_copy(gu_hbm.at[m], wgu.at[m], wload.at[m]) for m in range(2)]
+    loads.append(pltpu.make_async_copy(d_hbm, wd, wload.at[2]))
+    for copy in loads:
+        copy.start()
+
+    order = (3, 2, 1, 0)
+
+    def rows(i, b):
+        cc = c if i % 2 else c ^ 1
+        xx = x if b else x ^ 1
+        return block_rows(z ^ order[i // 2], xx * 2 + cc, quarter)
+
+    def fetch(i):
+        out = []
+        for a, src in enumerate((nt_hbm, dy_hbm)):
+            for b in range(2):
+                copy = pltpu.make_async_copy(
+                    src.at[rows(i, b)],
+                    xin.at[i % 2, a, pl.ds(b * quarter, quarter)],
+                    load.at[i % 2, a, b],
+                )
+                copy.start()
+                out.append(copy)
+        return out
+
+    pending = fetch(0)
+    greet(partners_of(z, r, t, zs=(1, 2), y=False))
+    copies = Copies(send, recv)
+    for copy in loads:
+        copy.wait()
+
+    def take_x(s):
+        copies.arrived(f"x{s}")
+        if s == 1:
+            copies.arrived("z0")
+        if s == 3:
+            copies.arrived("z2")
+            copies.arrived("z1")
+
+        @pl.loop(0, model // tile)
+        def _(n):
+            cols = pl.ds(pl.multiple_of(n * tile, tile), tile)
+            for a in range(2):
+                total = kept[s, a, :, cols].astype(fl) + recvx[s, a, :, cols].astype(fl)
+                if s == 1:
+                    total += recvz[0, a, :, cols].astype(fl)
+                if s == 3:
+                    total += recvz[1, a, :, cols].astype(fl) + recvz[2, a, :, cols].astype(fl)
+                    sums[a, :, cols] = total
+                else:
+                    recvx[s, a, :, cols] = total.astype(bf)
+
+        if s < 3:
+            copies.start(f"z{s}", recvx.at[s], recvz.at[s], at_z(z, r, t, 2 if s == 1 else 1))
+
+    stores = {}
+    for i in range(8):
+        s, own = i // 2, i % 2
+        for copy in pending:
+            copy.wait()
+        if i < 7:
+            pending = fetch(i + 1)
+        if i >= 2:
+            for copy in stores[i - 2]:
+                copy.wait()
+
+        dots[0] = dot(xin[i % 2, 0], wgu[0])
+        dots[1] = dot(xin[i % 2, 0], wgu[1])
+        dots[2] = times_trans(xin[i % 2, 1], wd[...])
+
+        @pl.loop(0, 2 * quarter // 16)
+        def _(n):
+            at = pl.ds(pl.multiple_of(n * 16, 16), 16)
+            for half in range(0, ff, 512):
+                cols = slice(half, half + 512)
+                gate, upper, dh = dots[0, at, cols], dots[1, at, cols], dots[2, at, cols]
+                square = gate * gate
+                bend = jnp.tanh(ROOT * gate * (1.0 + CUBE * square))
+                share = 0.5 * (1.0 + bend)
+                gelu = gate * share
+                slope = share + 0.5 * gate * (1.0 - bend * bend) * (ROOT * (1.0 + 3.0 * CUBE * square))
+                hgu[i % 2, 0, at, cols] = (gelu * upper).astype(bf)
+                hgu[i % 2, 1, at, cols] = (dh * upper * slope).astype(bf)
+                hgu[i % 2, 2, at, cols] = (dh * gelu).astype(bf)
+
+        stores[i] = []
+        for m in range(3):
+            for b in range(2):
+                copy = pltpu.make_async_copy(
+                    hgu.at[i % 2, m, pl.ds(b * quarter, quarter)],
+                    hgu_hbm.at[m, rows(i, b)],
+                    store.at[i % 2, m, b],
+                )
+                copy.start()
+                stores[i].append(copy)
+
+        if own:
+            copies.arrived(f"c{s}")
+            if s >= 2:
+                copies.left(f"x{s - 2}")
+        elif s >= 1:
+            copies.left(f"c{s - 1}")
+
+        @pl.loop(0, model // wide)
+        def _(n):
+            cols = pl.ds(pl.multiple_of(n * wide, wide), wide)
+            out = dot(hgu[i % 2, 0], wd[:, cols])
+            back = times_trans(hgu[i % 2, 1], wgu[0, cols]) + times_trans(hgu[i % 2, 2], wgu[1, cols])
+            for a, part in enumerate((out, back)):
+                if own:
+                    total = part + recvc[s % 2, a, :, cols].astype(fl)
+                    sendx[s % 2, a, :, cols] = total[:quarter].astype(bf)
+                    kept[s, a, :, cols] = total[quarter:].astype(bf)
+                else:
+                    sendc[a, :, cols] = part.astype(bf)
+
+        if own:
+            copies.start(f"x{s}", sendx.at[s % 2], recvx.at[s], (me, t ^ 2))
+            if s >= 2:
+                take_x(s - 2)
+        else:
+            copies.start(f"c{s}", sendc, recvc.at[s % 2], (me, t ^ 1))
+
+    take_x(2)
+    take_x(3)
+    for i in (6, 7):
+        for copy in stores[i]:
+            copy.wait()
+    for name in ("c3", "x2", "x3", "z0", "z1", "z2"):
+        copies.left(name)
+
+
+def feed_forward(nt, dy, wgu, wd):
+    group, model = nt.shape
+    ff = wd.shape[0]
+    quarter = group // 16
+    return pl.pallas_call(
+        ff_kernel,
+        out_shape=(
+            jax.ShapeDtypeStruct((3, group, ff), bf),
+            jax.ShapeDtypeStruct((2, quarter, model), fl),
+        ),
+        in_specs=[ANY] * 4,
+        out_specs=(ANY, VMEM),
+        scratch_shapes=[
+            pltpu.VMEM((2, model, ff), bf),
+            pltpu.VMEM((ff, model), bf),
+            pltpu.VMEM((3, 2 * quarter, ff), fl),
+            pltpu.VMEM((2, 2, 2 * quarter, model), bf),
+            pltpu.VMEM((2, 3, 2 * quarter, ff), bf),
+            pltpu.VMEM((2, 2 * quarter, model), bf),
+            pltpu.VMEM((2, 2, 2 * quarter, model), bf),
+            pltpu.VMEM((2, 2, quarter, model), bf),
+            pltpu.VMEM((4, 2, quarter, model), bf),
+            pltpu.VMEM((4, 2, quarter, model), bf),
+            pltpu.VMEM((3, 2, quarter, model), bf),
+            pltpu.SemaphoreType.DMA((11,)),
+            pltpu.SemaphoreType.DMA((11,)),
+            pltpu.SemaphoreType.DMA((2, 2, 2)),
+            pltpu.SemaphoreType.DMA((3,)),
+            pltpu.SemaphoreType.DMA((2, 3, 2)),
+        ],
+        compiler_params=remote_params(3),
+        name="feed_forward",
+    )(nt, dy, wgu, wd)
+
+
+def backward_kernel(
+    lengths, nt_hbm, dy_hbm, hgu_hbm, sums, resid, dy_own, x_own, gain, one_hbm, q_hbm, kv_hbm, mixed_hbm, qkv_hbm, o_hbm,
+    gu_out, d_out, qkv_grad, kv_grad, o_grad, block_out, input_out, gains_out,
+    sendy_gu, sendy_d, recvy_gu, recvy_d, own_gu, own_d,
+    a, d_resid, out_own, gacc, grecv, gmine, grecv_t,
+    gp, dkv_send, dkv_recv, dkv_x, dkv_rx, part, precv, sendx, recvx,
+    pk_send, po_send, pk_recv, po_recv, pk_own, po_own, pk_z, po_z,
+    send, recv, load, local,
+):
+    z, r, t = position()
+    me = z * 2 + r
+    quarter, model = resid.shape
+    slot = 4 * quarter
+    rows = model // 8
+    ff = own_d.shape[1]
+    kvt = dkv_x.shape[1]
+    width = gp.shape[1] - kvt
+    other = (z * 2 + (r ^ 1), t)
+    x_peer, core_peer, far_peer = (me, t ^ 2), (me, t ^ 1), (me, t ^ 3)
+
+    def d_block(k, j=0):
+        return pl.ds(pl.multiple_of(((z ^ k) * 2 + (r ^ j)) * rows, rows), rows)
+
+    def own_rows(j):
+        return pl.ds(pl.multiple_of((t ^ j) * quarter, quarter), quarter)
+
+    loads = [
+        pltpu.make_async_copy(sums.at[1], d_resid, load.at[0]),
+        pltpu.make_async_copy(sums.at[0], out_own, load.at[1]),
+    ]
+    for copy in loads:
+        copy.start()
+    greet(partners_of(z, r, t, zs=(1, 2, 3)) + [far_peer] + [((z ^ k) * 2 + (r ^ 1), t) for k in (1, 2, 3)])
+    copies = Copies(send, recv)
+    locals_ = []
+    counter = list(range(8))
+
+    def keep(src, dst):
+        copy = pltpu.make_async_copy(src, dst, local.at[counter.pop(0)])
+        copy.start()
+        locals_.append(copy)
+        return copy
+
+    def norm_back(v, grad, row):
+        inverse = lax.rsqrt(jnp.mean(v * v, axis=-1, keepdims=True) + norm_eps)
+        scaled = v * inverse
+        gacc[row : row + 1, :] += jnp.sum(grad * scaled, axis=0, keepdims=True)
+        inner = grad * gain[row : row + 1, :]
+        return inverse * (inner - scaled * jnp.mean(inner * scaled, axis=-1, keepdims=True))
+
+    gacc[...] = jnp.zeros_like(gacc)
+    for copy in loads:
+        copy.wait()
+
+    @pl.loop(0, quarter // 16)
+    def _(i):
+        at = pl.ds(pl.multiple_of(i * 16, 16), 16)
+        mine = pl.ds(pl.multiple_of(t * quarter + i * 16, 16), 16)
+        v = resid[at]
+        total = dy_own[at].astype(fl) + norm_back(v, d_resid[at], 1)
+        d_resid[at] = total
+        a[mine] = total.astype(bf)
+        out_own[at] += v
+
+    copies.start("ax", a.at[own_rows(0)], a.at[own_rows(0)], x_peer)
+    copies.start("ac", a.at[own_rows(0)], a.at[own_rows(0)], core_peer)
+    keep(out_own, block_out.at[own_rows(0)])
+    in_own = out_own
+    copies.start("bx", out_own, block_out.at[own_rows(0)], x_peer)
+    copies.start("bc", out_own, block_out.at[own_rows(0)], core_peer)
+
+    zorder = (1, 3, 2, 0)
+
+    def send_y(i):
+        k = zorder[i]
+        for m in range(2):
+            copies.start(f"y{k}{m}", lambda m=m: sendy_gu.at[i, m], lambda m=m: recvy_gu.at[i, m], other)
+        copies.start(f"y{k}2", lambda: sendy_d.at[i], lambda: recvy_d.at[i], other)
+
+    def feed_forward_grads(hgu, lhs):
+        loads = [pltpu.make_async_copy(hgu_hbm.at[m], hgu.at[m], load.at[m]) for m in range(3)]
+
+        def fetch(i):
+            cols = d_block(zorder[i % 4], 0 if i >= 4 else 1)
+            made = []
+            for n, src in enumerate((nt_hbm, dy_hbm)):
+                copy = pltpu.make_async_copy(src.at[:, cols], lhs.at[i % 2, n], load.at[3 + 2 * (i % 2) + n])
+                copy.start()
+                made.append(copy)
+            return made
+
+        pending = fetch(0)
+        for m in (1, 2, 0):
+            loads[m].start()
+        for i in range(8):
+            for copy in pending:
+                copy.wait()
+            if i < 7:
+                pending = fetch(i + 1)
+            to_gu, to_d = (sendy_gu, sendy_d) if i < 4 else (own_gu, own_d)
+            for m, (h, n) in enumerate(((1, 0), (2, 0), (0, 1))):
+                if i == 0:
+                    loads[h].wait()
+
+                @pl.loop(0, ff // 512)
+                def _(c):
+                    cols = pl.ds(pl.multiple_of(c * 512, 512), 512)
+                    grad = inner_rows(lhs[i % 2, n], hgu[h, :, cols])
+                    if m < 2:
+                        to_gu[i % 4, m, :, cols] = grad.astype(bf)
+                    else:
+                        to_d[i % 4, cols, :] = grad.T.astype(bf)
+
+            if i < 3:
+                send_y(i)
+
+    group = nt_hbm.shape[0]
+    pl.run_scoped(
+        feed_forward_grads, pltpu.VMEM((3, group, ff), bf), pltpu.VMEM((2, 2, group, rows), bf)
+    )
+
+    flows = [(i, m) for i in range(3) for m in range(3)]
+    taken = [0]
+
+    def own_of(i, m):
+        return own_d.at[i] if m == 2 else own_gu.at[i, m]
+
+    def add_y(i, m):
+        mine, theirs = own_of(i, m), (recvy_d.at[i] if m == 2 else recvy_gu.at[i, m])
+
+        @pl.loop(0, mine.shape[0] // 64)
+        def _(n):
+            at = pl.ds(pl.multiple_of(n * 64, 64), 64)
+            mine[at] = (mine[at].astype(fl) + theirs[at].astype(fl)).astype(bf)
+
+    def place(m):
+        cols = pl.ds(pl.multiple_of(z * ff, ff), ff)
+        return d_out.at[cols] if m == 2 else gu_out.at[m, :, cols]
+
+    at_zs = [at_z(z, r, t, k) for k in range(4)]
+
+    def pump(n):
+        for _ in range(n):
+            if taken[0] < len(flows):
+                i, m = flows[taken[0]]
+                k = zorder[i]
+                copies.arrived(f"y{k}{m}")
+                add_y(i, m)
+                copies.start(f"z{k}{m}", lambda i=i, m=m: own_of(i, m), lambda m=m: place(m), at_zs[k])
+                taken[0] += 1
+
+    pump(3)
+    copies.arrived("ax")
+    copies.start("af", a.at[own_rows(2)], a.at[own_rows(2)], core_peer)
+    copies.arrived("bx")
+    copies.start("bf", block_out.at[own_rows(2)], block_out.at[own_rows(2)], core_peer)
+
+    def attention(q, kv, mixed, qkv, o, one, dm, dkv):
+        loads = [
+            pltpu.make_async_copy(src, dst, load.at[i])
+            for i, (src, dst) in enumerate(
+                ((o_hbm, o), (q_hbm, q), (kv_hbm, kv), (mixed_hbm, mixed), (qkv_hbm, qkv), (one_hbm, one))
+            )
+        ]
+        for copy in loads:
+            copy.start()
+        copies.arrived("ac")
+        copies.arrived("af")
+        for copy in loads:
+            copy.wait()
+        dm[...] = times_trans(a[...], o[...]).astype(bf)
+        length = lengths[0]
+        step = 128
+        dkv[...] = jnp.zeros_like(dkv)
+        for h in range(width // HD):
+            head = slice(h * HD, (h + 1) * HD)
+            for i in range(slot // step):
+                at, upto = pl.ds(i * step, step), pl.ds(0, (i + 1) * step)
+                probs = probabilities(q[at, head], kv[upto, :HD], length, i * step)
+                d_probs = times_trans(dm[at, head], kv[upto, HD:])
+                d_scores = probs * (d_probs - jnp.sum(d_probs * probs, axis=-1, keepdims=True))
+                d_raw = (d_scores * HD ** (-0.5)).astype(bf)
+                gp[at, head] = dot(d_raw, kv[upto, :HD]).astype(bf)
+                dkv[upto, :HD] += inner_rows(d_raw, q[at, head])
+                dkv[upto, HD:] += inner_rows(probs.astype(bf), dm[at, head])
+            pump(1)
+
+        def kv_cols(j):
+            return pl.ds(pl.multiple_of((t ^ j) * kvt, kvt), kvt)
+
+        dkv_send[0] = dkv[:, kv_cols(1)].astype(bf)
+        dkv_send[1] = dkv[:, kv_cols(3)].astype(bf)
+        copies.start("kc", lambda: dkv_send, lambda: dkv_recv, core_peer)
+        copies.arrived("kc")
+        dkv_x[...] = (dkv[:, kv_cols(2)] + dkv_recv[1].astype(fl)).astype(bf)
+        copies.start("kx", lambda: dkv_x, lambda: dkv_rx, x_peer)
+        mine = dkv[:, kv_cols(0)] + dkv_recv[0].astype(fl)
+        copies.arrived("kx")
+        gp[:, width:] = (mine + dkv_rx[...].astype(fl)).astype(bf)
+
+        def part_of(j, store_part):
+            at = own_rows(j)
+            for n in range(0, model, 512):
+                store_part(times_trans(gp[at], qkv[n : n + 512]), slice(n, n + 512))
+
+        def into_part(i):
+            def put(value, cols):
+                part[i, :, cols] = value.astype(bf)
+
+            return put
+
+        part_of(3, into_part(0))
+        part_of(1, into_part(1))
+        copies.start("pc", lambda: part, lambda: precv, core_peer)
+
+        def pack_grads(k, j, to_k, to_o):
+            cols = d_block(k, j)
+            to_k[...] = inner_rows(one[:, cols], gp[...]).astype(to_k.dtype)
+            to_o[...] = inner_rows(mixed[...], a[:, cols]).astype(to_o.dtype)
+
+        for i, k in enumerate(zorder):
+            pack_grads(k, 1, pk_send.at[i], po_send.at[i])
+            copies.start(f"yp{k}", lambda i=i: pk_send.at[i], lambda i=i: pk_recv.at[i], other)
+            copies.start(f"yo{k}", lambda i=i: po_send.at[i], lambda i=i: po_recv.at[i], other)
+        send_y(3)
+
+        copies.arrived("pc")
+
+        def into_x(value, cols):
+            sendx[:, cols] = (value + precv[0, :, cols].astype(fl)).astype(bf)
+
+        part_of(2, into_x)
+        copies.start("px", lambda: sendx, lambda: recvx, x_peer)
+
+        copies.left("bx")
+        copies.left("bc")
+        locals_.pop(0).wait()
+
+        def into_own(value, cols):
+            in_own[:, cols] = value + precv[1, :, cols].astype(fl)
+
+        part_of(0, into_own)
+        for i, k in enumerate(zorder):
+            pack_grads(k, 0, pk_own.at[i], po_own.at[i])
+        copies.arrived("px")
+
+    pl.run_scoped(
+        attention,
+        pltpu.VMEM((slot, width), bf),
+        pltpu.VMEM((slot, 2 * HD), bf),
+        pltpu.VMEM((slot, width), bf),
+        pltpu.VMEM((model, width + kvt), bf),
+        pltpu.VMEM((width, model), bf),
+        pltpu.VMEM((slot, model), bf),
+        pltpu.VMEM((slot, width), bf),
+        pltpu.VMEM((slot, 2 * HD), fl),
+    )
+
+    @pl.loop(0, quarter // 16)
+    def _(i):
+        at = pl.ds(pl.multiple_of(i * 16, 16), 16)
+        grad = in_own[at] + recvx[at].astype(fl)
+        in_own[at] = d_resid[at] + norm_back(x_own[at].astype(fl), grad, 0)
+
+    keep(in_own, input_out.at[own_rows(0)])
+    copies.start("ix", in_own, input_out.at[own_rows(0)], x_peer)
+    copies.start("ic", in_own, input_out.at[own_rows(0)], core_peer)
+
+    for k in range(4):
+        for j in range(2):
+            if k or j:
+                copies.start(
+                    f"g{k}{j}", gacc.at[:, d_block(k, j)], grecv.at[2 * k + j], ((z ^ k) * 2 + (r ^ j), t)
+                )
+    pump(9)
+
+    def add_pack(i):
+        k = zorder[i]
+        copies.arrived(f"yp{k}")
+        copies.arrived(f"yo{k}")
+        for mine, theirs in ((pk_own.at[i], pk_recv.at[i]), (po_own.at[i], po_recv.at[i])):
+            mine[...] = (mine[...].astype(fl) + theirs[...].astype(fl)).astype(mine.dtype)
+
+    for i in range(3):
+        add_pack(i)
+        k = zorder[i]
+        copies.start(f"zp{k}", pk_own.at[i], pk_z.at[i], at_z(z, r, t, k))
+        copies.start(f"zo{k}", po_own.at[i], po_z.at[i], at_z(z, r, t, k))
+    add_pack(3)
+    total = gacc[:, d_block(0)]
+    for k in range(4):
+        for j in range(2):
+            if k or j:
+                copies.arrived(f"g{k}{j}")
+                total += grecv[2 * k + j]
+    gmine[...] = total
+    for j, peer in ((1, core_peer), (2, x_peer), (3, far_peer)):
+        copies.start(f"gt{j}", gmine, grecv_t.at[j], peer)
+    copies.arrived("ix")
+    copies.start("if", input_out.at[own_rows(2)], input_out.at[own_rows(2)], core_peer)
+
+    for m in range(3):
+        copies.arrived(f"y0{m}")
+        add_y(3, m)
+        keep(own_of(3, m), place(m))
+    for i in range(3):
+        copies.arrived(f"zp{zorder[i]}")
+        copies.arrived(f"zo{zorder[i]}")
+    pk_sum = pk_own[3].astype(fl)
+    po_sum = po_own[3].astype(fl)
+    for i in range(3):
+        pk_sum += pk_z[i].astype(fl)
+        po_sum += po_z[i].astype(fl)
+    qkv_grad[...] = pk_sum
+    o_grad[...] = po_sum
+    mine = pl.ds(pl.multiple_of(t * kvt, kvt), kvt)
+    kv_grad[:, mine] = pk_sum[:, width:]
+    for j, peer in ((1, core_peer), (2, x_peer), (3, far_peer)):
+        copies.start(f"kg{j}", kv_grad.at[:, mine], kv_grad.at[:, mine], peer)
+    total = gmine[...]
+    for j in (1, 2, 3):
+        copies.arrived(f"gt{j}")
+        total += grecv_t[j]
+    gains_out[...] = total
+    for name in ("ic", "if", "bc", "bf", "kg1", "kg2", "kg3"):
+        copies.arrived(name)
+    for i in range(3):
+        for m in range(3):
+            copies.arrived(f"z{zorder[i]}{m}")
+    copies.all_left()
+    for copy in locals_:
+        copy.wait()
+
+
+def backward_part(lengths, nt, dy, hgu, sums, resid, dy_own, x_own, gain, one, q, kv, mixed, qkv, o):
+    group, model = nt.shape
+    ff = hgu.shape[2]
+    rows = model // 8
+    quarter = resid.shape[0]
+    slot, width = q.shape
+    kvt = qkv.shape[1] - width
+    n = 2 + 2 + 2 + 12 + 9 + 2 + 8 + 2 + 3 + 7 + 6 + 3 + 3
+    shape = jax.ShapeDtypeStruct
+    buf = pltpu.VMEM
+    return pl.pallas_call(
+        backward_kernel,
+        out_shape=(
+            shape((2, rows, ZN * ff), bf),
+            shape((ZN * ff, rows), bf),
+            shape((rows, width + kvt), fl),
+            shape((rows, 4 * kvt), fl),
+            shape((width, rows), fl),
+            shape((slot, model), fl),
+            shape((slot, model), fl),
+            shape((8, rows), fl),
+        ),
+        in_specs=[pl.BlockSpec(memory_space=pltpu.SMEM)] + [ANY] * 4 + [VMEM] * 4 + [ANY] * 6,
+        out_specs=(ANY, ANY, VMEM, VMEM, VMEM, ANY, ANY, VMEM),
+        scratch_shapes=[
+            buf((4, 2, rows, ff), bf), buf((4, ff, rows), bf),
+            buf((4, 2, rows, ff), bf), buf((4, ff, rows), bf),
+            buf((4, 2, rows, ff), bf), buf((4, ff, rows), bf),
+            buf((slot, model), bf), buf((quarter, model), fl), buf((quarter, model), fl),
+            buf((8, model), fl), buf((8, 8, rows), fl), buf((8, rows), fl), buf((4, 8, rows), fl),
+            buf((slot, width + kvt), bf), buf((2, slot, kvt), bf), buf((2, slot, kvt), bf),
+            buf((slot, kvt), bf), buf((slot, kvt), bf),
+            buf((2, quarter, model), bf), buf((2, quarter, model), bf),
+            buf((quarter, model), bf), buf((quarter, model), bf),
+            buf((4, rows, width + kvt), bf), buf((4, width, rows), bf),
+            buf((4, rows, width + kvt), bf), buf((4, width, rows), bf),
+            buf((4, rows, width + kvt), bf), buf((4, width, rows), bf),
+            buf((3, rows, width + kvt), bf), buf((3, width, rows), bf),
+            pltpu.SemaphoreType.DMA((n,)),
+            pltpu.SemaphoreType.DMA((n,)),
+            pltpu.SemaphoreType.DMA((7,)),
+            pltpu.SemaphoreType.DMA((8,)),
+        ],
+        compiler_params=remote_params(4),
+        name="backward_part",
+    )(lengths, nt, dy, hgu, sums, resid, dy_own, x_own, gain, one, q, kv, mixed, qkv, o)
+
+
+def fast(
+    tokens,
+    cotangent,
+    lengths,
+    w_query,
+    w_keyval,
+    w_output,
+    w_gateup,
+    w_down,
+    norm_gains,
+    first_query,
+    first_keyval,
+    first_output,
+    first_gateup,
+    first_down,
+    first_gains,
+    second_query,
+    second_keyval,
+    second_output,
+    second_gateup,
+    second_down,
+    second_gains,
+):
+    t = lax.axis_index("tensor")
+    quarter = tokens.shape[0] // lax.axis_size("tensor")
+    length = lengths[0]
+
+    cot_own = lax.dynamic_slice_in_dim(cotangent, t * quarter, quarter, 0)
+    valid = (t * quarter + jnp.arange(quarter) < length)[:, None]
+    grad_own = jnp.where(valid, cot_own, jnp.zeros_like(cot_own))
+    gains_low = jnp.pad(norm_gains.astype(bf).astype(fl), ((0, 6), (0, 0)))
+    (
+        gateup, down, dy, normed_two, resid, normed_one, query, keyval, mixed, qkv_w, output_w, gain_full,
+    ) = forward_part(lengths, w_query, w_keyval, w_output, w_gateup, w_down, gains_low, tokens, grad_own)
+    x_own = lax.dynamic_slice_in_dim(tokens, t * quarter, quarter, 0)
+
+    hgu, sums = feed_forward(normed_two, dy, gateup, down)
+    (
+        gateup_grad, down_grad, qkv_grad, keyval_shard, output_shard, block_output, input_grad, gains_grad,
+    ) = backward_part(
+        lengths, normed_two, dy, hgu, sums, resid, grad_own, x_own, gain_full,
+        normed_one, query, keyval, mixed, qkv_w, output_w,
+    )
+    query_shard = qkv_grad[:, : w_query.shape[1]]
+    gateup_shard = gateup_grad.astype(fl)
+    down_shard = down_grad.astype(fl)
+    gains_shard = gains_grad[:2]
+
+    qa = adamw(w_query, query_shard, first_query, second_query, decay_rate)
+    ka = adamw(w_keyval, keyval_shard, first_keyval, second_keyval, decay_rate)
+    oa = adamw(w_output, output_shard, first_output, second_output, decay_rate)
+    ga = adamw(w_gateup, gateup_shard, first_gateup, second_gateup, decay_rate)
+    da = adamw(w_down, down_shard, first_down, second_down, decay_rate)
+    na = adamw(norm_gains, gains_shard, first_gains, second_gains, 0.0)
+    return (block_output, input_grad, *qa, *ka, *oa, *ga, *da, *na)
+
+
 def solution(mesh):
     query = P("dp", "tensor")
     keyval = P("dp", None)
@@ -342,7 +1420,7 @@
     gains = P(None, "dp")
     weights = (query, keyval, output, gateup, output, gains)
     return jax.shard_map(
-        shards,
+        fast if mesh.shape["dp"] == 2 * ZN and mesh.shape["tensor"] == 4 else general,
         mesh=mesh,
         in_specs=(P("dp", None), P("dp", None), P("dp")) + weights * 3,
         out_specs=(P("dp", None), P("dp", None)) + tuple(w for w in weights for _ in range(4)),

time: 1470 us -> 786 us (0.53)
  Pallas kernels: 0 us -> 725 us
  local copies, waits for them, and re-layouts: 552 us -> 7.05 us
  waiting for transfers between devices: 455 us -> 0 us
  matrix products: 210 us -> 0 us
  starting transfers between devices: 114 us -> 0 us
  other arithmetic: 116 us -> 43.9 us
    pallas_call x0 -> x3, Pallas kernels: none -> 725 us  [the longest x1 281 us: forward_part(): pl.pallas_call(forward_kernel, out_shape=(shape((2, model, ff), bf), shap...]
    ppermute x78 -> x0, waiting for transfers between devices: 455 us -> none  [swap(): lax.ppermute(value, axis, [(i, i ^ bit) for i in range(lax.axis_size(axis...]
    dynamic_update_slice x76 -> x0, local copies, waits for them, and re-layouts: 210 us -> none  [the longest x12 142 us: scatter_z(): out = lax.dynamic_update_index_in_dim(out, parts[k], z ^ k, axis)]
    dot_general x24 -> x0, matrix products: 210 us -> none  [the longest x5 77.8 us: times_trans(): lax.dot_general(left, right, (((1,), (1,)), ((), ())), preferred_element_...]
    dynamic_slice x14 -> x0, local copies, waits for them, and re-layouts: 150 us -> none  [take(): return lax.dynamic_index_in_dim(array, index, axis, keepdims=False)]
    ppermute x78 -> x0, starting transfers between devices: 114 us -> none  [swap(): lax.ppermute(value, axis, [(i, i ^ bit) for i in range(lax.axis_size(axis...]
    broadcast_in_dim x43 -> x0, local copies, waits for them, and re-layouts: 50.7 us -> none  [the longest x12 20.7 us: shards(): down_w = lax.dynamic_update_index_in_dim(down_w, block, z ^ k, 1)]
    another operation x10 -> x0, local copies, waits for them, and re-layouts: 41 us -> none  [the longest x2 35.4 us: columns(): array.reshape(group, ZN, rn, rows)]
  transfers between devices with their start and end apart: 78 -> 0, of which waited for: 38 -> 0; matrix products, arithmetic and copies ran while one was open for 42% -> 0% of each run, Pallas kernels for 0% -> 0%
where the time goes in v3:
time: 786 us; the launch traced here: 777 us
  Pallas kernels  725 us (92%)
  other arithmetic  43.9 us (6%)
    pallas_call x1, Pallas kernels, forward_part(): pl.pallas_call(forward_kernel, out_shape=(shape((2, model, ff), bf), shap...  281 us
    pallas_call x1, Pallas kernels, backward_part(): pl.pallas_call(backward_kernel, out_shape=(shape((2, rows, ZN * ff), bf),...  268 us
    pallas_call x1, Pallas kernels, feed_forward(): pl.pallas_call(ff_kernel, out_shape=(jax.ShapeDtypeStruct((3, group, ff),...  175 us
    mul x6, other arithmetic, adamw(): -learn_rate  40.1 us

profile of v3, /device:TPU:0, one launch (start us, length us, event | category | flops | bytes accessed | tf_op | source)
XLA Modules:
  0.0 777.4 jit_solution(14420833908409550726)
XLA Ops:
  1.3 2.5 dynamic-slice_select_fusion
  3.9 0.7 convert_element_type.12
  4.6 0.6 pad_convert_fusion.gains
  5.2 281.5 %forward_part.1 = (bf16[2,2048,1024]{2,1,0:T(8,128)(2,1)}, bf16[1024,2048]{1,0:T(8,128)(2,1)}, bf16[2560,2048]{1,0:T(8,128)(2,1)}, bf16[2560,2048]{1,0:T(8,128)(...) custom-call(s32[1]{0:T(128)} %copy.51.lengths, ...), custom_call_target="tpu_custom_call" | custom-call | tf_op jit(solution)/shard_map/forward_part/pallas_call | solution.py:742
  286.6 175.1 %feed_forward.1 = (bf16[3,2560,1024]{2,1,0:T(8,128)(2,1)}, f32[2,160,2048]{2,1,0:T(8,128)}) custom-call(bf16[2560,2048]{1,0:T(8,128)(2,1)} %get-tuple-element.48.nt_hbm, bf16[2560,2048]{1,0:T(8,128)(2,1)} %get-tuple-element.49.dy_hbm, bf16[2,2048,1024]{2,1,0:T(8,128)(2,1)} %get-tuple-element.50.gu_hbm, bf16[1024,2048]{1,0:T(8,128)(2,1)} %get-tuple-element.51.d_hbm), custom_call_target="tpu_custom_call" | custom-call | tf_op jit(solution)/shard_map/feed_forward/pallas_call | solution.py:945
  461.7 268.1 %backward_part.1 = (bf16[2,256,4096]{2,1,0:T(8,128)(2,1)}, bf16[4096,256]{1,0:T(8,128)(2,1)}, f32[256,640]{1,0:T(8,128)}, f32[256,512]{1,0:T(8,128)}, f32[512,25...) custom-call(s32[1]{0:T(128)} %copy.51.lengths, ...), custom_call_target="tpu_custom_call" | custom-call | tf_op jit(solution)/shard_map/backward_part/pallas_call | solution.py:1320
  729.8 22.7 %add_multiply_fusion = (f32[2,256,4096]{2,1,0:T(8,128)}, f32[2,256,4096]{2,1,0:T(8,128)}, f32[2,256,4096]{2,1,0:T(8,128)}, f32[2,256,4096]{2,1,0:T(8,128)}) fusion(f32[2,256,4096]{2,1,0:T(8,128)} %wgu.1, f32[2,256,4096]{2,1,0:T(8,128)} %param.39, f32[2,256,4096]{2,1,0:T(8,128)} %param.33, bf16[2,256,4096]{2,1,0:T(8,128)(2,1)} %get-tuple-element.67), kind=kLoop, calls=%fused_computation.2 | loop fusion | flops 27262976 | bytes 62914560 | tf_op jit(solution)/shard_map/mul | solution.py:87
  752.6 0.0 copy-start.4
  752.6 0.0 copy-start.10
  752.6 0.0 copy-start.11
  752.6 11.4 %add_multiply_fusion.1 = (f32[4096,256]{1,0:T(8,128)}, f32[4096,256]{1,0:T(8,128)}, f32[4096,256]{1,0:T(8,128)}, f32[4096,256]{1,0:T(8,128)}) fusion(f32[4096,256]{1,0:T(8,128)} %wd.1, f32[4096,256]{1,0:T(8,128)} %param.40, f32[4096,256]{1,0:T(8,128)} %param.34, bf16[4096,256]{1,0:T(8,128)(2,1)S(1)} %copy-done.5), kind=kLoop, calls=%fused_computation.6 | loop fusion | flops 13631488 | bytes 31457280 | tf_op jit(solution)/shard_map/mul | solution.py:87
  764.1 0.0 copy-start.6
  764.1 0.0 copy-start.8
  764.1 0.0 copy-start.9
  764.2 1.5 add_multiply_fusion.4
  765.7 0.1 copy-done.6
  765.8 0.5 copy-done.7
  766.3 1.4 add_multiply_fusion.3
  767.7 1.3 add_multiply_fusion.2
  769.1 1.8 add_multiply_fusion.5
  770.8 2.4 copy.52
  773.2 2.4 copy.53
  775.6 0.8 copy.54
  776.4 0.8 copy.55
  (35 shorter events, 0.1 us)
Async XLA Ops:
  729.8 22.7 %copy-start.5 = (bf16[4096,256]{1,0:T(8,128)(2,1)S(1)}, bf16[4096,256]{1,0:T(8,128)(2,1)}, u32[]{:S(2)}) copy-start(bf16[4096,256]{1,0:T(8,128)(2,1)} %get-tuple-element.68) | copy-start | bytes 6291460
  752.6 18.3 %slice-start.2 = ((s8[5242880]{0:T(1024)(128)(4,1)}), s8[4194304]{0:T(1024)(128)(4,1)S(1)}, s32[]{:S(2)}) async-start(s8[5242880]{0:T(1024)(128)(4,1)} %bitcast.4), calls=%async_computation.2 | async-start | bytes 8388608
  752.6 11.6 %copy-start.4 = (f32[256,512]{1,0:T(8,128)S(1)}, f32[256,512]{1,0:T(8,128)}, u32[]{:S(2)}) copy-start(f32[256,512]{1,0:T(8,128)} %wq.1) | copy-start | bytes 1572868
  752.6 11.6 %copy-start.10 = (f32[256,512]{1,0:T(8,128)S(1)}, f32[256,512]{1,0:T(8,128)}, u32[]{:S(2)}) copy-start(f32[256,512]{1,0:T(8,128)} %param.36) | copy-start | bytes 1572868
  752.6 11.6 %copy-start.11 = (f32[256,512]{1,0:T(8,128)S(1)}, f32[256,512]{1,0:T(8,128)}, u32[]{:S(2)}) copy-start(f32[256,512]{1,0:T(8,128)} %param.30) | copy-start | bytes 1572868
  752.6 11.6 %copy-start.12 = (f32[256,640]{1,0:T(8,128)S(1)}, f32[256,640]{1,0:T(8,128)}, u32[]{:S(2)}) copy-start(f32[256,640]{1,0:T(8,128)} %get-tuple-element.64) | copy-start | bytes 1966084
  752.6 18.2 %slice-start.3 = ((s8[5242880]{0:T(1024)(128)(4,1)}), s8[1048576]{0:T(1024)(128)(4,1)S(1)}, s32[]{:S(2)}) async-start(s8[5242880]{0:T(1024)(128)(4,1)} %bitcast.4), calls=%async_computation.3 | async-start | bytes 2097152
  764.0 1.6 copy-start
  764.0 1.6 copy-start.3
  764.1 1.8 copy-start.6
  764.1 2.3 copy-start.7
  764.1 3.6 copy-start.1
  764.1 3.6 copy-start.2
  764.1 3.6 copy-start.8
  764.1 3.6 copy-start.9
  765.6 3.4 copy-start.13
  765.6 3.4 copy-start.14
  765.7 3.4 copy-start.15
  767.7 5.5 slice-start
  770.8 2.4 slice-start.1

commit v4 on v3

--- a/solution.py
+++ b/solution.py
@@ -341,8 +341,9 @@
 MESH = pl.DeviceIdType.MESH
 ANY = pl.BlockSpec(memory_space=pl.ANY)
 VMEM = pl.BlockSpec(memory_space=pltpu.VMEM)
-LIMIT = 62 * 1024 * 1024
-WINDOW = 4
+LIMIT = 127 * 512 * 1024
+WINDOW = 1
+PIECES = 1
 
 
 def position():
@@ -366,9 +367,9 @@
     def __init__(self, send, recv):
         self.send, self.recv, self.made, self.gone = send, recv, {}, set()
 
-    def start(self, name, src, dst, device):
+    def start(self, name, src, dst, device, sent=None, got=None):
         i = len(self.made)
-        self.made[name] = lambda: pltpu.make_async_remote_copy(
+        make = lambda: pltpu.make_async_remote_copy(
             src_ref=src() if callable(src) else src,
             dst_ref=dst() if callable(dst) else dst,
             send_sem=self.send.at[i],
@@ -376,15 +377,18 @@
             device_id=device,
             device_id_type=MESH,
         )
-        self.made[name]().start()
+        self.made[name] = (make, sent, got)
+        maybe(sent, lambda: make().start())
 
     def arrived(self, name):
-        self.made[name]().wait_recv()
+        make, _, got = self.made[name]
+        maybe(got, lambda: make().wait_recv())
 
     def left(self, name):
         if name not in self.gone:
             self.gone.add(name)
-            self.made[name]().wait_send()
+            make, sent, _ = self.made[name]
+            maybe(sent, lambda: make().wait_send())
 
     def all_left(self, keep=lambda name: True):
         for name in self.made:
@@ -392,6 +396,35 @@
                 self.left(name)
 
 
+def maybe(condition, action):
+    if condition is None:
+        action()
+    else:
+        pl.when(condition)(action)
+
+
+class Line:
+    def __init__(self):
+        self.z, self.r, self.t = position()
+
+    def block(self, way, s):
+        return lax.max(lax.min(self.z - way * s, 3), 0)
+
+    def device(self, way):
+        return (lax.max(lax.min(self.z + way, 3), 0) * 2 + self.r, self.t)
+
+    def sent(self, way, s):
+        if way > 0:
+            return (self.z < 3) & (self.z >= s)
+        return (self.z > 0) & (self.z + s <= 3)
+
+    def got(self, way, s):
+        return self.z >= 1 + s if way > 0 else self.z + 1 + s <= 3
+
+
+WAYS = ((1, "u"), (-1, "d"))
+
+
 def remote_params(number, limit=LIMIT):
     return pltpu.CompilerParams(
         collective_id=number, has_side_effects=True, vmem_limit_bytes=limit
@@ -403,45 +436,62 @@
 
 
 class TokenGather:
-    count = 15
+    count = 27
 
     def __init__(self, copies, own, out, tag):
         self.copies, self.own, self.out, self.tag = copies, own, out, tag
+        self.line = Line()
         self.z, self.r, self.t = position()
         self.quarter = own.shape[0]
 
-    def rows(self, k, j):
-        return self.out.at[block_rows(self.z ^ k, self.t ^ j, self.quarter)]
-
-    def source(self, k, j):
-        return self.own if k == 0 and j == 0 else self.rows(k, j)
-
-    def send(self, name, k, j, device):
-        self.copies.start(self.tag + name, self.source(k, j), self.rows(k, j), device)
-
-    def send_z(self):
-        self.send("z2", 0, 0, at_z(self.z, self.r, self.t, 2))
-        self.send("z1", 0, 0, at_z(self.z, self.r, self.t, 1))
-
-    def send_x(self, k):
-        me = self.z * 2 + self.r
-        self.send(f"x{k}", k, 0, (me, self.t ^ 2))
-        self.send(f"c{k}0", k, 0, (me, self.t ^ 1))
-
-    def take_z(self, k):
-        self.copies.arrived(f"{self.tag}z{k}")
-        if k == 2:
-            self.send("z3", 2, 0, at_z(self.z, self.r, self.t, 1))
-        self.send_x(k)
-
-    def take_x(self, k):
-        self.copies.arrived(f"{self.tag}x{k}")
-        self.send(f"c{k}1", k, 2, (self.z * 2 + self.r, self.t ^ 1))
+    def rows(self, b, j):
+        return self.out.at[block_rows(b, self.t ^ j, self.quarter)]
+
+    def send_z(self, s):
+        for way, mark in WAYS:
+            b = self.line.block(way, s)
+            self.copies.start(
+                f"{self.tag}z{mark}{s}",
+                self.own if s == 0 else self.rows(b, 0),
+                self.rows(b, 0),
+                self.line.device(way),
+                self.line.sent(way, s),
+                self.line.got(way, s),
+            )
+
+    def over(self, name, src, b, j, step, got):
+        self.copies.start(
+            self.tag + name, src, self.rows(b, j), (self.z * 2 + self.r, self.t ^ step), got, got
+        )
+
+    def send_own(self):
+        self.over("xo", self.own, self.z, 0, 2, None)
+        self.over("co0", self.own, self.z, 0, 1, None)
+
+    def take_z(self, s):
+        for way, mark in WAYS:
+            self.copies.arrived(f"{self.tag}z{mark}{s}")
+        if s < 2:
+            self.send_z(s + 1)
+        for way, mark in WAYS:
+            b, got = self.line.block(way, s + 1), self.line.got(way, s)
+            self.over(f"x{mark}{s}", self.rows(b, 0), b, 0, 2, got)
+            self.over(f"c{mark}{s}0", self.rows(b, 0), b, 0, 1, got)
+
+    def take_own(self):
+        self.copies.arrived(f"{self.tag}xo")
+        self.over("co1", self.rows(self.z, 2), self.z, 2, 1, None)
+
+    def take_x(self, s):
+        for way, mark in WAYS:
+            self.copies.arrived(f"{self.tag}x{mark}{s}")
+            b = self.line.block(way, s + 1)
+            self.over(f"c{mark}{s}1", self.rows(b, 2), b, 2, 1, self.line.got(way, s))
 
     def finish(self):
-        for k in range(4):
-            for j in range(2):
-                self.copies.arrived(f"{self.tag}c{k}{j}")
+        for name in list(self.copies.made):
+            if name.startswith(self.tag + "c"):
+                self.copies.arrived(name)
         self.copies.all_left(lambda name: name.startswith(self.tag))
 
 
@@ -549,19 +599,34 @@
                     f"g{k}{j}", gain.at[:, d_block(0)], gain.at[:, d_block(0)], ((z ^ k) * 2 + (r ^ j), t)
                 )
 
-    def pack_send(name, k, device):
-        copies.start("q" + name, qkv.at[d_block(k)], qkv.at[d_block(k)], device)
-        copies.start("o" + name, o.at[:, d_block(k)], o.at[:, d_block(k)], device)
-
-    def pack_arrived(name):
-        copies.arrived("q" + name)
-        copies.arrived("o" + name)
-
-    pack_send("z2", 0, at_z(z, r, t, 2))
-    pack_send("z1", 0, at_z(z, r, t, 1))
-    pack_send("y0", 0, other)
-    d.send_z()
-    d.send_x(0)
+    line = Line()
+
+    def pack_send(tag, name, b, device, sent=None, got=None):
+        at = pl.ds(pl.multiple_of((b * 2 + r) * rows, rows), rows)
+        ref = qkv.at[at] if tag == "q" else o.at[:, at]
+        copies.start(tag + name, ref, ref, device, sent, got)
+
+    def pack_step(tag, s):
+        for way, mark in WAYS:
+            sent, got = line.sent(way, s), line.got(way, s)
+            pack_send(tag, f"z{mark}{s}", line.block(way, s), line.device(way), sent, got)
+
+    def pack_take(tag, s):
+        for way, mark in WAYS:
+            copies.arrived(f"{tag}z{mark}{s}")
+        if s < 2:
+            pack_step(tag, s + 1)
+        for way, mark in WAYS:
+            got = line.got(way, s)
+            pack_send(tag, f"y{mark}{s}", line.block(way, s + 1), other, got, got)
+
+    def pack_wait(tag):
+        for name in ["o"] + [mark + str(s) for s in range(3) for _, mark in WAYS]:
+            copies.arrived(tag + "y" + name)
+
+    pack_step("q", 0)
+    pack_send("q", "yo", z, other)
+    d.send_own()
 
     for copy in loads[4:]:
         copy.wait()
@@ -569,7 +634,7 @@
         cast_into(gu_f.at[m], gu_b.at[m])
     cast_into(d_f, d_b, 64)
 
-    pieces = 2
+    pieces = PIECES
 
     def owned(m, k, p):
         if m == 2:
@@ -621,33 +686,30 @@
     rms_into(x, gain[0:1, :], one)
     keep(one, one_out)
 
-    pack_arrived("z1")
-    pack_send("y1", 1, other)
-    pack_arrived("z2")
-    pack_send("z3", 2, at_z(z, r, t, 1))
-    pack_send("y2", 2, other)
-    d.take_z(1)
-    d.take_z(2)
-    pack_arrived("z3")
-    pack_send("y3", 3, other)
-    pump(2)
-    for k in range(4):
-        pack_arrived(f"y{k}")
-    for m in range(3):
-        for p in range(pieces):
-            forward(m, 0, p)
+    pack_take("q", 0)
+    pack_take("q", 1)
+    pack_step("o", 0)
+    for _ in range(WINDOW):
+        issue()
+    pack_take("q", 2)
+    pack_send("o", "yo", z, other)
+    d.send_z(0)
+    pack_wait("q")
+    for p in range(pieces):
+        forward(0, 0, p)
     keep(qkv, qkv_out)
-    keep(o, o_out)
 
     kv[:, kv_cols] = dot(one[...], qkv[:, width:]).astype(bf)
     for name, peer in (("k1", core_peer), ("k2", x_peer), ("k3", far_peer)):
         copies.start(name, kv.at[:, kv_cols], kv.at[:, kv_cols], peer)
     q[...] = dot(one[...], qkv[:, :width]).astype(bf)
     keep(q, q_out)
-    pump(1)
+    pack_take("o", 0)
     for name in ("k1", "k2", "k3"):
         copies.arrived(name)
     keep(kv, kv_out)
+    for p in range(pieces):
+        forward(1, 0, p)
     length = lengths[0]
     step = 128
     for h in range(width // HD):
@@ -655,8 +717,18 @@
             at, upto = pl.ds(i * step, step), pl.ds(0, (i + 1) * step)
             probs = probabilities(q[at, h * HD : (h + 1) * HD], kv[upto, :HD], length, i * step)
             mixed[at, h * HD : (h + 1) * HD] = dot(probs.astype(bf), kv[upto, HD:]).astype(bf)
-        pump(1)
+        if h == 0:
+            pack_take("o", 1)
+            pump(1)
     keep(mixed, mixed_out)
+    pack_take("o", 2)
+    pump(1)
+    pack_wait("o")
+    keep(o, o_out)
+    for p in range(pieces):
+        forward(2, 0, p)
+    d.take_z(0)
+    d.take_own()
 
     def part_of(j, store_part):
         at = pl.ds(pl.multiple_of((t ^ j) * quarter, quarter), quarter)
@@ -672,8 +744,7 @@
     part_of(3, into_part(0))
     part_of(1, into_part(1))
     copies.start("a1", part, recvc, core_peer)
-    d.take_x(0)
-    d.take_z(3)
+    pump(1)
     copies.arrived("a1")
 
     def into_x(value, cols):
@@ -686,6 +757,8 @@
         resid[:, cols] = value + recvc[1, :, cols].astype(fl)
 
     part_of(0, into_resid)
+    d.take_z(1)
+    d.take_x(0)
     copies.arrived("a2")
     first_row = t * quarter
 
@@ -701,24 +774,22 @@
     keep(resid, resid_out)
     keep(nt_own, nt_out.at[block_rows(z, t, quarter)])
     n = TokenGather(copies, nt_own, nt_out, "n")
-    n.send_z()
-    n.send_x(0)
+    n.send_z(0)
+    n.send_own()
+    pump(2)
+    d.take_z(2)
     d.take_x(1)
-    pump(WINDOW, more=False)
+    n.take_z(0)
+    n.take_own()
+    pump(2)
+    d.take_x(2)
     n.take_z(1)
-    n.take_z(2)
-    for _ in range(WINDOW):
-        issue()
-    d.take_x(2)
-    d.take_x(3)
     n.take_x(0)
     pump(2)
-    n.take_z(3)
+    n.take_z(2)
     n.take_x(1)
     pump(2)
     n.take_x(2)
-    pump(2)
-    n.take_x(3)
     pump(len(flows))
     n.finish()
     d.finish()
@@ -737,7 +808,7 @@
     quarter = dy.shape[0]
     kvt = wkv.shape[1] // 4
     ff = wd.shape[0] // ZN
-    n = 7 + 14 + 42 + 3 + 2 + 2 * TokenGather.count
+    n = 7 + 26 + 21 * PIECES + 3 + 2 + 2 * TokenGather.count
     shape = jax.ShapeDtypeStruct
     return pl.pallas_call(
         forward_kernel,
@@ -782,7 +853,7 @@
             pltpu.SemaphoreType.DMA((n,)),
             pltpu.SemaphoreType.DMA((n,)),
             pltpu.SemaphoreType.DMA((7,)),
-            pltpu.SemaphoreType.DMA((16,)),
+            pltpu.SemaphoreType.DMA((10 + 3 * PIECES,)),
         ],
         compiler_params=remote_params(1),
         name="forward_part",
@@ -796,7 +867,7 @@
 def ff_kernel(
     nt_hbm, dy_hbm, gu_hbm, d_hbm, hgu_hbm, sums,
     wgu, wd, dots, xin, hgu, sendc, recvc, sendx, kept, recvx, recvz,
-    send, recv, load, wload, store,
+    send, recv, zsend, zrecv, load, wload, store,
 ):
     z, r, t = position()
     x, c = t // 2, t % 2
@@ -811,12 +882,12 @@
     for copy in loads:
         copy.start()
 
-    order = (3, 2, 1, 0)
+    order = (3 * (1 - z // 2), (2 + 3 * z) % 5, 1 + z % 2, z)
 
     def rows(i, b):
         cc = c if i % 2 else c ^ 1
         xx = x if b else x ^ 1
-        return block_rows(z ^ order[i // 2], xx * 2 + cc, quarter)
+        return block_rows(order[i // 2], xx * 2 + cc, quarter)
 
     def fetch(i):
         out = []
@@ -837,30 +908,63 @@
     for copy in loads:
         copy.wait()
 
-    def take_x(s):
-        copies.arrived(f"x{s}")
-        if s == 1:
-            copies.arrived("z0")
-        if s == 3:
-            copies.arrived("z2")
-            copies.arrived("z1")
+    middle = lax.min(lax.rem(z, 3), 1)
+
+    def add_x(s, a, places):
+        for place in places:
+            pltpu.make_async_copy(recvz.at[place, a], recvz.at[place, a], zrecv.at[place, a]).wait()
 
         @pl.loop(0, model // tile)
         def _(n):
             cols = pl.ds(pl.multiple_of(n * tile, tile), tile)
-            for a in range(2):
-                total = kept[s, a, :, cols].astype(fl) + recvx[s, a, :, cols].astype(fl)
-                if s == 1:
-                    total += recvz[0, a, :, cols].astype(fl)
-                if s == 3:
-                    total += recvz[1, a, :, cols].astype(fl) + recvz[2, a, :, cols].astype(fl)
-                    sums[a, :, cols] = total
-                else:
-                    recvx[s, a, :, cols] = total.astype(bf)
-
-        if s < 3:
-            copies.start(f"z{s}", recvx.at[s], recvz.at[s], at_z(z, r, t, 2 if s == 1 else 1))
-
+            total = kept[s, a, :, cols].astype(fl) + recvx[s, a, :, cols].astype(fl)
+            for place in places:
+                total += recvz[place, a, :, cols].astype(fl)
+            if s == 3:
+                sums[a, :, cols] = total
+            else:
+                recvx[s, a, :, cols] = total.astype(bf)
+
+    def z_copy(s, a):
+        up = (order[s] + 4 - z) // 5
+        there = z + 2 * up - 1
+        same = 1 - lax.min((order[s] - there) * (order[s] - there), 1)
+        place = order[s] + (1 - up) * same * (4 - order[s])
+        return pltpu.make_async_remote_copy(
+            src_ref=recvx.at[s, a],
+            dst_ref=recvz.at[place, a],
+            send_sem=zsend.at[s, a],
+            recv_sem=zrecv.at[place, a],
+            device_id=(there * 2 + r, t),
+            device_id_type=MESH,
+        )
+
+    def take_x(s, a, mid):
+        copies.arrived(f"x{s}{a}")
+        if s == 3:
+            low = lax.min(z, 1)
+            add_x(s, a, (z, 4) if mid else (low * z + (1 - low) * 4,))
+        else:
+            add_x(s, a, (order[s],) if mid else ())
+            z_copy(s, a).start()
+
+    def take(at_ends, at_middle):
+        for mid, parts in enumerate((at_ends, at_middle)):
+            if parts:
+
+                @pl.when(middle == mid)
+                def _():
+                    for s, a in parts:
+                        take_x(s, a, bool(mid))
+
+    rest = [(s, a) for s in range(4) for a in range(2)]
+    takes = {
+        3: (rest[:1], ()),
+        4: (rest[1:2], ()),
+        5: (rest[2:3], rest[:1]),
+        6: (rest[3:4], rest[1:2]),
+        7: (rest[4:], rest[2:]),
+    }
     stores = {}
     for i in range(8):
         s, own = i // 2, i % 2
@@ -905,7 +1009,8 @@
         if own:
             copies.arrived(f"c{s}")
             if s >= 2:
-                copies.left(f"x{s - 2}")
+                for a in range(2):
+                    copies.left(f"x{s - 2}{a}")
         elif s >= 1:
             copies.left(f"c{s - 1}")
 
@@ -923,19 +1028,20 @@
                     sendc[a, :, cols] = part.astype(bf)
 
         if own:
-            copies.start(f"x{s}", sendx.at[s % 2], recvx.at[s], (me, t ^ 2))
-            if s >= 2:
-                take_x(s - 2)
+            for a in range(2):
+                copies.start(f"x{s}{a}", sendx.at[s % 2, a], recvx.at[s, a], (me, t ^ 2))
         else:
             copies.start(f"c{s}", sendc, recvc.at[s % 2], (me, t ^ 1))
-
-    take_x(2)
-    take_x(3)
+        if i in takes:
+            take(*takes[i])
+
     for i in (6, 7):
         for copy in stores[i]:
             copy.wait()
-    for name in ("c3", "x2", "x3", "z0", "z1", "z2"):
-        copies.left(name)
+    for s in range(3):
+        for a in range(2):
+            z_copy(s, a).wait_send()
+    copies.all_left()
 
 
 def feed_forward(nt, dy, wgu, wd):
@@ -961,9 +1067,11 @@
             pltpu.VMEM((2, 2, quarter, model), bf),
             pltpu.VMEM((4, 2, quarter, model), bf),
             pltpu.VMEM((4, 2, quarter, model), bf),
-            pltpu.VMEM((3, 2, quarter, model), bf),
-            pltpu.SemaphoreType.DMA((11,)),
-            pltpu.SemaphoreType.DMA((11,)),
+            pltpu.VMEM((5, 2, quarter, model), bf),
+            pltpu.SemaphoreType.DMA((12,)),
+            pltpu.SemaphoreType.DMA((12,)),
+            pltpu.SemaphoreType.DMA((3, 2)),
+            pltpu.SemaphoreType.DMA((5, 2)),
             pltpu.SemaphoreType.DMA((2, 2, 2)),
             pltpu.SemaphoreType.DMA((3,)),
             pltpu.SemaphoreType.DMA((2, 3, 2)),
@@ -980,7 +1088,7 @@
     a, d_resid, out_own, gacc, grecv, gmine, grecv_t,
     gp, dkv_send, dkv_recv, dkv_x, dkv_rx, part, precv, sendx, recvx,
     pk_send, po_send, pk_recv, po_recv, pk_own, po_own, pk_z, po_z,
-    send, recv, load, local,
+    send, recv, zsend, zrecv, load, local,
 ):
     z, r, t = position()
     me = z * 2 + r
@@ -1044,19 +1152,57 @@
     copies.start("bx", out_own, block_out.at[own_rows(0)], x_peer)
     copies.start("bc", out_own, block_out.at[own_rows(0)], core_peer)
 
-    zorder = (1, 3, 2, 0)
+    end = 1 - lax.min(lax.rem(z, 3), 1)
+    zorder = (3 - 2 * end, 2 + end, 1 + end, 0)
 
     def send_y(i):
+        for m in range(2):
+            copies.start(f"y{i}{m}", lambda m=m: sendy_gu.at[i, m], lambda m=m: recvy_gu.at[i, m], other)
+        copies.start(f"y{i}2", lambda: sendy_d.at[i], lambda: recvy_d.at[i], other)
+
+    flows = [(i, m) for i in range(3) for m in range(3)]
+    taken = [0]
+
+    def own_of(i, m):
+        return own_d.at[i] if m == 2 else own_gu.at[i, m]
+
+    def add_y(i, m):
+        mine, theirs = own_of(i, m), (recvy_d.at[i] if m == 2 else recvy_gu.at[i, m])
+
+        @pl.loop(0, mine.shape[0] // 64)
+        def _(n):
+            at = pl.ds(pl.multiple_of(n * 64, 64), 64)
+            mine[at] = (mine[at].astype(fl) + theirs[at].astype(fl)).astype(bf)
+
+    def place(m):
+        cols = pl.ds(pl.multiple_of(z * ff, ff), ff)
+        return d_out.at[cols] if m == 2 else gu_out.at[m, :, cols]
+
+    def z_copy(i, m):
         k = zorder[i]
-        for m in range(2):
-            copies.start(f"y{k}{m}", lambda m=m: sendy_gu.at[i, m], lambda m=m: recvy_gu.at[i, m], other)
-        copies.start(f"y{k}2", lambda: sendy_d.at[i], lambda: recvy_d.at[i], other)
-
-    def feed_forward_grads(hgu, lhs):
+        return pltpu.make_async_remote_copy(
+            src_ref=own_of(i, m),
+            dst_ref=place(m),
+            send_sem=zsend.at[i, m],
+            recv_sem=zrecv.at[k - 1, m],
+            device_id=at_z(z, r, t, k),
+            device_id_type=MESH,
+        )
+
+    def pump(n):
+        for _ in range(n):
+            if taken[0] < len(flows):
+                i, m = flows[taken[0]]
+                copies.arrived(f"y{i}{m}")
+                add_y(i, m)
+                z_copy(i, m).start()
+                taken[0] += 1
+
+    def feed_forward_grads(first, last, pumps, hgu, lhs):
         loads = [pltpu.make_async_copy(hgu_hbm.at[m], hgu.at[m], load.at[m]) for m in range(3)]
 
         def fetch(i):
-            cols = d_block(zorder[i % 4], 0 if i >= 4 else 1)
+            cols = d_block(zorder[i // 2], 1 - i % 2)
             made = []
             for n, src in enumerate((nt_hbm, dy_hbm)):
                 copy = pltpu.make_async_copy(src.at[:, cols], lhs.at[i % 2, n], load.at[3 + 2 * (i % 2) + n])
@@ -1064,17 +1210,17 @@
                 made.append(copy)
             return made
 
-        pending = fetch(0)
+        pending = fetch(first)
         for m in (1, 2, 0):
             loads[m].start()
-        for i in range(8):
+        for i in range(first, last):
             for copy in pending:
                 copy.wait()
-            if i < 7:
+            if i < last - 1:
                 pending = fetch(i + 1)
-            to_gu, to_d = (sendy_gu, sendy_d) if i < 4 else (own_gu, own_d)
+            to_gu, to_d = (own_gu, own_d) if i % 2 else (sendy_gu, sendy_d)
             for m, (h, n) in enumerate(((1, 0), (2, 0), (0, 1))):
-                if i == 0:
+                if i == first:
                     loads[h].wait()
 
                 @pl.loop(0, ff // 512)
@@ -1082,53 +1228,24 @@
                     cols = pl.ds(pl.multiple_of(c * 512, 512), 512)
                     grad = inner_rows(lhs[i % 2, n], hgu[h, :, cols])
                     if m < 2:
-                        to_gu[i % 4, m, :, cols] = grad.astype(bf)
+                        to_gu[i // 2, m, :, cols] = grad.astype(bf)
                     else:
-                        to_d[i % 4, cols, :] = grad.T.astype(bf)
-
-            if i < 3:
-                send_y(i)
+                        to_d[i // 2, cols, :] = grad.T.astype(bf)
+
+            if i % 2 == 0:
+                send_y(i // 2)
+            pump(pumps[i - first])
 
     group = nt_hbm.shape[0]
-    pl.run_scoped(
-        feed_forward_grads, pltpu.VMEM((3, group, ff), bf), pltpu.VMEM((2, 2, group, rows), bf)
-    )
-
-    flows = [(i, m) for i in range(3) for m in range(3)]
-    taken = [0]
-
-    def own_of(i, m):
-        return own_d.at[i] if m == 2 else own_gu.at[i, m]
-
-    def add_y(i, m):
-        mine, theirs = own_of(i, m), (recvy_d.at[i] if m == 2 else recvy_gu.at[i, m])
-
-        @pl.loop(0, mine.shape[0] // 64)
-        def _(n):
-            at = pl.ds(pl.multiple_of(n * 64, 64), 64)
-            mine[at] = (mine[at].astype(fl) + theirs[at].astype(fl)).astype(bf)
-
-    def place(m):
-        cols = pl.ds(pl.multiple_of(z * ff, ff), ff)
-        return d_out.at[cols] if m == 2 else gu_out.at[m, :, cols]
-
-    at_zs = [at_z(z, r, t, k) for k in range(4)]
-
-    def pump(n):
-        for _ in range(n):
-            if taken[0] < len(flows):
-                i, m = flows[taken[0]]
-                k = zorder[i]
-                copies.arrived(f"y{k}{m}")
-                add_y(i, m)
-                copies.start(f"z{k}{m}", lambda i=i, m=m: own_of(i, m), lambda m=m: place(m), at_zs[k])
-                taken[0] += 1
-
-    pump(3)
+    scope = (pltpu.VMEM((3, group, ff), bf), pltpu.VMEM((2, 2, group, rows), bf))
+    pl.run_scoped(functools.partial(feed_forward_grads, 0, 4, (0, 1, 0, 1)), *scope)
+
     copies.arrived("ax")
     copies.start("af", a.at[own_rows(2)], a.at[own_rows(2)], core_peer)
     copies.arrived("bx")
     copies.start("bf", block_out.at[own_rows(2)], block_out.at[own_rows(2)], core_peer)
+
+    pack_order = (1, 3, 2, 0)
 
     def attention(q, kv, mixed, qkv, o, one, dm, dkv):
         loads = [
@@ -1193,11 +1310,11 @@
             to_k[...] = inner_rows(one[:, cols], gp[...]).astype(to_k.dtype)
             to_o[...] = inner_rows(mixed[...], a[:, cols]).astype(to_o.dtype)
 
-        for i, k in enumerate(zorder):
+        for i, k in enumerate(pack_order):
             pack_grads(k, 1, pk_send.at[i], po_send.at[i])
             copies.start(f"yp{k}", lambda i=i: pk_send.at[i], lambda i=i: pk_recv.at[i], other)
             copies.start(f"yo{k}", lambda i=i: po_send.at[i], lambda i=i: po_recv.at[i], other)
-        send_y(3)
+        pump(1)
 
         copies.arrived("pc")
 
@@ -1215,7 +1332,7 @@
             in_own[:, cols] = value + precv[1, :, cols].astype(fl)
 
         part_of(0, into_own)
-        for i, k in enumerate(zorder):
+        for i, k in enumerate(pack_order):
             pack_grads(k, 0, pk_own.at[i], po_own.at[i])
         copies.arrived("px")
 
@@ -1230,6 +1347,7 @@
         pltpu.VMEM((slot, width), bf),
         pltpu.VMEM((slot, 2 * HD), fl),
     )
+    pl.run_scoped(functools.partial(feed_forward_grads, 4, 8, (1, 0, 0, 0)), *scope)
 
     @pl.loop(0, quarter // 16)
     def _(i):
@@ -1247,20 +1365,34 @@
                 copies.start(
                     f"g{k}{j}", gacc.at[:, d_block(k, j)], grecv.at[2 * k + j], ((z ^ k) * 2 + (r ^ j), t)
                 )
-    pump(9)
+    pump(6 - taken[0])
 
     def add_pack(i):
-        k = zorder[i]
+        k = pack_order[i]
         copies.arrived(f"yp{k}")
         copies.arrived(f"yo{k}")
         for mine, theirs in ((pk_own.at[i], pk_recv.at[i]), (po_own.at[i], po_recv.at[i])):
             mine[...] = (mine[...].astype(fl) + theirs[...].astype(fl)).astype(mine.dtype)
 
-    for i in range(3):
-        add_pack(i)
-        k = zorder[i]
-        copies.start(f"zp{k}", pk_own.at[i], pk_z.at[i], at_z(z, r, t, k))
-        copies.start(f"zo{k}", po_own.at[i], po_z.at[i], at_z(z, r, t, k))
+    def send_pack(i, k):
+        copies.start(f"zp{i}", pk_own.at[i], pk_z.at[i], at_z(z, r, t, k))
+        copies.start(f"zo{i}", po_own.at[i], po_z.at[i], at_z(z, r, t, k))
+
+    def pack_arrived(i):
+        copies.arrived(f"zp{i}")
+        copies.arrived(f"zo{i}")
+
+    add_pack(0)
+    send_pack(0, 1)
+    add_pack(1)
+    send_pack(1, 1)
+    add_pack(2)
+    pump(1)
+    pack_arrived(1)
+    pk_own[2] = (pk_own[2].astype(fl) + pk_z[1].astype(fl)).astype(bf)
+    po_own[2] = (po_own[2].astype(fl) + po_z[1].astype(fl)).astype(bf)
+    send_pack(2, 2)
+    pump(9)
     add_pack(3)
     total = gacc[:, d_block(0)]
     for k in range(4):
@@ -1275,15 +1407,13 @@
     copies.start("if", input_out.at[own_rows(2)], input_out.at[own_rows(2)], core_peer)
 
     for m in range(3):
-        copies.arrived(f"y0{m}")
+        copies.arrived(f"y3{m}")
         add_y(3, m)
         keep(own_of(3, m), place(m))
-    for i in range(3):
-        copies.arrived(f"zp{zorder[i]}")
-        copies.arrived(f"zo{zorder[i]}")
     pk_sum = pk_own[3].astype(fl)
     po_sum = po_own[3].astype(fl)
-    for i in range(3):
+    for i in (0, 2):
+        pack_arrived(i)
         pk_sum += pk_z[i].astype(fl)
         po_sum += po_z[i].astype(fl)
     qkv_grad[...] = pk_sum
@@ -1299,9 +1429,10 @@
     gains_out[...] = total
     for name in ("ic", "if", "bc", "bf", "kg1", "kg2", "kg3"):
         copies.arrived(name)
-    for i in range(3):
-        for m in range(3):
-            copies.arrived(f"z{zorder[i]}{m}")
+    for m in range(3):
+        for i in range(3):
+            pltpu.make_async_copy(place(m), place(m), zrecv.at[i, m]).wait()
+            z_copy(i, m).wait_send()
     copies.all_left()
     for copy in locals_:
         copy.wait()
@@ -1314,7 +1445,7 @@
     quarter = resid.shape[0]
     slot, width = q.shape
     kvt = qkv.shape[1] - width
-    n = 2 + 2 + 2 + 12 + 9 + 2 + 8 + 2 + 3 + 7 + 6 + 3 + 3
+    n = 2 + 2 + 2 + 12 + 2 + 8 + 2 + 3 + 7 + 6 + 3 + 3
     shape = jax.ShapeDtypeStruct
     buf = pltpu.VMEM
     return pl.pallas_call(
@@ -1347,6 +1478,8 @@
             buf((3, rows, width + kvt), bf), buf((3, width, rows), bf),
             pltpu.SemaphoreType.DMA((n,)),
             pltpu.SemaphoreType.DMA((n,)),
+            pltpu.SemaphoreType.DMA((3, 3)),
+            pltpu.SemaphoreType.DMA((3, 3)),
             pltpu.SemaphoreType.DMA((7,)),
             pltpu.SemaphoreType.DMA((8,)),
         ],

time: 786 us -> 669 us (0.85)
  Pallas kernels: 725 us -> 607 us
    pallas_call x1, Pallas kernels: 268 us -> 217 us  [backward_part(): pl.pallas_call(backward_kernel, out_shape=(shape((2, rows, ZN * ff), bf),...]
    pallas_call x1, Pallas kernels: 175 us -> 140 us  [feed_forward(): pl.pallas_call(ff_kernel, out_shape=(jax.ShapeDtypeStruct((3, group, ff),...]
    pallas_call x1, Pallas kernels: 281 us -> 250 us  [forward_part(): pl.pallas_call(forward_kernel, out_shape=(shape((2, model, ff), bf), shap...]
where the time goes in v4:
time: 669 us; the launch traced here: 660 us
  Pallas kernels  607 us (91%)
  other arithmetic  44 us (7%)
  local copies, waits for them, and re-layouts  7.05 us (1%)
    pallas_call x1, Pallas kernels, forward_part(): pl.pallas_call(forward_kernel, out_shape=(shape((2, model, ff), bf), shap...  250 us
    pallas_call x1, Pallas kernels, backward_part(): pl.pallas_call(backward_kernel, out_shape=(shape((2, rows, ZN * ff), bf),...  217 us
    pallas_call x1, Pallas kernels, feed_forward(): pl.pallas_call(ff_kernel, out_shape=(jax.ShapeDtypeStruct((3, group, ff),...  140 us
    mul x6, other arithmetic, adamw(): -learn_rate  40.2 us

profile of v4, /device:TPU:0, one launch (start us, length us, event | category | flops | bytes accessed | tf_op | source)
XLA Modules:
  0.0 660.3 jit_solution(15753026016867373538)
XLA Ops:
  1.3 2.5 dynamic-slice_select_fusion
  3.9 0.7 convert_element_type.12
  4.6 0.6 pad_convert_fusion.gains
  5.2 250.2 %forward_part.1 = (bf16[2,2048,1024]{2,1,0:T(8,128)(2,1)}, bf16[1024,2048]{1,0:T(8,128)(2,1)}, bf16[2560,2048]{1,0:T(8,128)(2,1)}, bf16[2560,2048]{1,0:T(8,128)(...) custom-call(s32[1]{0:T(128)} %copy.51.lengths, ...), custom_call_target="tpu_custom_call" | custom-call | tf_op jit(solution)/shard_map/forward_part/pallas_call | solution.py:813
  255.4 140.4 %feed_forward.1 = (bf16[3,2560,1024]{2,1,0:T(8,128)(2,1)}, f32[2,160,2048]{2,1,0:T(8,128)}) custom-call(bf16[2560,2048]{1,0:T(8,128)(2,1)} %get-tuple-element.48.nt_hbm, bf16[2560,2048]{1,0:T(8,128)(2,1)} %get-tuple-element.49.dy_hbm, bf16[2,2048,1024]{2,1,0:T(8,128)(2,1)} %get-tuple-element.50.gu_hbm, bf16[1024,2048]{1,0:T(8,128)(2,1)} %get-tuple-element.51.d_hbm), custom_call_target="tpu_custom_call" | custom-call | tf_op jit(solution)/shard_map/feed_forward/pallas_call | solution.py:1051
  395.8 216.7 %backward_part.1 = (bf16[2,256,4096]{2,1,0:T(8,128)(2,1)}, bf16[4096,256]{1,0:T(8,128)(2,1)}, f32[256,640]{1,0:T(8,128)}, f32[256,512]{1,0:T(8,128)}, f32[512,25...) custom-call(s32[1]{0:T(128)} %copy.51.lengths, ...), custom_call_target="tpu_custom_call" | custom-call | tf_op jit(solution)/shard_map/backward_part/pallas_call | solution.py:1451
  612.5 22.7 %add_multiply_fusion = (f32[2,256,4096]{2,1,0:T(8,128)}, f32[2,256,4096]{2,1,0:T(8,128)}, f32[2,256,4096]{2,1,0:T(8,128)}, f32[2,256,4096]{2,1,0:T(8,128)}) fusion(f32[2,256,4096]{2,1,0:T(8,128)} %wgu.1, f32[2,256,4096]{2,1,0:T(8,128)} %param.39, f32[2,256,4096]{2,1,0:T(8,128)} %param.33, bf16[2,256,4096]{2,1,0:T(8,128)(2,1)} %get-tuple-element.67), kind=kLoop, calls=%fused_computation.2 | loop fusion | flops 27262976 | bytes 62914560 | tf_op jit(solution)/shard_map/mul | solution.py:87
  635.2 0.0 copy-start.4
  635.3 0.0 copy-start.10
  635.3 0.0 copy-start.11
  635.3 11.5 %add_multiply_fusion.1 = (f32[4096,256]{1,0:T(8,128)}, f32[4096,256]{1,0:T(8,128)}, f32[4096,256]{1,0:T(8,128)}, f32[4096,256]{1,0:T(8,128)}) fusion(f32[4096,256]{1,0:T(8,128)} %wd.1, f32[4096,256]{1,0:T(8,128)} %param.40, f32[4096,256]{1,0:T(8,128)} %param.34, bf16[4096,256]{1,0:T(8,128)(2,1)S(1)} %copy-done.5), kind=kLoop, calls=%fused_computation.6 | loop fusion | flops 13631488 | bytes 31457280 | tf_op jit(solution)/shard_map/mul | solution.py:87
  646.8 0.0 copy-start.6
  646.8 0.0 copy-start.7
  646.8 0.0 copy-start.1
  646.9 1.5 add_multiply_fusion.4
  648.4 0.1 copy-done.6
  648.5 0.5 copy-done.7
  649.1 1.4 add_multiply_fusion.3
  650.5 1.3 add_multiply_fusion.2
  651.8 1.8 add_multiply_fusion.5
  653.6 2.4 copy.52
  655.9 2.4 copy.53
  658.3 0.8 copy.54
  659.1 0.8 copy.55
  (35 shorter events, 0.1 us)
Async XLA Ops:
  612.5 22.7 %copy-start.5 = (bf16[4096,256]{1,0:T(8,128)(2,1)S(1)}, bf16[4096,256]{1,0:T(8,128)(2,1)}, u32[]{:S(2)}) copy-start(bf16[4096,256]{1,0:T(8,128)(2,1)} %get-tuple-element.68) | copy-start | bytes 6291460
  635.2 18.3 %slice-start.2 = ((s8[5242880]{0:T(1024)(128)(4,1)}), s8[4194304]{0:T(1024)(128)(4,1)S(1)}, s32[]{:S(2)}) async-start(s8[5242880]{0:T(1024)(128)(4,1)} %bitcast.4), calls=%async_computation.2 | async-start | bytes 8388608
  635.2 11.6 %copy-start.4 = (f32[256,512]{1,0:T(8,128)S(1)}, f32[256,512]{1,0:T(8,128)}, u32[]{:S(2)}) copy-start(f32[256,512]{1,0:T(8,128)} %wq.1) | copy-start | bytes 1572868
  635.3 11.6 %copy-start.10 = (f32[256,512]{1,0:T(8,128)S(1)}, f32[256,512]{1,0:T(8,128)}, u32[]{:S(2)}) copy-start(f32[256,512]{1,0:T(8,128)} %param.36) | copy-start | bytes 1572868
  635.3 11.6 %copy-start.11 = (f32[256,512]{1,0:T(8,128)S(1)}, f32[256,512]{1,0:T(8,128)}, u32[]{:S(2)}) copy-start(f32[256,512]{1,0:T(8,128)} %param.30) | copy-start | bytes 1572868
  635.3 11.6 %copy-start.12 = (f32[256,640]{1,0:T(8,128)S(1)}, f32[256,640]{1,0:T(8,128)}, u32[]{:S(2)}) copy-start(f32[256,640]{1,0:T(8,128)} %get-tuple-element.64) | copy-start | bytes 1966084
  635.3 18.3 %slice-start.3 = ((s8[5242880]{0:T(1024)(128)(4,1)}), s8[1048576]{0:T(1024)(128)(4,1)S(1)}, s32[]{:S(2)}) async-start(s8[5242880]{0:T(1024)(128)(4,1)} %bitcast.4), calls=%async_computation.3 | async-start | bytes 2097152
  646.8 1.6 copy-start
  646.8 1.6 copy-start.3
  646.8 1.8 copy-start.6
  646.8 2.3 copy-start.7
  646.8 3.6 copy-start.1
  646.8 3.6 copy-start.2
  646.8 3.6 copy-start.8
  646.8 3.6 copy-start.9
  648.4 3.4 copy-start.13
  648.4 3.4 copy-start.14
  648.4 3.4 copy-start.15
  650.4 5.5 slice-start
  653.6 2.4 slice-start.1

commit v5 on v4

--- a/solution.py
+++ b/solution.py
@@ -530,17 +530,17 @@
 
 
 def forward_kernel(
-    lengths, wq, wkv, wo, wgu, wd, gains, tokens, dy,
+    lengths, wq, wkv, wo, wgu, wd, gains, tokens, cotangent,
     gu_out, d_out, dy_out, nt_out, resid_out, one_out, q_out, kv_out, mixed_out, qkv_out, o_out, gain_out,
     wq_f, wkv_f, wo_f, gu_f, d_f, gu_b, d_b, x, qkv, o, gain, one, q, kv, mixed,
-    part, recvc, sendx, recvx, resid, nt_own,
+    part, recvc, sendx, recvx, resid, nt_own, dy,
     send, recv, load, store,
 ):
     z, r, t = position()
     me = z * 2 + r
     rows = wq.shape[0]
     slot, model = tokens.shape
-    quarter = dy.shape[0]
+    quarter = slot // 4
     width = wq.shape[1]
     kvt = qkv.shape[1] - width
     ff = d_out.shape[0]
@@ -559,6 +559,9 @@
         pltpu.make_async_copy(wkv.at[:, kv_cols], wkv_f, load.at[1]),
         pltpu.make_async_copy(wo, wo_f, load.at[2]),
         pltpu.make_async_copy(gains, gain.at[:, d_block(0)], load.at[3]),
+        pltpu.make_async_copy(
+            cotangent.at[pl.ds(pl.multiple_of(t * quarter, quarter), quarter)], dy, load.at[7]
+        ),
         pltpu.make_async_copy(tokens, x, load.at[4]),
         pltpu.make_async_copy(wgu, gu_f, load.at[5]),
         pltpu.make_async_copy(wd, d_f, load.at[6]),
@@ -572,9 +575,17 @@
         copy.start()
         stores.append(copy)
 
+    for copy in loads[:5]:
+        copy.wait()
+    length = lengths[0]
+
+    @pl.loop(0, quarter // 16)
+    def _(i):
+        at = pl.ds(pl.multiple_of(i * 16, 16), 16)
+        row = t * quarter + i * 16 + lax.broadcasted_iota(jnp.int32, (16, model), 0)
+        dy[at] = jnp.where(row < length, dy[at].astype(fl), 0.0).astype(bf)
+
     keep(dy, dy_out.at[block_rows(z, t, quarter)])
-    for copy in loads[:4]:
-        copy.wait()
 
     @pl.loop(0, rows // 16)
     def _(i):
@@ -628,7 +639,7 @@
     pack_send("q", "yo", z, other)
     d.send_own()
 
-    for copy in loads[4:]:
+    for copy in loads[5:]:
         copy.wait()
     for m in range(2):
         cast_into(gu_f.at[m], gu_b.at[m])
@@ -710,7 +721,6 @@
     keep(kv, kv_out)
     for p in range(pieces):
         forward(1, 0, p)
-    length = lengths[0]
     step = 128
     for h in range(width // HD):
         for i in range(slot // step):
@@ -802,10 +812,10 @@
         copy.wait()
 
 
-def forward_part(lengths, wq, wkv, wo, wgu, wd, gains, tokens, dy):
+def forward_part(lengths, wq, wkv, wo, wgu, wd, gains, tokens, cotangent):
     rows, width = wq.shape
     slot, model = tokens.shape
-    quarter = dy.shape[0]
+    quarter = slot // 4
     kvt = wkv.shape[1] // 4
     ff = wd.shape[0] // ZN
     n = 7 + 26 + 21 * PIECES + 3 + 2 + 2 * TokenGather.count
@@ -850,37 +860,60 @@
             pltpu.VMEM((quarter, model), bf),
             pltpu.VMEM((quarter, model), fl),
             pltpu.VMEM((quarter, model), bf),
+            pltpu.VMEM((quarter, model), bf),
             pltpu.SemaphoreType.DMA((n,)),
             pltpu.SemaphoreType.DMA((n,)),
-            pltpu.SemaphoreType.DMA((7,)),
+            pltpu.SemaphoreType.DMA((8,)),
             pltpu.SemaphoreType.DMA((10 + 3 * PIECES,)),
         ],
         compiler_params=remote_params(1),
         name="forward_part",
-    )(lengths, wq, wkv, wo, wgu, wd, gains, tokens, dy)
+    )(lengths, wq, wkv, wo, wgu, wd, gains, tokens, cotangent)
 
 
 ROOT = 0.7978845608028654
 CUBE = 0.044715
 
 
+def z_order(z):
+    end = 1 - lax.min(lax.rem(z, 3), 1)
+    return (3 - 2 * end, 2 + end, 1 + end, 0)
+
+
+def block_grads(h, lhs, to_gu, to_d):
+    for m, (which, n) in enumerate(((1, 0), (2, 0), (0, 1))):
+
+        @pl.loop(0, h.shape[2] // 512)
+        def _(c):
+            cols = pl.ds(pl.multiple_of(c * 512, 512), 512)
+            grad = inner_rows(lhs[n], h[which, :, cols])
+            if m < 2:
+                to_gu[m, :, cols] = grad.astype(bf)
+            else:
+                to_d[cols, :] = grad.T.astype(bf)
+
+
+def add_to(mine, theirs):
+    @pl.loop(0, mine.shape[0] // 64)
+    def _(n):
+        at = pl.ds(pl.multiple_of(n * 64, 64), 64)
+        mine[at] = (mine[at].astype(fl) + theirs[at].astype(fl)).astype(bf)
+
+
 def ff_kernel(
-    nt_hbm, dy_hbm, gu_hbm, d_hbm, hgu_hbm, sums,
-    wgu, wd, dots, xin, hgu, sendc, recvc, sendx, kept, recvx, recvz,
+    nt_hbm, dy_hbm, gu_hbm, d_hbm, hgu_hbm, sums, first_gu, first_d,
+    sendc, recvc, sendx, kept, recvx, recvz, recvy_gu, recvy_d,
     send, recv, zsend, zrecv, load, wload, store,
 ):
     z, r, t = position()
     x, c = t // 2, t % 2
     me = z * 2 + r
     quarter = sums.shape[1]
-    ff, model = wd.shape
+    other, x_peer, core_peer = (z * 2 + (r ^ 1), t), (me, t ^ 2), (me, t ^ 1)
+    drows = recvy_d.shape[1]
+    ff, model = d_hbm.shape
     tile = 256
     wide = 1024
-
-    loads = [pltpu.make_async_copy(gu_hbm.at[m], wgu.at[m], wload.at[m]) for m in range(2)]
-    loads.append(pltpu.make_async_copy(d_hbm, wd, wload.at[2]))
-    for copy in loads:
-        copy.start()
 
     order = (3 * (1 - z // 2), (2 + 3 * z) % 5, 1 + z % 2, z)
 
@@ -889,24 +922,8 @@
         xx = x if b else x ^ 1
         return block_rows(order[i // 2], xx * 2 + cc, quarter)
 
-    def fetch(i):
-        out = []
-        for a, src in enumerate((nt_hbm, dy_hbm)):
-            for b in range(2):
-                copy = pltpu.make_async_copy(
-                    src.at[rows(i, b)],
-                    xin.at[i % 2, a, pl.ds(b * quarter, quarter)],
-                    load.at[i % 2, a, b],
-                )
-                copy.start()
-                out.append(copy)
-        return out
-
-    pending = fetch(0)
-    greet(partners_of(z, r, t, zs=(1, 2), y=False))
+    greet(partners_of(z, r, t, zs=(1, 2)))
     copies = Copies(send, recv)
-    for copy in loads:
-        copy.wait()
 
     middle = lax.min(lax.rem(z, 3), 1)
 
@@ -963,81 +980,173 @@
         4: (rest[1:2], ()),
         5: (rest[2:3], rest[:1]),
         6: (rest[3:4], rest[1:2]),
-        7: (rest[4:], rest[2:]),
+        7: (rest[4:5], rest[2:4]),
     }
-    stores = {}
-    for i in range(8):
-        s, own = i // 2, i % 2
+    def layers(wgu, wd, dots, xin, hgu):
+        loads = [pltpu.make_async_copy(gu_hbm.at[m], wgu.at[m], wload.at[m]) for m in range(2)]
+        loads.append(pltpu.make_async_copy(d_hbm, wd, wload.at[2]))
+        for copy in loads:
+            copy.start()
+
+
+        def fetch(i):
+            out = []
+            for a, src in enumerate((nt_hbm, dy_hbm)):
+                for b in range(2):
+                    copy = pltpu.make_async_copy(
+                        src.at[rows(i, b)],
+                        xin.at[i % 2, a, pl.ds(b * quarter, quarter)],
+                        load.at[i % 2, a, b],
+                    )
+                    copy.start()
+                    out.append(copy)
+            return out
+
+        pending = fetch(0)
+        for copy in loads:
+            copy.wait()
+
+
+        stores = {}
+        for i in range(8):
+            s, own = i // 2, i % 2
+            for copy in pending:
+                copy.wait()
+            if i < 7:
+                pending = fetch(i + 1)
+            if i >= 2:
+                for copy in stores[i - 2]:
+                    copy.wait()
+
+            dots[0] = dot(xin[i % 2, 0], wgu[0])
+            dots[1] = dot(xin[i % 2, 0], wgu[1])
+            dots[2] = times_trans(xin[i % 2, 1], wd[...])
+
+            @pl.loop(0, 2 * quarter // 16)
+            def _(n):
+                at = pl.ds(pl.multiple_of(n * 16, 16), 16)
+                for half in range(0, ff, 512):
+                    cols = slice(half, half + 512)
+                    gate, upper, dh = dots[0, at, cols], dots[1, at, cols], dots[2, at, cols]
+                    square = gate * gate
+                    bend = jnp.tanh(ROOT * gate * (1.0 + CUBE * square))
+                    share = 0.5 * (1.0 + bend)
+                    gelu = gate * share
+                    slope = share + 0.5 * gate * (1.0 - bend * bend) * (ROOT * (1.0 + 3.0 * CUBE * square))
+                    hgu[i % 2, 0, at, cols] = (gelu * upper).astype(bf)
+                    hgu[i % 2, 1, at, cols] = (dh * upper * slope).astype(bf)
+                    hgu[i % 2, 2, at, cols] = (dh * gelu).astype(bf)
+
+            stores[i] = []
+            for m in range(3):
+                for b in range(2):
+                    copy = pltpu.make_async_copy(
+                        hgu.at[i % 2, m, pl.ds(b * quarter, quarter)],
+                        hgu_hbm.at[m, rows(i, b)],
+                        store.at[i % 2, m, b],
+                    )
+                    copy.start()
+                    stores[i].append(copy)
+
+            if own:
+                copies.arrived(f"c{s}")
+                if s >= 2:
+                    for a in range(2):
+                        copies.left(f"x{s - 2}{a}")
+            elif s >= 1:
+                copies.left(f"c{s - 1}")
+
+            @pl.loop(0, model // wide)
+            def _(n):
+                cols = pl.ds(pl.multiple_of(n * wide, wide), wide)
+                out = dot(hgu[i % 2, 0], wd[:, cols])
+                back = times_trans(hgu[i % 2, 1], wgu[0, cols]) + times_trans(hgu[i % 2, 2], wgu[1, cols])
+                for a, part in enumerate((out, back)):
+                    if own:
+                        total = part + recvc[s % 2, a, :, cols].astype(fl)
+                        sendx[s % 2, a, :, cols] = total[:quarter].astype(bf)
+                        kept[s, a, :, cols] = total[quarter:].astype(bf)
+                    else:
+                        sendc[a, :, cols] = part.astype(bf)
+
+            if own:
+                for a in range(2):
+                    copies.start(
+                        f"x{s}{a}",
+                        lambda s=s, a=a: sendx.at[s % 2, a],
+                        lambda s=s, a=a: recvx.at[s, a],
+                        x_peer,
+                    )
+            else:
+                copies.start(f"c{s}", lambda: sendc, lambda s=s: recvc.at[s % 2], core_peer)
+            if i in takes:
+                take(*takes[i])
+
+        for i in (6, 7):
+            for copy in stores[i]:
+                copy.wait()
+
+    pl.run_scoped(
+        layers,
+        pltpu.VMEM((2, model, ff), bf),
+        pltpu.VMEM((ff, model), bf),
+        pltpu.VMEM((3, 2 * quarter, ff), fl),
+        pltpu.VMEM((2, 2, 2 * quarter, model), bf),
+        pltpu.VMEM((2, 3, 2 * quarter, ff), bf),
+    )
+
+    first = z_order(z)[0]
+
+    def first_grads(h, lhs, to_gu, to_d, own_gu, own_d):
+        loads = [pltpu.make_async_copy(hgu_hbm.at[m], h.at[m], wload.at[m]) for m in range(3)]
+
+        def fetch(j):
+            block = pl.multiple_of(((z ^ first) * 2 + (r ^ j)) * drows, drows)
+            made = []
+            for n, src in enumerate((nt_hbm, dy_hbm)):
+                copy = pltpu.make_async_copy(src.at[:, pl.ds(block, drows)], lhs.at[n], load.at[0, 0, n])
+                copy.start()
+                made.append(copy)
+            return made
+
+        pending = fetch(1)
+        for m in (1, 2, 0):
+            loads[m].start()
+        for m in (1, 2, 0):
+            loads[m].wait()
         for copy in pending:
             copy.wait()
-        if i < 7:
-            pending = fetch(i + 1)
-        if i >= 2:
-            for copy in stores[i - 2]:
-                copy.wait()
-
-        dots[0] = dot(xin[i % 2, 0], wgu[0])
-        dots[1] = dot(xin[i % 2, 0], wgu[1])
-        dots[2] = times_trans(xin[i % 2, 1], wd[...])
-
-        @pl.loop(0, 2 * quarter // 16)
-        def _(n):
-            at = pl.ds(pl.multiple_of(n * 16, 16), 16)
-            for half in range(0, ff, 512):
-                cols = slice(half, half + 512)
-                gate, upper, dh = dots[0, at, cols], dots[1, at, cols], dots[2, at, cols]
-                square = gate * gate
-                bend = jnp.tanh(ROOT * gate * (1.0 + CUBE * square))
-                share = 0.5 * (1.0 + bend)
-                gelu = gate * share
-                slope = share + 0.5 * gate * (1.0 - bend * bend) * (ROOT * (1.0 + 3.0 * CUBE * square))
-                hgu[i % 2, 0, at, cols] = (gelu * upper).astype(bf)
-                hgu[i % 2, 1, at, cols] = (dh * upper * slope).astype(bf)
-                hgu[i % 2, 2, at, cols] = (dh * gelu).astype(bf)
-
-        stores[i] = []
+        block_grads(h, lhs, to_gu, to_d)
+        for m in range(2):
+            copies.start(f"y{m}", lambda m=m: to_gu.at[m], lambda m=m: recvy_gu.at[m], other)
+        copies.start("y2", lambda: to_d, lambda: recvy_d, other)
+        pending = fetch(0)
+        take(rest[5:6], rest[4:6])
+        for copy in pending:
+            copy.wait()
+        block_grads(h, lhs, own_gu, own_d)
+        take(rest[6:], rest[6:])
         for m in range(3):
-            for b in range(2):
-                copy = pltpu.make_async_copy(
-                    hgu.at[i % 2, m, pl.ds(b * quarter, quarter)],
-                    hgu_hbm.at[m, rows(i, b)],
-                    store.at[i % 2, m, b],
-                )
-                copy.start()
-                stores[i].append(copy)
-
-        if own:
-            copies.arrived(f"c{s}")
-            if s >= 2:
-                for a in range(2):
-                    copies.left(f"x{s - 2}{a}")
-        elif s >= 1:
-            copies.left(f"c{s - 1}")
-
-        @pl.loop(0, model // wide)
-        def _(n):
-            cols = pl.ds(pl.multiple_of(n * wide, wide), wide)
-            out = dot(hgu[i % 2, 0], wd[:, cols])
-            back = times_trans(hgu[i % 2, 1], wgu[0, cols]) + times_trans(hgu[i % 2, 2], wgu[1, cols])
-            for a, part in enumerate((out, back)):
-                if own:
-                    total = part + recvc[s % 2, a, :, cols].astype(fl)
-                    sendx[s % 2, a, :, cols] = total[:quarter].astype(bf)
-                    kept[s, a, :, cols] = total[quarter:].astype(bf)
-                else:
-                    sendc[a, :, cols] = part.astype(bf)
-
-        if own:
-            for a in range(2):
-                copies.start(f"x{s}{a}", sendx.at[s % 2, a], recvx.at[s, a], (me, t ^ 2))
-        else:
-            copies.start(f"c{s}", sendc, recvc.at[s % 2], (me, t ^ 1))
-        if i in takes:
-            take(*takes[i])
-
-    for i in (6, 7):
-        for copy in stores[i]:
-            copy.wait()
+            copies.arrived(f"y{m}")
+            mine, theirs = (own_d, recvy_d) if m == 2 else (own_gu.at[m], recvy_gu.at[m])
+            add_to(mine, theirs)
+            copy = pltpu.make_async_copy(mine, first_d if m == 2 else first_gu.at[m], wload.at[m])
+            copy.start()
+        for m in range(3):
+            mine = own_d if m == 2 else own_gu.at[m]
+            pltpu.make_async_copy(mine, first_d if m == 2 else first_gu.at[m], wload.at[m]).wait()
+            copies.left(f"y{m}")
+
+    group = nt_hbm.shape[0]
+    pl.run_scoped(
+        first_grads,
+        pltpu.VMEM((3, group, ff), bf),
+        pltpu.VMEM((2, group, drows), bf),
+        pltpu.VMEM((2, drows, ff), bf),
+        pltpu.VMEM((ff, drows), bf),
+        pltpu.VMEM((2, drows, ff), bf),
+        pltpu.VMEM((ff, drows), bf),
+    )
     for s in range(3):
         for a in range(2):
             z_copy(s, a).wait_send()
@@ -1048,28 +1157,28 @@
     group, model = nt.shape
     ff = wd.shape[0]
     quarter = group // 16
+    rows = model // 8
     return pl.pallas_call(
         ff_kernel,
         out_shape=(
             jax.ShapeDtypeStruct((3, group, ff), bf),
             jax.ShapeDtypeStruct((2, quarter, model), fl),
+            jax.ShapeDtypeStruct((2, rows, ff), bf),
+            jax.ShapeDtypeStruct((ff, rows), bf),
         ),
         in_specs=[ANY] * 4,
-        out_specs=(ANY, VMEM),
+        out_specs=(ANY, VMEM, ANY, ANY),
         scratch_shapes=[
-            pltpu.VMEM((2, model, ff), bf),
-            pltpu.VMEM((ff, model), bf),
-            pltpu.VMEM((3, 2 * quarter, ff), fl),
-            pltpu.VMEM((2, 2, 2 * quarter, model), bf),
-            pltpu.VMEM((2, 3, 2 * quarter, ff), bf),
             pltpu.VMEM((2, 2 * quarter, model), bf),
             pltpu.VMEM((2, 2, 2 * quarter, model), bf),
             pltpu.VMEM((2, 2, quarter, model), bf),
             pltpu.VMEM((4, 2, quarter, model), bf),
             pltpu.VMEM((4, 2, quarter, model), bf),
             pltpu.VMEM((5, 2, quarter, model), bf),
-            pltpu.SemaphoreType.DMA((12,)),
-            pltpu.SemaphoreType.DMA((12,)),
+            pltpu.VMEM((2, rows, ff), bf),
+            pltpu.VMEM((ff, rows), bf),
+            pltpu.SemaphoreType.DMA((15,)),
+            pltpu.SemaphoreType.DMA((15,)),
             pltpu.SemaphoreType.DMA((3, 2)),
             pltpu.SemaphoreType.DMA((5, 2)),
             pltpu.SemaphoreType.DMA((2, 2, 2)),
@@ -1082,10 +1191,10 @@
 
 
 def backward_kernel(
-    lengths, nt_hbm, dy_hbm, hgu_hbm, sums, resid, dy_own, x_own, gain, one_hbm, q_hbm, kv_hbm, mixed_hbm, qkv_hbm, o_hbm,
+    lengths, nt_hbm, dy_hbm, hgu_hbm, sums, first_gu, first_d, tokens, resid, gain, one_hbm, q_hbm, kv_hbm, mixed_hbm, qkv_hbm, o_hbm,
     gu_out, d_out, qkv_grad, kv_grad, o_grad, block_out, input_out, gains_out,
     sendy_gu, sendy_d, recvy_gu, recvy_d, own_gu, own_d,
-    a, d_resid, out_own, gacc, grecv, gmine, grecv_t,
+    a, dy_own, x_own, d_resid, out_own, gacc, grecv, gmine, grecv_t,
     gp, dkv_send, dkv_recv, dkv_x, dkv_rx, part, precv, sendx, recvx,
     pk_send, po_send, pk_recv, po_recv, pk_own, po_own, pk_z, po_z,
     send, recv, zsend, zrecv, load, local,
@@ -1110,6 +1219,8 @@
     loads = [
         pltpu.make_async_copy(sums.at[1], d_resid, load.at[0]),
         pltpu.make_async_copy(sums.at[0], out_own, load.at[1]),
+        pltpu.make_async_copy(dy_hbm.at[block_rows(z, t, quarter)], dy_own, load.at[2]),
+        pltpu.make_async_copy(tokens.at[own_rows(0)], x_own, load.at[3]),
     ]
     for copy in loads:
         copy.start()
@@ -1152,27 +1263,23 @@
     copies.start("bx", out_own, block_out.at[own_rows(0)], x_peer)
     copies.start("bc", out_own, block_out.at[own_rows(0)], core_peer)
 
-    end = 1 - lax.min(lax.rem(z, 3), 1)
-    zorder = (3 - 2 * end, 2 + end, 1 + end, 0)
+    zorder = z_order(z)
 
     def send_y(i):
         for m in range(2):
-            copies.start(f"y{i}{m}", lambda m=m: sendy_gu.at[i, m], lambda m=m: recvy_gu.at[i, m], other)
-        copies.start(f"y{i}2", lambda: sendy_d.at[i], lambda: recvy_d.at[i], other)
-
-    flows = [(i, m) for i in range(3) for m in range(3)]
+            copies.start(f"y{i}{m}", lambda m=m: sendy_gu.at[i - 1, m], lambda m=m: recvy_gu.at[i - 1, m], other)
+        copies.start(f"y{i}2", lambda: sendy_d.at[i - 1], lambda: recvy_d.at[i - 1], other)
+
+    flows = [(i, m) for i in (1, 2) for m in range(3)]
     taken = [0]
 
     def own_of(i, m):
-        return own_d.at[i] if m == 2 else own_gu.at[i, m]
+        if i == 0:
+            return first_d if m == 2 else first_gu.at[m]
+        return own_d.at[i - 1] if m == 2 else own_gu.at[i - 1, m]
 
     def add_y(i, m):
-        mine, theirs = own_of(i, m), (recvy_d.at[i] if m == 2 else recvy_gu.at[i, m])
-
-        @pl.loop(0, mine.shape[0] // 64)
-        def _(n):
-            at = pl.ds(pl.multiple_of(n * 64, 64), 64)
-            mine[at] = (mine[at].astype(fl) + theirs[at].astype(fl)).astype(bf)
+        add_to(own_of(i, m), recvy_d.at[i - 1] if m == 2 else recvy_gu.at[i - 1, m])
 
     def place(m):
         cols = pl.ds(pl.multiple_of(z * ff, ff), ff)
@@ -1218,27 +1325,20 @@
                 copy.wait()
             if i < last - 1:
                 pending = fetch(i + 1)
+            if i == first:
+                for m in range(3):
+                    loads[m].wait()
             to_gu, to_d = (own_gu, own_d) if i % 2 else (sendy_gu, sendy_d)
-            for m, (h, n) in enumerate(((1, 0), (2, 0), (0, 1))):
-                if i == first:
-                    loads[h].wait()
-
-                @pl.loop(0, ff // 512)
-                def _(c):
-                    cols = pl.ds(pl.multiple_of(c * 512, 512), 512)
-                    grad = inner_rows(lhs[i % 2, n], hgu[h, :, cols])
-                    if m < 2:
-                        to_gu[i // 2, m, :, cols] = grad.astype(bf)
-                    else:
-                        to_d[i // 2, cols, :] = grad.T.astype(bf)
-
-            if i % 2 == 0:
+            block_grads(hgu, lhs.at[i % 2], to_gu.at[i // 2 - 1], to_d.at[i // 2 - 1])
+            if i in (2, 6):
                 send_y(i // 2)
             pump(pumps[i - first])
 
+    for m in range(3):
+        z_copy(0, m).start()
     group = nt_hbm.shape[0]
     scope = (pltpu.VMEM((3, group, ff), bf), pltpu.VMEM((2, 2, group, rows), bf))
-    pl.run_scoped(functools.partial(feed_forward_grads, 0, 4, (0, 1, 0, 1)), *scope)
+    pl.run_scoped(functools.partial(feed_forward_grads, 2, 5, (0, 1, 0)), *scope)
 
     copies.arrived("ax")
     copies.start("af", a.at[own_rows(2)], a.at[own_rows(2)], core_peer)
@@ -1246,6 +1346,29 @@
     copies.start("bf", block_out.at[own_rows(2)], block_out.at[own_rows(2)], core_peer)
 
     pack_order = (1, 3, 2, 0)
+    at_zs = [at_z(z, r, t, k) for k in range(4)]
+    packs = {"p": (pk_own, pk_recv, pk_z), "o": (po_own, po_recv, po_z)}
+
+    def add_pack(tag, i):
+        own, theirs, _ = packs[tag]
+        copies.arrived(f"y{tag}{i}")
+        own[i] = (own[i].astype(fl) + theirs[i].astype(fl)).astype(bf)
+
+    def send_pack(tag, i, k):
+        copies.start(f"z{tag}{i}", lambda: packs[tag][0].at[i], lambda: packs[tag][2].at[i], at_zs[k])
+
+    def pack_first(tag, i):
+        add_pack(tag, i)
+        send_pack(tag, i, 1)
+
+    def pack_second(tag):
+        own, _, came = packs[tag]
+        add_pack(tag, 2)
+        copies.arrived(f"z{tag}1")
+        own[2] = (own[2].astype(fl) + came[1].astype(fl)).astype(bf)
+        send_pack(tag, 2, 2)
+        add_pack(tag, 3)
+
 
     def attention(q, kv, mixed, qkv, o, one, dm, dkv):
         loads = [
@@ -1260,6 +1383,12 @@
         copies.arrived("af")
         for copy in loads:
             copy.wait()
+        for i, k in enumerate(pack_order):
+            po_send[i] = inner_rows(mixed[...], a[:, d_block(k, 1)]).astype(bf)
+            copies.start(f"yo{i}", lambda i=i: po_send.at[i], lambda i=i: po_recv.at[i], other)
+        send_y(2)
+        for i, k in enumerate(pack_order):
+            po_own[i] = inner_rows(mixed[...], a[:, d_block(k, 0)]).astype(bf)
         dm[...] = times_trans(a[...], o[...]).astype(bf)
         length = lengths[0]
         step = 128
@@ -1286,6 +1415,8 @@
         copies.arrived("kc")
         dkv_x[...] = (dkv[:, kv_cols(2)] + dkv_recv[1].astype(fl)).astype(bf)
         copies.start("kx", lambda: dkv_x, lambda: dkv_rx, x_peer)
+        pack_first("o", 0)
+        pack_first("o", 1)
         mine = dkv[:, kv_cols(0)] + dkv_recv[0].astype(fl)
         copies.arrived("kx")
         gp[:, width:] = (mine + dkv_rx[...].astype(fl)).astype(bf)
@@ -1305,16 +1436,9 @@
         part_of(1, into_part(1))
         copies.start("pc", lambda: part, lambda: precv, core_peer)
 
-        def pack_grads(k, j, to_k, to_o):
-            cols = d_block(k, j)
-            to_k[...] = inner_rows(one[:, cols], gp[...]).astype(to_k.dtype)
-            to_o[...] = inner_rows(mixed[...], a[:, cols]).astype(to_o.dtype)
-
         for i, k in enumerate(pack_order):
-            pack_grads(k, 1, pk_send.at[i], po_send.at[i])
-            copies.start(f"yp{k}", lambda i=i: pk_send.at[i], lambda i=i: pk_recv.at[i], other)
-            copies.start(f"yo{k}", lambda i=i: po_send.at[i], lambda i=i: po_recv.at[i], other)
-        pump(1)
+            pk_send[i] = inner_rows(one[:, d_block(k, 1)], gp[...]).astype(bf)
+            copies.start(f"yp{i}", lambda i=i: pk_send.at[i], lambda i=i: pk_recv.at[i], other)
 
         copies.arrived("pc")
 
@@ -1333,7 +1457,7 @@
 
         part_of(0, into_own)
         for i, k in enumerate(pack_order):
-            pack_grads(k, 0, pk_own.at[i], po_own.at[i])
+            pk_own[i] = inner_rows(one[:, d_block(k, 0)], gp[...]).astype(bf)
         copies.arrived("px")
 
     pl.run_scoped(
@@ -1347,7 +1471,7 @@
         pltpu.VMEM((slot, width), bf),
         pltpu.VMEM((slot, 2 * HD), fl),
     )
-    pl.run_scoped(functools.partial(feed_forward_grads, 4, 8, (1, 0, 0, 0)), *scope)
+    pl.run_scoped(functools.partial(feed_forward_grads, 5, 8, (1, 1, 1)), *scope)
 
     @pl.loop(0, quarter // 16)
     def _(i):
@@ -1365,35 +1489,12 @@
                 copies.start(
                     f"g{k}{j}", gacc.at[:, d_block(k, j)], grecv.at[2 * k + j], ((z ^ k) * 2 + (r ^ j), t)
                 )
-    pump(6 - taken[0])
-
-    def add_pack(i):
-        k = pack_order[i]
-        copies.arrived(f"yp{k}")
-        copies.arrived(f"yo{k}")
-        for mine, theirs in ((pk_own.at[i], pk_recv.at[i]), (po_own.at[i], po_recv.at[i])):
-            mine[...] = (mine[...].astype(fl) + theirs[...].astype(fl)).astype(mine.dtype)
-
-    def send_pack(i, k):
-        copies.start(f"zp{i}", pk_own.at[i], pk_z.at[i], at_z(z, r, t, k))
-        copies.start(f"zo{i}", po_own.at[i], po_z.at[i], at_z(z, r, t, k))
-
-    def pack_arrived(i):
-        copies.arrived(f"zp{i}")
-        copies.arrived(f"zo{i}")
-
-    add_pack(0)
-    send_pack(0, 1)
-    add_pack(1)
-    send_pack(1, 1)
-    add_pack(2)
-    pump(1)
-    pack_arrived(1)
-    pk_own[2] = (pk_own[2].astype(fl) + pk_z[1].astype(fl)).astype(bf)
-    po_own[2] = (po_own[2].astype(fl) + po_z[1].astype(fl)).astype(bf)
-    send_pack(2, 2)
-    pump(9)
-    add_pack(3)
+    pump(len(flows))
+
+    pack_second("o")
+    pack_first("p", 0)
+    pack_first("p", 1)
+    pack_second("p")
     total = gacc[:, d_block(0)]
     for k in range(4):
         for j in range(2):
@@ -1413,7 +1514,8 @@
     pk_sum = pk_own[3].astype(fl)
     po_sum = po_own[3].astype(fl)
     for i in (0, 2):
-        pack_arrived(i)
+        copies.arrived(f"zp{i}")
+        copies.arrived(f"zo{i}")
         pk_sum += pk_z[i].astype(fl)
         po_sum += po_z[i].astype(fl)
     qkv_grad[...] = pk_sum
@@ -1438,7 +1540,7 @@
         copy.wait()
 
 
-def backward_part(lengths, nt, dy, hgu, sums, resid, dy_own, x_own, gain, one, q, kv, mixed, qkv, o):
+def backward_part(lengths, nt, dy, hgu, sums, first_gu, first_d, tokens, resid, gain, one, q, kv, mixed, qkv, o):
     group, model = nt.shape
     ff = hgu.shape[2]
     rows = model // 8
@@ -1460,13 +1562,13 @@
             shape((slot, model), fl),
             shape((8, rows), fl),
         ),
-        in_specs=[pl.BlockSpec(memory_space=pltpu.SMEM)] + [ANY] * 4 + [VMEM] * 4 + [ANY] * 6,
+        in_specs=[pl.BlockSpec(memory_space=pltpu.SMEM)] + [ANY] * 7 + [VMEM] * 2 + [ANY] * 6,
         out_specs=(ANY, ANY, VMEM, VMEM, VMEM, ANY, ANY, VMEM),
         scratch_shapes=[
-            buf((4, 2, rows, ff), bf), buf((4, ff, rows), bf),
-            buf((4, 2, rows, ff), bf), buf((4, ff, rows), bf),
-            buf((4, 2, rows, ff), bf), buf((4, ff, rows), bf),
-            buf((slot, model), bf), buf((quarter, model), fl), buf((quarter, model), fl),
+            buf((3, 2, rows, ff), bf), buf((3, ff, rows), bf),
+            buf((3, 2, rows, ff), bf), buf((3, ff, rows), bf),
+            buf((3, 2, rows, ff), bf), buf((3, ff, rows), bf),
+            buf((slot, model), bf), buf((quarter, model), bf), buf((quarter, model), bf), buf((quarter, model), fl), buf((quarter, model), fl),
             buf((8, model), fl), buf((8, 8, rows), fl), buf((8, rows), fl), buf((4, 8, rows), fl),
             buf((slot, width + kvt), bf), buf((2, slot, kvt), bf), buf((2, slot, kvt), bf),
             buf((slot, kvt), bf), buf((slot, kvt), bf),
@@ -1485,7 +1587,7 @@
         ],
         compiler_params=remote_params(4),
         name="backward_part",
-    )(lengths, nt, dy, hgu, sums, resid, dy_own, x_own, gain, one, q, kv, mixed, qkv, o)
+    )(lengths, nt, dy, hgu, sums, first_gu, first_d, tokens, resid, gain, one, q, kv, mixed, qkv, o)
 
 
 def fast(
@@ -1511,24 +1613,16 @@
     second_down,
     second_gains,
 ):
-    t = lax.axis_index("tensor")
-    quarter = tokens.shape[0] // lax.axis_size("tensor")
-    length = lengths[0]
-
-    cot_own = lax.dynamic_slice_in_dim(cotangent, t * quarter, quarter, 0)
-    valid = (t * quarter + jnp.arange(quarter) < length)[:, None]
-    grad_own = jnp.where(valid, cot_own, jnp.zeros_like(cot_own))
     gains_low = jnp.pad(norm_gains.astype(bf).astype(fl), ((0, 6), (0, 0)))
     (
         gateup, down, dy, normed_two, resid, normed_one, query, keyval, mixed, qkv_w, output_w, gain_full,
-    ) = forward_part(lengths, w_query, w_keyval, w_output, w_gateup, w_down, gains_low, tokens, grad_own)
-    x_own = lax.dynamic_slice_in_dim(tokens, t * quarter, quarter, 0)
-
-    hgu, sums = feed_forward(normed_two, dy, gateup, down)
+    ) = forward_part(lengths, w_query, w_keyval, w_output, w_gateup, w_down, gains_low, tokens, cotangent)
+
+    hgu, sums, first_gu, first_d = feed_forward(normed_two, dy, gateup, down)
     (
         gateup_grad, down_grad, qkv_grad, keyval_shard, output_shard, block_output, input_grad, gains_grad,
     ) = backward_part(
-        lengths, normed_two, dy, hgu, sums, resid, grad_own, x_own, gain_full,
+        lengths, normed_two, dy, hgu, sums, first_gu, first_d, tokens, resid, gain_full,
         normed_one, query, keyval, mixed, qkv_w, output_w,
     )
     query_shard = qkv_grad[:, : w_query.shape[1]]

time: 669 us -> 659 us (0.985)
  the two profiles are of different devices: /device:TPU:0 before, /device:TPU:9 now
where the time goes in v5:
time: 659 us; the launch traced here: 651 us
  Pallas kernels  596 us (90%)
  other arithmetic  40.5 us (6%)
  local copies, waits for them, and re-layouts  12.7 us (2%)
    pallas_call x1, Pallas kernels, forward_part(): pl.pallas_call(forward_kernel, out_shape=(shape((2, model, ff), bf), shap...  231 us
    pallas_call x1, Pallas kernels, backward_part(): pl.pallas_call(backward_kernel, out_shape=(shape((2, rows, ZN * ff), bf),...  203 us
    pallas_call x1, Pallas kernels, feed_forward(): pl.pallas_call(ff_kernel, out_shape=(jax.ShapeDtypeStruct((3, group, ff),...  162 us
    mul x5, other arithmetic, adamw(): -learn_rate  39.2 us

profile of v5, /device:TPU:9, one launch (start us, length us, event | category | flops | bytes accessed | tf_op | source)
XLA Modules:
  0.0 650.7 jit_solution(8686778382967305637)
XLA Ops:
  1.3 0.7 convert_element_type.12
  2.0 0.6 pad_convert_fusion.gains
  2.6 230.8 %forward_part.1 = (bf16[2,2048,1024]{2,1,0:T(8,128)(2,1)}, bf16[1024,2048]{1,0:T(8,128)(2,1)}, bf16[2560,2048]{1,0:T(8,128)(2,1)}, bf16[2560,2048]{1,0:T(8,128)(...) custom-call(s32[1]{0:T(128)S(6)} %copy.51.lengths, ...), custom_call_target="tpu_custom_call" | custom-call | tf_op jit(solution)/shard_map/forward_part/pallas_call | solution.py:823
  233.4 161.7 %feed_forward.1 = (bf16[3,2560,1024]{2,1,0:T(8,128)(2,1)}, f32[2,160,2048]{2,1,0:T(8,128)}, bf16[2,256,1024]{2,1,0:T(8,128)(2,1)}, bf16[1024,256]{1,0:T(8,128)(2,1)}) custom-call(bf16[2560,2048]{1,0:T(8,128)(2,1)} %get-tuple-element.50.nt_hbm, bf16[2560,2048]{1,0:T(8,128)(2,1)} %get-tuple-element.51.dy_hbm, bf16[2,2048,1024]{2,1,0:T(8,128)(2,1)} %get-tuple-element.52.gu_hbm, ...), custom_call_target="tpu_custom_call" | custom-call | tf_op jit(solution)/shard_map/feed_forward/pallas_call | solution.py:1161
  395.1 203.2 %backward_part.1 = (bf16[2,256,4096]{2,1,0:T(8,128)(2,1)}, bf16[4096,256]{1,0:T(8,128)(2,1)}, f32[256,640]{1,0:T(8,128)}, f32[256,512]{1,0:T(8,128)}, f32[512,25...) custom-call(s32[1]{0:T(128)S(6)} %copy.51.lengths, ...), custom_call_target="tpu_custom_call" | custom-call | tf_op jit(solution)/shard_map/backward_part/pallas_call | solution.py:1553
  598.3 0.0 copy-start
  598.3 0.0 copy-start.3
  598.3 0.0 copy-start.4
  598.3 0.0 copy-start.5
  598.4 4.4 add_multiply_fusion.3
  602.8 0.0 copy-done.3
  602.8 1.3 add_multiply_fusion.2
  604.1 22.8 %add_multiply_fusion = (f32[2,256,4096]{2,1,0:T(8,128)}, f32[2,256,4096]{2,1,0:T(8,128)}, f32[2,256,4096]{2,1,0:T(8,128)}, f32[2,256,4096]{2,1,0:T(8,128)}) fusion(f32[2,256,4096]{2,1,0:T(8,128)} %wgu.1, f32[2,256,4096]{2,1,0:T(8,128)} %param.39, f32[2,256,4096]{2,1,0:T(8,128)} %param.33, bf16[2,256,4096]{2,1,0:T(8,128)(2,1)} %get-tuple-element.71), kind=kLoop, calls=%fused_computation.2 | loop fusion | flops 27262976 | bytes 62914560 | tf_op jit(solution)/shard_map/mul | solution.py:87
  626.9 0.0 copy-start.6
  626.9 0.0 copy-start.7
  626.9 0.0 copy-start.8
  626.9 9.4 %add_multiply_fusion.1 = (f32[4096,256]{1,0:T(8,128)}, f32[4096,256]{1,0:T(8,128)}, f32[4096,256]{1,0:T(8,128)}, f32[4096,256]{1,0:T(8,128)}) fusion(f32[4096,256]{1,0:T(8,128)} %wd.1, f32[4096,256]{1,0:T(8,128)} %param.40, f32[4096,256]{1,0:T(8,128)} %param.34, bf16[4096,256]{1,0:T(8,128)(2,1)S(1)} %copy-done.2), kind=kLoop, calls=%fused_computation.6 | loop fusion | flops 13631488 | bytes 31457280 | tf_op jit(solution)/shard_map/mul | solution.py:87
  636.3 0.0 copy-done.7
  636.3 0.0 copy-done.8
  636.3 1.3 add_multiply_fusion.5
  637.6 5.5 copy.52
  643.1 5.5 copy.53
  648.6 0.8 copy.54
  649.4 0.8 copy.55
  (8 shorter events, 0.0 us)
Async XLA Ops:
  598.3 4.5 copy-start
  598.3 4.4 copy-start.3
  598.3 4.4 copy-start.4
  598.3 4.4 copy-start.5
  604.1 22.8 %copy-start.2 = (bf16[4096,256]{1,0:T(8,128)(2,1)S(1)}, bf16[4096,256]{1,0:T(8,128)(2,1)}, u32[]{:S(2)}) copy-start(bf16[4096,256]{1,0:T(8,128)(2,1)} %get-tuple-element.72) | copy-start | bytes 6291460
  626.9 9.4 %copy-start.6 = (f32[2,256]{1,0:T(2,128)S(1)}, f32[2,256]{1,0:T(2,128)}, u32[]{:S(2)}) copy-start(f32[2,256]{1,0:T(2,128)} %param.29) | copy-start | bytes 6148
  626.9 9.4 %copy-start.7 = (f32[2,256]{1,0:T(2,128)S(1)}, f32[2,256]{1,0:T(2,128)}, u32[]{:S(2)}) copy-start(f32[2,256]{1,0:T(2,128)} %param.41) | copy-start | bytes 6148
  626.9 9.4 %copy-start.8 = (f32[2,256]{1,0:T(2,128)S(1)}, f32[2,256]{1,0:T(2,128)}, u32[]{:S(2)}) copy-start(f32[2,256]{1,0:T(2,128)} %param.35) | copy-start | bytes 6148
  643.1 5.5 copy-start.1

commit v6 on v5

--- a/solution.py
+++ b/solution.py
@@ -699,12 +699,12 @@
 
     pack_take("q", 0)
     pack_take("q", 1)
+    d.send_z(0)
     pack_step("o", 0)
     for _ in range(WINDOW):
         issue()
     pack_take("q", 2)
     pack_send("o", "yo", z, other)
-    d.send_z(0)
     pack_wait("q")
     for p in range(pieces):
         forward(0, 0, p)
@@ -980,7 +980,6 @@
         4: (rest[1:2], ()),
         5: (rest[2:3], rest[:1]),
         6: (rest[3:4], rest[1:2]),
-        7: (rest[4:5], rest[2:4]),
     }
     def layers(wgu, wd, dots, xin, hgu):
         loads = [pltpu.make_async_copy(gu_hbm.at[m], wgu.at[m], wload.at[m]) for m in range(2)]
@@ -1003,8 +1002,6 @@
             return out
 
         pending = fetch(0)
-        for copy in loads:
-            copy.wait()
 
 
         stores = {}
@@ -1018,8 +1015,14 @@
                 for copy in stores[i - 2]:
                     copy.wait()
 
+            if i == 0:
+                loads[0].wait()
             dots[0] = dot(xin[i % 2, 0], wgu[0])
+            if i == 0:
+                loads[1].wait()
             dots[1] = dot(xin[i % 2, 0], wgu[1])
+            if i == 0:
+                loads[2].wait()
             dots[2] = times_trans(xin[i % 2, 1], wd[...])
 
             @pl.loop(0, 2 * quarter // 16)
@@ -1112,6 +1115,7 @@
         pending = fetch(1)
         for m in (1, 2, 0):
             loads[m].start()
+        take(rest[4:5], rest[2:4])
         for m in (1, 2, 0):
             loads[m].wait()
         for copy in pending:
@@ -1216,18 +1220,18 @@
     def own_rows(j):
         return pl.ds(pl.multiple_of((t ^ j) * quarter, quarter), quarter)
 
-    loads = [
-        pltpu.make_async_copy(sums.at[1], d_resid, load.at[0]),
-        pltpu.make_async_copy(sums.at[0], out_own, load.at[1]),
-        pltpu.make_async_copy(dy_hbm.at[block_rows(z, t, quarter)], dy_own, load.at[2]),
-        pltpu.make_async_copy(tokens.at[own_rows(0)], x_own, load.at[3]),
+    first_loads = [
+        pltpu.make_async_copy(sums.at[1], d_resid, load.at[7]),
+        pltpu.make_async_copy(sums.at[0], out_own, load.at[8]),
+        pltpu.make_async_copy(dy_hbm.at[block_rows(z, t, quarter)], dy_own, load.at[9]),
+        pltpu.make_async_copy(tokens.at[own_rows(0)], x_own, load.at[10]),
     ]
-    for copy in loads:
+    for copy in first_loads:
         copy.start()
     greet(partners_of(z, r, t, zs=(1, 2, 3)) + [far_peer] + [((z ^ k) * 2 + (r ^ 1), t) for k in (1, 2, 3)])
     copies = Copies(send, recv)
     locals_ = []
-    counter = list(range(8))
+    counter = list(range(7))
 
     def keep(src, dst):
         copy = pltpu.make_async_copy(src, dst, local.at[counter.pop(0)])
@@ -1243,25 +1247,7 @@
         return inverse * (inner - scaled * jnp.mean(inner * scaled, axis=-1, keepdims=True))
 
     gacc[...] = jnp.zeros_like(gacc)
-    for copy in loads:
-        copy.wait()
-
-    @pl.loop(0, quarter // 16)
-    def _(i):
-        at = pl.ds(pl.multiple_of(i * 16, 16), 16)
-        mine = pl.ds(pl.multiple_of(t * quarter + i * 16, 16), 16)
-        v = resid[at]
-        total = dy_own[at].astype(fl) + norm_back(v, d_resid[at], 1)
-        d_resid[at] = total
-        a[mine] = total.astype(bf)
-        out_own[at] += v
-
-    copies.start("ax", a.at[own_rows(0)], a.at[own_rows(0)], x_peer)
-    copies.start("ac", a.at[own_rows(0)], a.at[own_rows(0)], core_peer)
-    keep(out_own, block_out.at[own_rows(0)])
     in_own = out_own
-    copies.start("bx", out_own, block_out.at[own_rows(0)], x_peer)
-    copies.start("bc", out_own, block_out.at[own_rows(0)], core_peer)
 
     zorder = z_order(z)
 
@@ -1305,6 +1291,29 @@
                 z_copy(i, m).start()
                 taken[0] += 1
 
+    def block_copy():
+        return pltpu.make_async_copy(out_own, block_out.at[own_rows(0)], local.at[7])
+
+    def second_norm():
+        for copy in first_loads:
+            copy.wait()
+
+        @pl.loop(0, quarter // 16)
+        def _(i):
+            at = pl.ds(pl.multiple_of(i * 16, 16), 16)
+            mine = pl.ds(pl.multiple_of(t * quarter + i * 16, 16), 16)
+            v = resid[at]
+            total = dy_own[at].astype(fl) + norm_back(v, d_resid[at], 1)
+            d_resid[at] = total
+            a[mine] = total.astype(bf)
+            out_own[at] += v
+
+        copies.start("ax", lambda: a.at[own_rows(0)], lambda: a.at[own_rows(0)], x_peer)
+        copies.start("ac", lambda: a.at[own_rows(0)], lambda: a.at[own_rows(0)], core_peer)
+        block_copy().start()
+        copies.start("bx", lambda: out_own, lambda: block_out.at[own_rows(0)], x_peer)
+        copies.start("bc", lambda: out_own, lambda: block_out.at[own_rows(0)], core_peer)
+
     def feed_forward_grads(first, last, pumps, hgu, lhs):
         loads = [pltpu.make_async_copy(hgu_hbm.at[m], hgu.at[m], load.at[m]) for m in range(3)]
 
@@ -1320,6 +1329,8 @@
         pending = fetch(first)
         for m in (1, 2, 0):
             loads[m].start()
+        if first == 2:
+            second_norm()
         for i in range(first, last):
             for copy in pending:
                 copy.wait()
@@ -1450,7 +1461,7 @@
 
         copies.left("bx")
         copies.left("bc")
-        locals_.pop(0).wait()
+        block_copy().wait()
 
         def into_own(value, cols):
             in_own[:, cols] = value + precv[1, :, cols].astype(fl)
@@ -1582,7 +1593,7 @@
             pltpu.SemaphoreType.DMA((n,)),
             pltpu.SemaphoreType.DMA((3, 3)),
             pltpu.SemaphoreType.DMA((3, 3)),
-            pltpu.SemaphoreType.DMA((7,)),
+            pltpu.SemaphoreType.DMA((11,)),
             pltpu.SemaphoreType.DMA((8,)),
         ],
         compiler_params=remote_params(4),

time: 659 us -> 653 us (level)
  no operation moved by 1% of the time
where the time goes in v6:
time: 653 us; the launch traced here: 645 us
  Pallas kernels  590 us (90%)
  other arithmetic  40.5 us (6%)
  local copies, waits for them, and re-layouts  12.7 us (2%)
    pallas_call x1, Pallas kernels, forward_part(): pl.pallas_call(forward_kernel, out_shape=(shape((2, model, ff), bf), shap...  226 us
    pallas_call x1, Pallas kernels, backward_part(): pl.pallas_call(backward_kernel, out_shape=(shape((2, rows, ZN * ff), bf),...  199 us
    pallas_call x1, Pallas kernels, feed_forward(): pl.pallas_call(ff_kernel, out_shape=(jax.ShapeDtypeStruct((3, group, ff),...  165 us
    mul x5, other arithmetic, adamw(): -learn_rate  39.2 us

profile of v6, /device:TPU:9, one launch (start us, length us, event | category | flops | bytes accessed | tf_op | source)
XLA Modules:
  0.0 644.5 jit_solution(16904588880144142113)
XLA Ops:
  1.3 0.7 convert_element_type.12
  2.0 0.6 pad_convert_fusion.gains
  2.6 225.6 %forward_part.1 = (bf16[2,2048,1024]{2,1,0:T(8,128)(2,1)}, bf16[1024,2048]{1,0:T(8,128)(2,1)}, bf16[2560,2048]{1,0:T(8,128)(2,1)}, bf16[2560,2048]{1,0:T(8,128)(...) custom-call(s32[1]{0:T(128)S(6)} %copy.51.lengths, ...), custom_call_target="tpu_custom_call" | custom-call | tf_op jit(solution)/shard_map/forward_part/pallas_call | solution.py:823
  228.2 164.9 %feed_forward.1 = (bf16[3,2560,1024]{2,1,0:T(8,128)(2,1)}, f32[2,160,2048]{2,1,0:T(8,128)}, bf16[2,256,1024]{2,1,0:T(8,128)(2,1)}, bf16[1024,256]{1,0:T(8,128)(2,1)}) custom-call(bf16[2560,2048]{1,0:T(8,128)(2,1)} %get-tuple-element.50.nt_hbm, bf16[2560,2048]{1,0:T(8,128)(2,1)} %get-tuple-element.51.dy_hbm, bf16[2,2048,1024]{2,1,0:T(8,128)(2,1)} %get-tuple-element.52.gu_hbm, ...), custom_call_target="tpu_custom_call" | custom-call | tf_op jit(solution)/shard_map/feed_forward/pallas_call | solution.py:1165
  393.1 199.1 %backward_part.1 = (bf16[2,256,4096]{2,1,0:T(8,128)(2,1)}, bf16[4096,256]{1,0:T(8,128)(2,1)}, f32[256,640]{1,0:T(8,128)}, f32[256,512]{1,0:T(8,128)}, f32[512,25...) custom-call(s32[1]{0:T(128)S(6)} %copy.51.lengths, ...), custom_call_target="tpu_custom_call" | custom-call | tf_op jit(solution)/shard_map/backward_part/pallas_call | solution.py:1564
  592.1 0.0 copy-start
  592.1 0.0 copy-start.3
  592.2 0.0 copy-start.4
  592.2 0.0 copy-start.5
  592.2 4.4 add_multiply_fusion.3
  596.6 0.0 copy-done
  596.6 0.0 copy-done.3
  596.6 0.0 copy-done.4
  596.6 1.3 add_multiply_fusion.2
  597.9 22.8 %add_multiply_fusion = (f32[2,256,4096]{2,1,0:T(8,128)}, f32[2,256,4096]{2,1,0:T(8,128)}, f32[2,256,4096]{2,1,0:T(8,128)}, f32[2,256,4096]{2,1,0:T(8,128)}) fusion(f32[2,256,4096]{2,1,0:T(8,128)} %wgu.1, f32[2,256,4096]{2,1,0:T(8,128)} %param.39, f32[2,256,4096]{2,1,0:T(8,128)} %param.33, bf16[2,256,4096]{2,1,0:T(8,128)(2,1)} %get-tuple-element.71), kind=kLoop, calls=%fused_computation.2 | loop fusion | flops 27262976 | bytes 62914560 | tf_op jit(solution)/shard_map/mul | solution.py:87
  620.7 0.0 copy-start.6
  620.7 0.0 copy-start.7
  620.7 0.0 copy-start.8
  620.7 9.4 %add_multiply_fusion.1 = (f32[4096,256]{1,0:T(8,128)}, f32[4096,256]{1,0:T(8,128)}, f32[4096,256]{1,0:T(8,128)}, f32[4096,256]{1,0:T(8,128)}) fusion(f32[4096,256]{1,0:T(8,128)} %wd.1, f32[4096,256]{1,0:T(8,128)} %param.40, f32[4096,256]{1,0:T(8,128)} %param.34, bf16[4096,256]{1,0:T(8,128)(2,1)S(1)} %copy-done.2), kind=kLoop, calls=%fused_computation.6 | loop fusion | flops 13631488 | bytes 31457280 | tf_op jit(solution)/shard_map/mul | solution.py:87
  630.1 1.3 add_multiply_fusion.5
  631.4 5.5 copy.52
  636.9 5.5 copy.53
  642.5 0.8 copy.54
  643.3 0.8 copy.55
  (8 shorter events, 0.0 us)
Async XLA Ops:
  592.1 4.5 copy-start
  592.1 4.4 copy-start.3
  592.2 4.4 copy-start.4
  592.2 4.4 copy-start.5
  597.9 22.8 %copy-start.2 = (bf16[4096,256]{1,0:T(8,128)(2,1)S(1)}, bf16[4096,256]{1,0:T(8,128)(2,1)}, u32[]{:S(2)}) copy-start(bf16[4096,256]{1,0:T(8,128)(2,1)} %get-tuple-element.72) | copy-start | bytes 6291460
  620.7 9.4 %copy-start.6 = (f32[2,256]{1,0:T(2,128)S(1)}, f32[2,256]{1,0:T(2,128)}, u32[]{:S(2)}) copy-start(f32[2,256]{1,0:T(2,128)} %param.29) | copy-start | bytes 6148
  620.7 9.4 %copy-start.7 = (f32[2,256]{1,0:T(2,128)S(1)}, f32[2,256]{1,0:T(2,128)}, u32[]{:S(2)}) copy-start(f32[2,256]{1,0:T(2,128)} %param.41) | copy-start | bytes 6148
  620.7 9.4 %copy-start.8 = (f32[2,256]{1,0:T(2,128)S(1)}, f32[2,256]{1,0:T(2,128)}, u32[]{:S(2)}) copy-start(f32[2,256]{1,0:T(2,128)} %param.35) | copy-start | bytes 6148
  636.9 5.5 copy-start.1

commit v7 on v6

--- a/solution.py
+++ b/solution.py
@@ -1503,9 +1503,10 @@
     pump(len(flows))
 
     pack_second("o")
-    pack_first("p", 0)
-    pack_first("p", 1)
-    pack_second("p")
+    for i, k in enumerate((1, 3, 2)):
+        add_pack("p", i)
+        send_pack("p", i, k)
+    add_pack("p", 3)
     total = gacc[:, d_block(0)]
     for k in range(4):
         for j in range(2):
@@ -1525,10 +1526,11 @@
     pk_sum = pk_own[3].astype(fl)
     po_sum = po_own[3].astype(fl)
     for i in (0, 2):
+        copies.arrived(f"zo{i}")
+        po_sum += po_z[i].astype(fl)
+    for i in range(3):
         copies.arrived(f"zp{i}")
-        copies.arrived(f"zo{i}")
         pk_sum += pk_z[i].astype(fl)
-        po_sum += po_z[i].astype(fl)
     qkv_grad[...] = pk_sum
     o_grad[...] = po_sum
     mine = pl.ds(pl.multiple_of(t * kvt, kvt), kvt)

time: 653 us -> 647 us (level)
  the two profiles are of different devices: /device:TPU:9 before, /device:TPU:0 now
where the time goes in v7:
time: 647 us; the launch traced here: 639 us
  Pallas kernels  584 us (90%)
  other arithmetic  40.5 us (6%)
  local copies, waits for them, and re-layouts  12.7 us (2%)
    pallas_call x1, Pallas kernels, forward_part(): pl.pallas_call(forward_kernel, out_shape=(shape((2, model, ff), bf), shap...  248 us
    pallas_call x1, Pallas kernels, backward_part(): pl.pallas_call(backward_kernel, out_shape=(shape((2, rows, ZN * ff), bf),...  191 us
    pallas_call x1, Pallas kernels, feed_forward(): pl.pallas_call(ff_kernel, out_shape=(jax.ShapeDtypeStruct((3, group, ff),...  145 us
    mul x5, other arithmetic, adamw(): -learn_rate  39.2 us

profile of v7, /device:TPU:0, one launch (start us, length us, event | category | flops | bytes accessed | tf_op | source)
XLA Modules:
  0.0 638.7 jit_solution(5000364163706106202)
XLA Ops:
  1.3 0.7 convert_element_type.12
  2.0 0.6 pad_convert_fusion.gains
  2.6 248.2 %forward_part.1 = (bf16[2,2048,1024]{2,1,0:T(8,128)(2,1)}, bf16[1024,2048]{1,0:T(8,128)(2,1)}, bf16[2560,2048]{1,0:T(8,128)(2,1)}, bf16[2560,2048]{1,0:T(8,128)(...) custom-call(s32[1]{0:T(128)S(6)} %copy.51.lengths, ...), custom_call_target="tpu_custom_call" | custom-call | tf_op jit(solution)/shard_map/forward_part/pallas_call | solution.py:823
  250.8 144.9 %feed_forward.1 = (bf16[3,2560,1024]{2,1,0:T(8,128)(2,1)}, f32[2,160,2048]{2,1,0:T(8,128)}, bf16[2,256,1024]{2,1,0:T(8,128)(2,1)}, bf16[1024,256]{1,0:T(8,128)(2,1)}) custom-call(bf16[2560,2048]{1,0:T(8,128)(2,1)} %get-tuple-element.50.nt_hbm, bf16[2560,2048]{1,0:T(8,128)(2,1)} %get-tuple-element.51.dy_hbm, bf16[2,2048,1024]{2,1,0:T(8,128)(2,1)} %get-tuple-element.52.gu_hbm, ...), custom_call_target="tpu_custom_call" | custom-call | tf_op jit(solution)/shard_map/feed_forward/pallas_call | solution.py:1165
  395.7 190.6 %backward_part.1 = (bf16[2,256,4096]{2,1,0:T(8,128)(2,1)}, bf16[4096,256]{1,0:T(8,128)(2,1)}, f32[256,640]{1,0:T(8,128)}, f32[256,512]{1,0:T(8,128)}, f32[512,25...) custom-call(s32[1]{0:T(128)S(6)} %copy.51.lengths, ...), custom_call_target="tpu_custom_call" | custom-call | tf_op jit(solution)/shard_map/backward_part/pallas_call | solution.py:1566
  586.3 0.0 copy-start
  586.3 0.0 copy-start.3
  586.3 0.0 copy-start.4
  586.3 0.0 copy-start.5
  586.3 4.4 add_multiply_fusion.3
  590.8 1.3 add_multiply_fusion.2
  592.1 22.8 %add_multiply_fusion = (f32[2,256,4096]{2,1,0:T(8,128)}, f32[2,256,4096]{2,1,0:T(8,128)}, f32[2,256,4096]{2,1,0:T(8,128)}, f32[2,256,4096]{2,1,0:T(8,128)}) fusion(f32[2,256,4096]{2,1,0:T(8,128)} %wgu.1, f32[2,256,4096]{2,1,0:T(8,128)} %param.39, f32[2,256,4096]{2,1,0:T(8,128)} %param.33, bf16[2,256,4096]{2,1,0:T(8,128)(2,1)} %get-tuple-element.71), kind=kLoop, calls=%fused_computation.2 | loop fusion | flops 27262976 | bytes 62914560 | tf_op jit(solution)/shard_map/mul | solution.py:87
  614.9 0.0 copy-done.2
  614.9 0.0 copy-start.6
  614.9 0.0 copy-start.7
  614.9 0.0 copy-start.8
  614.9 9.4 %add_multiply_fusion.1 = (f32[4096,256]{1,0:T(8,128)}, f32[4096,256]{1,0:T(8,128)}, f32[4096,256]{1,0:T(8,128)}, f32[4096,256]{1,0:T(8,128)}) fusion(f32[4096,256]{1,0:T(8,128)} %wd.1, f32[4096,256]{1,0:T(8,128)} %param.40, f32[4096,256]{1,0:T(8,128)} %param.34, bf16[4096,256]{1,0:T(8,128)(2,1)S(1)} %copy-done.2), kind=kLoop, calls=%fused_computation.6 | loop fusion | flops 13631488 | bytes 31457280 | tf_op jit(solution)/shard_map/mul | solution.py:87
  624.3 0.0 copy-done.7
  624.3 1.3 add_multiply_fusion.5
  625.6 5.5 copy.52
  631.1 5.5 copy.53
  636.6 0.0 copy-done.1
  636.6 0.8 copy.54
  637.4 0.8 copy.55
  (8 shorter events, 0.0 us)
Async XLA Ops:
  586.3 4.5 copy-start
  586.3 4.4 copy-start.3
  586.3 4.4 copy-start.4
  586.3 4.4 copy-start.5
  592.1 22.8 %copy-start.2 = (bf16[4096,256]{1,0:T(8,128)(2,1)S(1)}, bf16[4096,256]{1,0:T(8,128)(2,1)}, u32[]{:S(2)}) copy-start(bf16[4096,256]{1,0:T(8,128)(2,1)} %get-tuple-element.72) | copy-start | bytes 6291460
  614.9 9.4 %copy-start.6 = (f32[2,256]{1,0:T(2,128)S(1)}, f32[2,256]{1,0:T(2,128)}, u32[]{:S(2)}) copy-start(f32[2,256]{1,0:T(2,128)} %param.29) | copy-start | bytes 6148
  614.9 9.4 %copy-start.7 = (f32[2,256]{1,0:T(2,128)S(1)}, f32[2,256]{1,0:T(2,128)}, u32[]{:S(2)}) copy-start(f32[2,256]{1,0:T(2,128)} %param.41) | copy-start | bytes 6148
  614.9 9.4 %copy-start.8 = (f32[2,256]{1,0:T(2,128)S(1)}, f32[2,256]{1,0:T(2,128)}, u32[]{:S(2)}) copy-start(f32[2,256]{1,0:T(2,128)} %param.35) | copy-start | bytes 6148
  631.1 5.5 copy-start.1
